TPU v7x, 512 devices: a whole 4x4x16 slice. The times are simulated.
512 devices in a mesh: space: 128 (over z_lo, x, y, core), case: 4 (over z_hi).
Axes of the slice: x: 4, y: 4, z: 16 (z_hi: 4, z_lo: 4; z = z_hi * 4 + z_lo), core: 2. Of those that a mesh axis runs over, the one named last changes fastest.
Arguments:
- spectrum: float32 [4, 36, 32, 16384], P('case', None, None, 'space'), may hold values from 0.25 to 7.5, as said below
- cotangent: float32 [4, 36, 32, 16384], P('case', None, None, 'space'), may hold values from -6 to 6
- courant: float32 [36, 16384], P(None, 'space'), may hold values from 0.05 to 0.9
- upwind: int32 [36, 16384], P(None, 'space'), may hold values from 0 to 255, as said below
- w_in: bfloat16 [32, 128], replicated, may hold values from -1 to 1
- b_in: float32 [128], replicated, may hold values from -3 to 3
- w_mid: bfloat16 [128, 128], replicated, may hold values from -0.5 to 0.5
- b_mid: float32 [128], replicated, may hold values from -3 to 3
- w_out: bfloat16 [128, 32], replicated, may hold values from -0.5 to 0.5
- b_out: float32 [32], replicated, may hold values from -3 to 3
Outputs:
- state_grad: float32 [4, 36, 32, 16384], P('case', None, None, 'space')
- grad_w_in: float32 [32, 128], replicated
- grad_b_in: float32 [128], replicated
- grad_w_mid: float32 [128, 128], replicated
- grad_b_mid: float32 [128], replicated
- grad_w_out: float32 [128, 32], replicated
- grad_b_out: float32 [32], replicated
Inputs may be any that keep to these rules, and one draw needn't show every extreme that they name: `spectrum`: positive spectral densities. `upwind`: an index into a device's own 128 nodes extended by 64 nodes on each side: value i stands for node i - 64 of the device's block. It lies within 64 of the node's own extended index and never equals it.
All inputs are finite; a program needn't handle non-finite values.
Results may differ from a plain program's by a relative error of at most 0.0065.
The roundings to bfloat16 on the way count: a program that leaves them out, or rounds other values in their place, can miss the bound.
Values sent between devices are 32-bit elements; how exact they have to be, the bound alone decides.
No kernel may reach another device: no remote copies, remote signals or barrier semaphores. Data moves between devices by JAX's collectives and lax.ppermute only.
A program may use at most 64 MiB of HBM per device.

v0:
```python
import jax
import jax.numpy as jnp
from jax import lax
from jax.sharding import PartitionSpec as P

HALO = 64


time_step = 0.3
clip_norm = 100.0


def passed_along(value, axis, steps):
    count = lax.axis_size(axis)
    initial, last = (max(0, -steps), min(count, count - steps))
    return lax.ppermute(value, axis, [(source, source + steps) for source in range(initial, last)])


def padded(block, sides, width):
    for axis, dim in sides:
        count = lax.axis_size(axis)
        forward = [(i, i + 1) for i in range(count - 1)]
        backward = [(target, source) for source, target in forward]
        low = lax.ppermute(
            lax.slice_in_dim(block, block.shape[dim] - width, None, axis=dim), axis, forward
        )
        high = lax.ppermute(lax.slice_in_dim(block, 0, width, axis=dim), axis, backward)
        block = jnp.concatenate([low, block, high], axis=dim)
    return block


def silu_slope(pre):
    logistic = jax.nn.sigmoid(pre)
    return logistic * (1.0 + pre * (1.0 - logistic))


def forward_mlp(field, weights):
    w_in, b_in, w_mid, b_mid, w_out, b_out = weights
    rounded = field.astype(jnp.bfloat16)
    pre_one = (
        jnp.einsum("fk,cdfn->cdkn", w_in, rounded, preferred_element_type=jnp.float32)
        + b_in[None, None, :, None]
    )
    act_one = jax.nn.silu(pre_one).astype(jnp.bfloat16)
    pre_two = (
        jnp.einsum("kj,cdkn->cdjn", w_mid, act_one, preferred_element_type=jnp.float32)
        + b_mid[None, None, :, None]
    )
    act_two = jax.nn.silu(pre_two).astype(jnp.bfloat16)
    source = (
        jnp.einsum("kf,cdkn->cdfn", w_out, act_two, preferred_element_type=jnp.float32)
        + b_out[None, None, :, None]
    )
    return (rounded, pre_one, act_one, pre_two, act_two, source)


def backward_step(field, forward_parts, incoming, courant_b, selector, weights):
    w_in, b_in, w_mid, b_mid, w_out, b_out = weights
    rounded, pre_one, act_one, pre_two, act_two, source = forward_parts
    damping = jax.nn.softplus(source)
    g_source = (-time_step * incoming * field * jax.nn.sigmoid(source)).astype(jnp.bfloat16)
    grad_w_out = jnp.einsum("cdkn,cdfn->kf", act_two, g_source, preferred_element_type=jnp.float32)
    grad_b_out = jnp.sum(g_source, axis=(0, 1, 3), dtype=jnp.float32)
    back_two = (
        jnp.einsum("kf,cdfn->cdkn", w_out, g_source, preferred_element_type=jnp.float32)
        * silu_slope(pre_two)
    ).astype(jnp.bfloat16)
    grad_w_mid = jnp.einsum("cdkn,cdjn->kj", act_one, back_two, preferred_element_type=jnp.float32)
    grad_b_mid = jnp.sum(back_two, axis=(0, 1, 3), dtype=jnp.float32)
    back_one = (
        jnp.einsum("kj,cdjn->cdkn", w_mid, back_two, preferred_element_type=jnp.float32)
        * silu_slope(pre_one)
    ).astype(jnp.bfloat16)
    grad_w_in = jnp.einsum("cdfn,cdkn->fk", rounded, back_one, preferred_element_type=jnp.float32)
    grad_b_in = jnp.sum(back_one, axis=(0, 1, 3), dtype=jnp.float32)
    back_state = jnp.einsum("fk,cdkn->cdfn", w_in, back_one, preferred_element_type=jnp.float32)
    width = field.shape[3]
    extended_grad = jnp.einsum(
        "cdfn,dmn->cdfm",
        courant_b * incoming,
        selector,
        preferred_element_type=jnp.float32,
        precision=lax.Precision.HIGHEST,
    )
    local_grad = (
        incoming * (1.0 - courant_b - time_step * damping)
        + back_state
        + extended_grad[:, :, :, HALO : HALO + width]
    )
    lower_rim = extended_grad[:, :, :, :HALO]
    upper_rim = extended_grad[:, :, :, HALO + width :]
    from_above = passed_along(lower_rim, "space", -1)
    from_below = passed_along(upper_rim, "space", 1)
    local_grad = local_grad + jnp.pad(from_below, ((0, 0), (0, 0), (0, 0), (0, width - HALO)))
    local_grad = local_grad + jnp.pad(from_above, ((0, 0), (0, 0), (0, 0), (width - HALO, 0)))
    return (local_grad, (grad_w_in, grad_b_in, grad_w_mid, grad_b_mid, grad_w_out, grad_b_out))


def shards(spectrum, cotangent, courant, upwind, w_in, b_in, w_mid, b_mid, w_out, b_out):
    weights = (w_in, b_in, w_mid, b_mid, w_out, b_out)
    width = spectrum.shape[3]
    courant_b = courant[None, :, None, :]
    slots = jnp.arange(width + 2 * HALO, dtype=jnp.int32)[None, :, None]
    selector = (upwind[:, None, :] == slots).astype(jnp.float32)
    extended = padded(spectrum, (("space", 3),), HALO)
    upstream = jnp.einsum(
        "cdfm,dmn->cdfn",
        extended,
        selector,
        preferred_element_type=jnp.float32,
        precision=lax.Precision.HIGHEST,
    )
    start_parts = forward_mlp(spectrum, weights)
    damping = jax.nn.softplus(start_parts[5])
    field_next = spectrum - courant_b * (spectrum - upstream) - time_step * damping * spectrum
    grad_mid, later = backward_step(
        field_next, forward_mlp(field_next, weights), cotangent, courant_b, selector, weights
    )
    grad_first, earlier = backward_step(
        spectrum, start_parts, grad_mid, courant_b, selector, weights
    )
    both = tuple((a + b for a, b in zip(later, earlier)))
    totals = lax.psum((both[0], both[1], both[2], both[3], both[4], both[5]), ("space", "case"))
    squares = jnp.float32(0.0)
    for part in totals:
        squares = squares + jnp.sum(part * part)
    factor = clip_norm / jnp.maximum(jnp.sqrt(squares), clip_norm)
    return (
        grad_first,
        totals[0] * factor,
        totals[1] * factor,
        totals[2] * factor,
        totals[3] * factor,
        totals[4] * factor,
        totals[5] * factor,
    )


def solution(mesh):
    placed = (
        P("case", None, None, "space"),
        P("case", None, None, "space"),
        P(None, "space"),
        P(None, "space"),
        P(),
        P(),
        P(),
        P(),
        P(),
        P(),
    )
    return jax.shard_map(
        shards,
        mesh=mesh,
        in_specs=placed,
        out_specs=(P("case", None, None, "space"), P(), P(), P(), P(), P(), P()),
        check_vma=False,
    )
```

profile of v0, /device:TPU:1, one launch (start us, length us, event | category | flops | bytes accessed | tf_op | source)
XLA Modules:
  0.0 621.0 jit_solution(13773417934276840559)
XLA Ops:
  7.2 0.0 all-reduce.7.cloned.1.call-start
  7.2 3.8 fusion.34
  11.1 0.2 fusion.170
  11.3 4.6 collective-permute-start.2
  15.9 5.5 collective-permute-start.3
  21.4 0.2 fusion.171
  21.7 1.9 collective-permute-start
  23.6 2.6 collective-permute-start.1
  26.2 0.5 fusion.128
  26.8 0.8 fusion.73
  27.6 0.8 fusion.38
  28.5 1.9 collective-permute-done
  30.4 4.4 collective-permute-done.1
  34.8 2.1 fusion.46
  37.0 0.5 fusion.125
  37.5 0.8 fusion.67
  38.2 0.3 copy-done.6
  38.5 1.0 convert_reduce_fusion.5
  39.6 1.1 convert_reduce_fusion.1
  40.7 1.1 convert_reduce_fusion.3
  41.7 0.9 fusion.75
  42.6 0.3 fusion.96
  43.0 1.9 convert_reduce_fusion.4
  44.8 0.8 fusion.90
  45.6 1.1 convert_reduce_fusion
  46.7 1.0 fusion.105
  47.7 1.1 convert_reduce_fusion.2
  48.7 1.5 fusion.85
  50.2 0.3 fusion.102
  50.5 115.0 %all-reduce.4 = (f32[32,128]{1,0:T(8,128)S(1)}, f32[128]{0:T(128)S(1)}, f32[128]{0:T(128)S(1)}, f32[128,32]{0,1:T(8,128)S(1)}, f32[32]{0:T(128)S(1)}) all-reduce(f32[32,128]{1,0:T(8,128)S(1)} %fusion.102, f32[128]{0:T(128)S(1)} %add.216, f32[128]{0:T(128)S(1)} %add.220, ...), channel_id=1, replica_groups=mesh['space'=128,'case'=4] {'space','case'}, use_global_device_ids=true, to_apply=%region_0.1 | all-reduce | flops 8480 | bytes 67840 | tf_op jit(solution)/shard_map/psum | solution.py:123
  165.6 0.6 multiply_reduce_fusion.3
  166.2 0.6 multiply_reduce_fusion.1
  166.8 0.6 multiply_reduce_fusion.2
  167.4 0.0 all-reduce.7.cloned.1.call-update
  167.4 3.8 fusion.35
  171.2 1.2 fusion.169
  172.4 1.9 collective-permute-start.4
  174.4 3.3 collective-permute-start.5
  177.7 0.6 multiply_reduce_fusion.4
  179.6 423.2 %all-reduce.7.cloned.1.call-done = f32[128,128]{1,0:T(8,128)} async-done(((f32[128,128]{1,0:T(8,128)}), f32[128,128]{1,0:T(8,128)}) %all-reduce.7.cloned.1.call-update) | async-done | bytes 65552 | tf_op jit(solution)/shard_map/psum | solution.py:123
  602.8 1.5 multiply_reduce_fusion
  606.9 0.5 broadcast_multiply_fusion.4
  607.4 0.5 broadcast_multiply_fusion.3
  607.9 0.6 broadcast_multiply_fusion.1
  608.5 0.6 broadcast_multiply_fusion.2
  609.2 0.5 broadcast_multiply_fusion.5
  609.7 1.5 broadcast_multiply_fusion
  611.2 3.0 fusion.113
  (31 shorter events, 0.1 us)
Async XLA Ops:
  7.2 19.6 %copy-start = (bf16[128,128]{1,0:T(8,128)(2,1)S(1)}, bf16[128,128]{1,0:T(8,128)(2,1)}, u32[]{:S(2)}) copy-start(bf16[128,128]{1,0:T(8,128)(2,1)} %param.16) | copy-start | bytes 98308
  7.2 14.3 %copy-start.1 = (f32[1,36,32,128]{3,2,1,0:T(8,128)S(1)}, f32[1,36,32,128]{3,2,1,0:T(8,128)}, u32[]{:S(2)}) copy-start(f32[1,36,32,128]{3,2,1,0:T(8,128)} %param.10) | copy-start | bytes 1769476
  7.2 595.6 %all-reduce.7.cloned.1.call-start = ((), (), s32[]{:S(2)}) async-start(), calls=%async_computation | async-start | bytes 131072 | tf_op jit(solution)/shard_map/psum | solution.py:123
  11.0 15.2 %copy-start.4 = (bf16[32,128]{1,0:T(8,128)(2,1)S(1)}, bf16[32,128]{1,0:T(8,128)(2,1)}, u32[]{:S(2)}) copy-start(bf16[32,128]{1,0:T(8,128)(2,1)} %param.14) | copy-start | bytes 24580
  11.3 31.6 %collective-permute-start.2 = (f32[1,36,32,64]{3,2,1,0:T(8,128)S(1)}, f32[1,36,32,64]{3,2,1,0:T(8,128)S(1)}, u32[]{:S(2)}, u32[]{:S(2)}) collective-permute-start(f32[1,36,32,64]{3,2,1,0:T(8,128)S(1)} %get-tuple-element.18), channel_id=1, source_target_pairs={{0,4},{4,8},{8,12},{12,16},{16,20},{20,24},{24,28},{28,32},{32,36}... | collective-permute-start | bytes 884744 | tf_op jit(solution)/shard_map/ppermute | solution.py:16
  15.9 10.9 %copy-start.11 = (f32[128]{0:T(128)S(1)}, f32[128]{0:T(128)}, u32[]{:S(2)}) copy-start(f32[128]{0:T(128)} %param.15) | copy-start | bytes 1540
  15.9 27.0 %collective-permute-start.3 = (f32[1,36,32,64]{3,2,1,0:T(8,128)S(1)}, f32[1,36,32,64]{3,2,1,0:T(8,128)S(1)}, u32[]{:S(2)}, u32[]{:S(2)}) collective-permute-start(f32[1,36,32,64]{3,2,1,0:T(8,128)S(1)} %get-tuple-element.19), channel_id=1, source_target_pairs={{4,0},{8,4},{12,8},{16,12},{20,16},{24,20},{28,24},{32,28},{36,32}... | collective-permute-start | bytes 884744 | tf_op jit(solution)/shard_map/ppermute | solution.py:16
  21.7 8.7 %collective-permute-start = (f32[1,36,32,64]{3,2,1,0:T(8,128)S(1)}, f32[1,36,32,64]{3,2,1,0:T(8,128)S(1)}, u32[]{:S(2)}, u32[]{:S(2)}) collective-permute-start(f32[1,36,32,64]{3,2,1,0:T(8,128)S(1)} %get-tuple-element.20), channel_id=1, source_target_pairs={{0,4},{4,8},{8,12},{12,16},{16,20},{20,24},{24,28},{28,32},{32,36}... | collective-permute-start | bytes 884744 | tf_op jit(solution)/shard_map/ppermute | solution.py:24
  23.6 11.2 %collective-permute-start.1 = (f32[1,36,32,64]{3,2,1,0:T(8,128)S(1)}, f32[1,36,32,64]{3,2,1,0:T(8,128)S(1)}, u32[]{:S(2)}, u32[]{:S(2)}) collective-permute-start(f32[1,36,32,64]{3,2,1,0:T(8,128)S(1)} %get-tuple-element.21), channel_id=1, source_target_pairs={{4,0},{8,4},{12,8},{16,12},{20,16},{24,20},{28,24},{32,28},{36,32}... | collective-permute-start | bytes 884744 | tf_op jit(solution)/shard_map/ppermute | solution.py:27
  26.8 0.8 copy-start.8
  26.8 0.8 copy-start.9
  26.8 0.8 copy-start.10
  27.6 0.9 copy-start.5
  27.6 7.2 %copy-start.7 = (s32[36,128]{1,0:T(8,128)S(1)}, s32[36,128]{1,0:T(8,128)}, u32[]{:S(2)}) copy-start(s32[36,128]{1,0:T(8,128)} %param.13) | copy-start | bytes 55300
  28.4 14.5 %copy-start.2 = (f32[1,36,32,128]{3,2,1,0:T(8,128)}, f32[1,36,32,128]{3,2,1,0:T(8,128)S(1)}, u32[]{:S(2)}) copy-start(f32[1,36,32,128]{3,2,1,0:T(8,128)S(1)} %fusion.38) | copy-start | bytes 1769476
  37.5 1.1 copy-start.6
  167.4 443.7 %copy-start.3 = (f32[1,36,32,128]{3,2,1,0:T(8,128)S(1)}, f32[1,36,32,128]{3,2,1,0:T(8,128)}, u32[]{:S(2)}) copy-start(f32[1,36,32,128]{3,2,1,0:T(8,128)} %copy-done.2) | copy-start | bytes 1769476
  172.4 438.7 %collective-permute-start.4 = (f32[1,36,32,64]{3,2,1,0:T(8,128)}, f32[1,36,32,64]{3,2,1,0:T(8,128)}, u32[]{:S(2)}, u32[]{:S(2)}) collective-permute-start(f32[1,36,32,64]{3,2,1,0:T(8,128)} %get-tuple-element.16), channel_id=1, source_target_pairs={{0,4},{4,8},{8,12},{12,16},{16,20},{20,24},{24,28},{28,32},{32,36}... | collective-permute-start | bytes 884744 | tf_op jit(solution)/shard_map/ppermute | solution.py:16
  174.4 436.8 %collective-permute-start.5 = (f32[1,36,32,64]{3,2,1,0:T(8,128)}, f32[1,36,32,64]{3,2,1,0:T(8,128)}, u32[]{:S(2)}, u32[]{:S(2)}) collective-permute-start(f32[1,36,32,64]{3,2,1,0:T(8,128)} %get-tuple-element.17), channel_id=1, source_target_pairs={{4,0},{8,4},{12,8},{16,12},{20,16},{24,20},{28,24},{32,28},{36,32}... | collective-permute-start | bytes 884744 | tf_op jit(solution)/shard_map/ppermute | solution.py:16
Sparse Core Ops, SparseCore 0:
  167.5 435.1 all-reduce.6
where the time goes:
time: 622 us; the launch traced here: 621 us
  waiting for transfers between devices  430 us (69%)
  blocking collectives  115 us (18%)
  matrix products  28 us (5%)
  starting transfers between devices  19.9 us (3%)
  between operations  18.3 us (3%)
  other arithmetic  8.11 us (1%)
    psum x1, waiting for transfers between devices, shards(): lax.psum((both[0], both[1], both[2], both[3], both[4], both[5]), ('space'...  423 us
    psum x1, blocking collectives, shards(): lax.psum((both[0], both[1], both[2], both[3], both[4], both[5]), ('space'...  115 us
    ppermute x4, starting transfers between devices, passed_along(): lax.ppermute(value, axis, [(source, source + steps) for source in range(i...  15.3 us
  transfers between devices with their start and end apart: 7, of which 3 were waited for; matrix products, arithmetic and copies ran while one was open for 3% of the time, Pallas kernels for 0%

commit v1 on v0

v1 whole, which is shorter than its diff:
```python
import jax
import jax.numpy as jnp
import numpy as np
from jax import lax
from jax.experimental import pallas as pl
from jax.experimental.pallas import tpu as pltpu
from jax.sharding import PartitionSpec as P

DIRS = 36
FREQS = 32
HID = 128
HALO = 64
WIDTH = 128
TAIL = 48
CHUNK = 12
BLOCK = 12
ROWS = 256

time_step = 0.3
clip_norm = 100.0
F32 = jnp.float32
BF16 = jnp.bfloat16
LIMIT = 40 * 1024 * 1024


def dot(a, b):
    return jnp.dot(a, b, preferred_element_type=F32)


def dot_nt(a, b):
    return lax.dot_general(a, b, (((1,), (1,)), ((), ())), preferred_element_type=F32)


def lanes(shape):
    return lax.broadcasted_iota(jnp.int32, shape, len(shape) - 1)


def turned(x):
    return pltpu.roll(x, HALO, x.ndim - 1)


def low_lanes(a, b):
    return jnp.where(lanes(a.shape) < HALO, a, b)


def in_hbm(*arrays):
    return [pltpu.with_memory_space_constraint(x, pltpu.HBM) for x in arrays]


def is_odd():
    return lax.axis_index("space") % 2 == 1


def pack_kernel(spec, cot, courant, upwind, far, near):
    main = DIRS * FREQS
    sides = lanes((8, WIDTH)) < HALO
    mine = jnp.where(is_odd(), sides.astype(jnp.int32), 1 - sides.astype(jnp.int32))

    def put(rows, x, g):
        here = jnp.broadcast_to(mine[:1], x.shape) == 1
        x = turned(x)
        far[rows] = jnp.where(here, x, g)
        near[rows] = jnp.where(here, g, x)

    put(slice(0, main), spec[0].reshape(main, WIDTH), cot[0].reshape(main, WIDTH))
    put(slice(main, main + DIRS), upwind[...].astype(F32), courant[...])
    rest = jnp.zeros((TAIL - DIRS, WIDTH), F32)
    far[main + DIRS :] = rest
    near[main + DIRS :] = rest


def packed_halo(spectrum, cotangent, courant, upwind):
    out = jax.ShapeDtypeStruct((DIRS * FREQS + TAIL, WIDTH), F32)
    return pl.pallas_call(
        pack_kernel,
        out_shape=(out, out),
        compiler_params=pltpu.CompilerParams(vmem_limit_bytes=LIMIT),
        name="pack_halo",
    )(*in_hbm(spectrum, cotangent, courant, upwind))


def set_rim(far, near, rim_c, rim_u):
    odd = is_odd()
    below = jnp.where(odd, near[...], far[...])
    above = jnp.where(odd, far[...], near[...])
    rim_c[...] = low_lanes(above, below)
    own = turned(low_lanes(below, above))
    offset = jnp.where(lanes(own.shape) < HALO, WIDTH - HALO, -(HALO + WIDTH))
    rim_u[...] = own.astype(jnp.int32) + offset


def one_hot(target):
    place = lax.broadcasted_iota(jnp.int32, (WIDTH, WIDTH), 0)
    return jnp.where(place == target, 1.0, 0.0).astype(BF16)


def spread(value, hot):
    high = value.astype(BF16)
    low = (value - high.astype(F32)).astype(BF16)
    both = dot_nt(jnp.concatenate([high, low], axis=0), hot)
    return both[:FREQS] + both[FREQS:]


def gathered(x, index):
    return jnp.take_along_axis(x, index & (WIDTH - 1), axis=1, mode="promise_in_bounds")


def from_inside(index):
    return (index >= HALO) & (index < HALO + WIDTH)


def column(row):
    return jnp.broadcast_to(row, (HID, HID)).T


def wide(tile, width):
    return jnp.concatenate([tile] * (width // tile.shape[1]), axis=1)


def activated(pre):
    logistic = 0.5 + 0.5 * jnp.tanh(0.5 * pre)
    act = pre * logistic
    return act.astype(BF16), logistic + act * (1.0 - logistic)


def forward(x, w_in_t, b_in, w_mid_t, b_mid, w_out_t, b_out):
    width = x.shape[1]
    rounded = x.astype(BF16)
    act_one, slope_one = activated(dot(w_in_t, rounded) + wide(b_in, width))
    act_two, slope_two = activated(dot(w_mid_t, act_one) + wide(b_mid, width))
    source = dot(w_out_t, act_two) + wide(b_out, width)
    damping = jnp.maximum(source, 0.0) + jnp.log(1.0 + jnp.exp(-jnp.abs(source)))
    logistic = 0.5 + 0.5 * jnp.tanh(0.5 * source)
    return rounded, act_one, slope_one, act_two, slope_two, damping, logistic


def set_weights(w_in, b_in, w_mid, b_mid, w_out_t, b_out, w_in_t, b_in_c, w_mid_t, b_mid_c, b_out_c, w_out=None):
    w_in_t[...] = w_in[...].astype(F32).T.astype(BF16)
    w_mid_t[...] = w_mid[...].astype(F32).T.astype(BF16)
    b_in_c[...] = column(b_in[...])
    b_mid_c[...] = column(b_mid[...])
    row = jnp.broadcast_to(b_out[...], (HID, FREQS))
    b_out_c[...] = row.T
    if w_out is not None:
        w_out[...] = w_out_t[...].astype(F32).T.astype(BF16)


def side_by_side(ref, at):
    return jnp.concatenate([ref[at + i] for i in range(CHUNK)], axis=1)


def put_apart(ref, at, value):
    for i in range(CHUNK):
        ref[at + i] = value[:, i * WIDTH : (i + 1) * WIDTH]


def forward_kernel(
    spec, cot, courant, upwind, w_in, b_in, w_mid, b_mid, w_out_t, b_out,
    act_one, slope_one, act_two, slope_two, damped, driven, inside, sent,
    w_in_t, b_in_c, w_mid_t, b_mid_c, b_out_c,
):
    step = pl.program_id(0)

    @pl.when(step == 0)
    def _():
        set_weights(w_in, b_in, w_mid, b_mid, w_out_t, b_out, w_in_t, b_in_c, w_mid_t, b_mid_c, b_out_c)

    for part in range(BLOCK // CHUNK):
        at = part * CHUNK
        x = side_by_side(spec, at)
        _, a1, s1, a2, s2, damping, logistic = forward(
            x, w_in_t[...], b_in_c[...], w_mid_t[...], b_mid_c[...], w_out_t[...], b_out_c[...]
        )
        act_one[part] = a1
        slope_one[part] = s1
        act_two[part] = a2
        slope_two[part] = s2
        damped[part] = time_step * damping
        driven[part] = (-time_step) * x * logistic
        for i in range(CHUNK):
            d = step * BLOCK + at + i
            columns = slice(i * WIDTH, (i + 1) * WIDTH)
            up, c = upwind[pl.ds(d, 1), :], courant[pl.ds(d, 1), :]
            index = jnp.broadcast_to(up, (FREQS, WIDTH))
            own = spec[at + i]
            upstream = jnp.where(from_inside(index), gathered(own, index + HALO), 0.0)
            damp = time_step * damping[:, columns]
            inside[part, :, columns] = own - c * (own - upstream) - damp * own
            hot = one_hot(jnp.broadcast_to(up - HALO, (WIDTH, WIDTH)))
            sent[part, :, columns] = spread(c * cot[at + i], hot)


def weight_specs():
    fixed = lambda i: (0, 0)
    return [
        pl.BlockSpec((FREQS, HID), fixed),
        pl.BlockSpec((1, HID), fixed),
        pl.BlockSpec((HID, HID), fixed),
        pl.BlockSpec((1, HID), fixed),
        pl.BlockSpec((FREQS, HID), fixed),
        pl.BlockSpec((1, FREQS), fixed),
    ]


def weight_scratch():
    return [
        pltpu.VMEM((HID, FREQS), BF16),
        pltpu.VMEM((HID, HID), F32),
        pltpu.VMEM((HID, HID), BF16),
        pltpu.VMEM((HID, HID), F32),
        pltpu.VMEM((FREQS, HID), F32),
    ]


PARTS = DIRS // CHUNK
SPAN = CHUNK * WIDTH


def saved_specs():
    per = BLOCK // CHUNK
    hid = pl.BlockSpec((per, HID, SPAN), lambda i: (i, 0, 0))
    freq = pl.BlockSpec((per, FREQS, SPAN), lambda i: (i, 0, 0))
    return [hid, hid, hid, hid, freq, freq, freq, freq]


def directions(rows=FREQS):
    return pl.BlockSpec((BLOCK, rows, WIDTH), lambda i: (i, 0, 0))


def whole_rows():
    return pl.BlockSpec((DIRS, WIDTH), lambda i: (0, 0))


def forward_saved(field, cotangent, courant, upwind, weights):
    hid = lambda kind: jax.ShapeDtypeStruct((PARTS, HID, SPAN), kind)
    freq = jax.ShapeDtypeStruct((PARTS, FREQS, SPAN), F32)
    return pl.pallas_call(
        forward_kernel,
        grid=(DIRS // BLOCK,),
        in_specs=[directions(), directions(), whole_rows(), whole_rows()] + weight_specs(),
        out_specs=saved_specs(),
        out_shape=[hid(BF16), hid(F32), hid(BF16), hid(F32), freq, freq, freq, freq],
        scratch_shapes=weight_scratch(),
        compiler_params=pltpu.CompilerParams(vmem_limit_bytes=LIMIT),
        cost_estimate=pl.CostEstimate(
            flops=2 * 24576 * DIRS * WIDTH, bytes_accessed=9_000_000, transcendentals=2 * HID * DIRS * WIDTH
        ),
        name="forward_start",
    )(*in_hbm(field, cotangent, courant, upwind, *weights))


def adjoint(incoming, rounded, driven, a1, s1, a2, s2, w_in, w_mid, w_out, grads, b_out_sum):
    width = incoming.shape[1]
    ones = jnp.ones((16, width), BF16)
    g_source = (incoming * driven).astype(BF16)
    grads[160:192] += dot_nt(g_source, a2)
    b_out_sum[...] += sum(
        g_source[:, i * WIDTH : (i + 1) * WIDTH].astype(F32) for i in range(width // WIDTH)
    )
    back_two = (dot(w_out, g_source) * s2).astype(BF16)
    grad = dot_nt(jnp.concatenate([a1, ones], axis=0), back_two)
    grads[:128] += grad[:128]
    grads[193:194] += grad[128:129]
    back_one = (dot(w_mid, back_two) * s1).astype(BF16)
    grad = dot_nt(jnp.concatenate([rounded, ones], axis=0), back_one)
    grads[128:160] += grad[:32]
    grads[192:193] += grad[32:33]
    return dot(w_in, back_one)


def main_kernel(
    spec, cot, courant, upwind, far, near, far_tail, near_tail,
    act_one, slope_one, act_two, slope_two, damped, driven, inside, sent,
    w_in, b_in, w_mid, b_mid, w_out_t, b_out,
    middle_out, rest_out, grads,
    w_in_t, b_in_c, w_mid_t, b_mid_c, b_out_c, w_out, b_out_sum, rim_cs, rim_us,
):
    step = pl.program_id(0)

    @pl.when(step == 0)
    def _():
        set_weights(
            w_in, b_in, w_mid, b_mid, w_out_t, b_out, w_in_t, b_in_c, w_mid_t, b_mid_c, b_out_c, w_out
        )
        set_rim(far_tail, near_tail, rim_cs, rim_us)
        grads[...] = jnp.zeros_like(grads)
        b_out_sum[...] = jnp.zeros_like(b_out_sum)

    odd = is_odd()
    sides = (lanes((FREQS, WIDTH)) < HALO).astype(jnp.int32)
    far_side = jnp.where(odd, 1 - sides, sides) == 1
    for part in range(BLOCK // CHUNK):
        at = part * CHUNK
        outside, courants, from_rim = [], [], []
        for i in range(CHUNK):
            d = step * BLOCK + at + i
            rows = slice((at + i) * FREQS, (at + i + 1) * FREQS)
            rim_x = jnp.where(far_side, far[rows], near[rows])
            rim_g = jnp.where(far_side, near[rows], far[rows])
            index = jnp.broadcast_to(upwind[pl.ds(d, 1), :], (FREQS, WIDTH))
            c = jnp.broadcast_to(courant[pl.ds(d, 1), :], (FREQS, WIDTH))
            outside.append(jnp.where(from_inside(index), 0.0, c * gathered(rim_x, index)))
            courants.append(c)
            rim_c, rim_u = rim_cs[pl.ds(d, 1), :], rim_us[pl.ds(d, 1), :]
            from_rim.append(spread(rim_c * rim_g, one_hot(jnp.broadcast_to(rim_u, (WIDTH, WIDTH)))))
        x = side_by_side(spec, at)
        g = side_by_side(cot, at)
        c = jnp.concatenate(courants, axis=1)
        field = inside[part] + jnp.concatenate(outside, axis=1)
        rounded, a1, s1, a2, s2, damping, logistic = forward(
            field, w_in_t[...], b_in_c[...], w_mid_t[...], b_mid_c[...], w_out_t[...], b_out_c[...]
        )
        back = adjoint(
            g, rounded, (-time_step) * field * logistic, a1, s1, a2, s2,
            w_in[...], w_mid[...], w_out[...], grads, b_out_sum,
        )
        middle = (
            g * (1.0 - c - time_step * damping) + back + sent[part] + jnp.concatenate(from_rim, axis=1)
        )
        back = adjoint(
            middle, x.astype(BF16), driven[part], act_one[part], slope_one[part], act_two[part],
            slope_two[part], w_in[...], w_mid[...], w_out[...], grads, b_out_sum,
        )
        put_apart(middle_out, at, middle)
        put_apart(rest_out, at, middle * (1.0 - c - damped[part]) + back)

    @pl.when(step == pl.num_programs(0) - 1)
    def _():
        grads[194:195, :FREQS] = jnp.sum(b_out_sum[...].T, axis=0, keepdims=True)


def both_adjoints(field, cotangent, courant, upwind, far, near, saved, weights):
    halo = pl.BlockSpec((BLOCK * FREQS, WIDTH), lambda i: (i, 0))
    tail = pl.BlockSpec((TAIL, WIDTH), lambda i: (DIRS * FREQS // TAIL, 0))
    state = jax.ShapeDtypeStruct((DIRS, FREQS, WIDTH), F32)
    return pl.pallas_call(
        main_kernel,
        grid=(DIRS // BLOCK,),
        in_specs=[directions(), directions(), whole_rows(), whole_rows(), halo, halo, tail, tail]
        + saved_specs()
        + weight_specs(),
        out_specs=[directions(), directions(), pl.BlockSpec((ROWS, WIDTH), lambda i: (0, 0))],
        out_shape=[state, state, jax.ShapeDtypeStruct((ROWS, WIDTH), F32)],
        scratch_shapes=weight_scratch()
        + [
            pltpu.VMEM((HID, FREQS), BF16),
            pltpu.VMEM((FREQS, WIDTH), F32),
            pltpu.VMEM((TAIL, WIDTH), F32),
            pltpu.VMEM((TAIL, WIDTH), jnp.int32),
        ],
        compiler_params=pltpu.CompilerParams(vmem_limit_bytes=LIMIT),
        cost_estimate=pl.CostEstimate(
            flops=10 * 24576 * DIRS * WIDTH, bytes_accessed=14_000_000, transcendentals=2 * HID * DIRS * WIDTH
        ),
        name="both_adjoints",
    )(field, cotangent, courant, upwind, far, near, far, near, *saved, *weights)


def edge_kernel(middle, to_far, to_near):
    odd = is_odd()
    first, second = middle[:, : FREQS // 2, :], middle[:, FREQS // 2 :, :]
    to_next = low_lanes(turned(first), second)
    to_prev = low_lanes(first, turned(second))
    to_far[...] = jnp.where(odd, to_next, to_prev)
    to_near[...] = jnp.where(odd, to_prev, to_next)


def packed_edges(middle):
    half = jax.ShapeDtypeStruct((DIRS, FREQS // 2, WIDTH), F32)
    return pl.pallas_call(
        edge_kernel,
        out_shape=(half, half),
        compiler_params=pltpu.CompilerParams(vmem_limit_bytes=LIMIT),
        cost_estimate=pl.CostEstimate(flops=1_000_000, bytes_accessed=1_200_000, transcendentals=0),
        name="pack_edges",
    )(middle)


def last_kernel(rest, middle, courant, upwind, far, near, far_tail, near_tail, out, rim_cs, rim_us):
    step = pl.program_id(0)

    @pl.when(step == 0)
    def _():
        set_rim(far_tail, near_tail, rim_cs, rim_us)

    odd = is_odd()
    for i in range(BLOCK):
        d = step * BLOCK + i
        low, high = jnp.where(odd, near[i], far[i]), jnp.where(odd, far[i], near[i])
        rim = jnp.concatenate([low_lanes(high, turned(low)), low_lanes(turned(high), low)], axis=0)
        rim_c, rim_u = rim_cs[pl.ds(d, 1), :], rim_us[pl.ds(d, 1), :]
        own_u = upwind[pl.ds(d, 1), :] - HALO
        hot = jnp.concatenate(
            [one_hot(jnp.broadcast_to(u, (WIDTH, WIDTH))) for u in (own_u, rim_u)], axis=1
        )
        moved = jnp.concatenate([courant[pl.ds(d, 1), :] * middle[i], rim_c * rim], axis=1)
        out[0, i] = rest[i] + spread(moved, hot)


def last_state(rest, middle, courant, upwind, far, near, far_first, near_first):
    tail = pl.BlockSpec((TAIL, WIDTH), lambda i: (DIRS * FREQS // TAIL, 0))
    edges = directions(FREQS // 2)
    return pl.pallas_call(
        last_kernel,
        grid=(DIRS // BLOCK,),
        in_specs=[directions(), directions(), whole_rows(), whole_rows(), edges, edges, tail, tail],
        out_specs=pl.BlockSpec((1, BLOCK, FREQS, WIDTH), lambda i: (0, i, 0, 0)),
        out_shape=jax.ShapeDtypeStruct((1, DIRS, FREQS, WIDTH), F32),
        scratch_shapes=[pltpu.VMEM((TAIL, WIDTH), F32), pltpu.VMEM((TAIL, WIDTH), jnp.int32)],
        compiler_params=pltpu.CompilerParams(vmem_limit_bytes=LIMIT),
        cost_estimate=pl.CostEstimate(
            flops=8 * FREQS * WIDTH * WIDTH * DIRS, bytes_accessed=2_400_000, transcendentals=0
        ),
        name="last_state",
    )(rest, middle, courant, upwind, far, near, far_first, near_first)


def clip_kernel(whole, w_in, b_in, w_mid, b_mid, w_out_t, b_out):
    x = whole[...]
    squares = jnp.sum(x * x, keepdims=True)
    factor = clip_norm / jnp.maximum(jnp.sqrt(squares), clip_norm)
    w_mid[...] = x[:128] * factor
    w_in[...] = x[128:160] * factor
    w_out_t[...] = x[160:192] * factor
    b_in[...] = x[192:193] * factor
    b_mid[...] = x[193:194] * factor
    b_out[...] = x[194:195, :FREQS] * factor


def clipped(whole):
    shape = lambda *s: jax.ShapeDtypeStruct(s, F32)
    w_in, b_in, w_mid, b_mid, w_out_t, b_out = pl.pallas_call(
        clip_kernel,
        out_shape=[
            shape(FREQS, HID),
            shape(1, HID),
            shape(HID, HID),
            shape(1, HID),
            shape(FREQS, HID),
            shape(1, FREQS),
        ],
        compiler_params=pltpu.CompilerParams(vmem_limit_bytes=LIMIT),
        name="clip",
    )(whole)
    return (w_in, b_in[0], w_mid, b_mid[0], w_out_t.T, b_out[0])


def exchanged(blocks, groups):
    return lax.all_to_all(
        blocks, ("space", "case"), 0, 0, axis_index_groups=groups, tiled=True
    )


def copied(parts, copies):
    total = jnp.sum(parts, axis=0)
    return jnp.broadcast_to(total[None], (copies,) + total.shape)


def device_groups():
    spaces, cases = lax.axis_size("space"), lax.axis_size("case")
    grid = np.arange(spaces * cases).reshape(spaces // 32, 4, 8, cases)
    along = lambda axis: np.moveaxis(grid, axis, -1).reshape(-1, grid.shape[axis]).tolist()
    return [along(axis) for axis in range(4)]


def summed_everywhere(parts):
    z_lo, x, y_core, z_hi = device_groups()
    first, second = len(y_core[0]), len(x[0])
    rows = ROWS // first
    parts = exchanged(parts.reshape(first, rows, WIDTH), y_core)
    parts = exchanged(jnp.sum(parts, axis=0).reshape(second, rows // second, WIDTH), x)
    parts = exchanged(copied(parts, len(z_lo[0])), z_lo)
    parts = exchanged(copied(parts, len(z_hi[0])), z_hi)
    parts = exchanged(copied(parts, second), x)
    whole = jnp.broadcast_to(parts.reshape(1, rows, WIDTH), (first, rows, WIDTH))
    return exchanged(whole, y_core).reshape(ROWS, WIDTH)


def by_pairs(far, near):
    count = lax.axis_size("space")
    swapped = lambda first: [
        pair for i in range(first, count - 1, 2) for pair in ((i, i + 1), (i + 1, i))
    ]
    return lax.ppermute(far, "space", swapped(1)), lax.ppermute(near, "space", swapped(0))


def shards(spectrum, cotangent, courant, upwind, w_in, b_in, w_mid, b_mid, w_out, b_out):
    weights = (w_in, b_in[None], w_mid, b_mid[None], w_out.T, b_out[None])
    field, incoming = spectrum[0], cotangent[0]
    far, near = by_pairs(*packed_halo(spectrum, cotangent, courant, upwind))
    saved = forward_saved(field, incoming, courant, upwind, weights)
    middle, rest, grads = both_adjoints(
        field, incoming, courant, upwind, far, near, saved, weights
    )
    totals = clipped(summed_everywhere(grads))
    far_mid, near_mid = by_pairs(*packed_edges(middle))
    state = last_state(rest, middle, courant, upwind, far_mid, near_mid, far, near)
    return (state, *totals)


def solution(mesh):
    placed = (
        P("case", None, None, "space"),
        P("case", None, None, "space"),
        P(None, "space"),
        P(None, "space"),
        P(),
        P(),
        P(),
        P(),
        P(),
        P(),
    )
    return jax.shard_map(
        shards,
        mesh=mesh,
        in_specs=placed,
        out_specs=(P("case", None, None, "space"), P(), P(), P(), P(), P(), P()),
        check_vma=False,
    )
```

time: 622 us -> 103 us (0.17)
  waiting for transfers between devices: 430 us -> 2.93 us
  blocking collectives: 115 us -> 52.4 us
  matrix products: 28 us -> 0 us
  Pallas kernels: 0 us -> 17.8 us
  between operations: 18.3 us -> 0.87 us
  other arithmetic: 8.11 us -> 0.03 us
  starting transfers between devices: 19.9 us -> 27.9 us
    psum x1 -> x0, waiting for transfers between devices: 423 us -> none  [shards(): lax.psum((both[0], both[1], both[2], both[3], both[4], both[5]), ('space'...]
    psum x1 -> x0, blocking collectives: 115 us -> none  [shards(): lax.psum((both[0], both[1], both[2], both[3], both[4], both[5]), ('space'...]
    all_to_all x0 -> x4, blocking collectives: none -> 52.4 us  [exchanged(): lax.all_to_all(blocks, ('space', 'case'), 0, 0, axis_index_groups=groups,...]
    dot_general x21 -> x0, matrix products: 28 us -> none  [the longest x2 7.62 us: backward_step(): jnp.einsum('cdfn,dmn->cdfm', courant_b * incoming, selector, preferred_el...]
    pallas_call x0 -> x6, Pallas kernels: none -> 17.8 us  [the longest x1 7.37 us: both_adjoints(): pl.pallas_call(main_kernel, grid=(DIRS // BLOCK,), in_specs=[directions()...]
    all_to_all x0 -> x2, starting transfers between devices: none -> 13 us  [exchanged(): lax.all_to_all(blocks, ('space', 'case'), 0, 0, axis_index_groups=groups,...]
    ppermute x6 -> x4, waiting for transfers between devices: 6.33 us -> 0.02 us  [the longest x2 0.01 us: by_pairs(): lax.ppermute(far, 'space', swapped(1))]
    ppermute x6 -> x4, starting transfers between devices: 19.8 us -> 14.9 us  [the longest x2 8.12 us: by_pairs(): lax.ppermute(far, 'space', swapped(1))]
  transfers between devices with their start and end apart: 7 -> 6, of which waited for: 3 -> 1; matrix products, arithmetic and copies ran while one was open for 3% -> 1% of each run, Pallas kernels for 0% -> 8%
where the time goes in v1:
time: 103 us
  blocking collectives  52.4 us (51%)
  starting transfers between devices  27.9 us (27%)
  Pallas kernels  17.8 us (17%)
  waiting for transfers between devices  2.93 us (3%)
    all_to_all x4, blocking collectives, exchanged(): lax.all_to_all(blocks, ('space', 'case'), 0, 0, axis_index_groups=groups,...  52.4 us
    all_to_all x2, starting transfers between devices, exchanged(): lax.all_to_all(blocks, ('space', 'case'), 0, 0, axis_index_groups=groups,...  13 us
    ppermute x2, starting transfers between devices, by_pairs(): lax.ppermute(far, 'space', swapped(1))  8.12 us
    pallas_call x1, Pallas kernels, both_adjoints(): pl.pallas_call(main_kernel, grid=(DIRS // BLOCK,), in_specs=[directions()...  7.37 us
    ppermute x2, starting transfers between devices, by_pairs(): lax.ppermute(near, 'space', swapped(0))  6.81 us
    pallas_call x1, Pallas kernels, forward_saved(): pl.pallas_call(forward_kernel, grid=(DIRS // BLOCK,), in_specs=[direction...  4.74 us
    all_to_all x2, waiting for transfers between devices, exchanged(): lax.all_to_all(blocks, ('space', 'case'), 0, 0, axis_index_groups=groups,...  2.91 us
    pallas_call x1, Pallas kernels, last_state(): pl.pallas_call(last_kernel, grid=(DIRS // BLOCK,), in_specs=[directions()...  2.38 us
  transfers between devices with their start and end apart: 6, of which 1 were waited for; matrix products, arithmetic and copies ran while one was open for 1% of the time, Pallas kernels for 8%

profile of v1, /device:TPU:1, one launch (start us, length us, event | category | flops | bytes accessed | tf_op | source)
XLA Modules:
  0.0 102.6 jit_solution(11714601218828749911)
XLA Ops:
  0.6 0.0 copy-start.3
  0.6 0.0 copy-start.2
  0.7 0.0 copy-start.1
  0.7 0.0 copy-start
  0.7 0.0 copy-start.4
  0.7 0.0 copy-start.5
  0.7 0.0 copy-start.9
  0.7 0.0 copy-start.6
  0.7 0.0 copy-start.8
  0.7 0.0 copy-start.7
  0.8 1.5 %pack_halo.1 = (f32[1200,128]{1,0:T(8,128)S(1)}, f32[1200,128]{1,0:T(8,128)S(1)}) custom-call(f32[1,36,32,128]{3,2,1,0:T(8,128)} %spec.1, f32[1,36,32,128]{3,2,1,0:T(8,128)} %cot.1, f32[36,128]{1,0:T(8,128)} %courant.7, s32[36,128]{1,0:T(8,128)} %upwind.7), custom_call_target="tpu_custom_call" | custom-call | tf_op jit(solution)/shard_map/pack_halo/pallas_call | solution.py:74
  2.3 4.6 %collective-permute-start = (f32[1200,128]{1,0:T(8,128)S(1)}, f32[1200,128]{1,0:T(8,128)S(1)}, u32[]{:S(2)}, u32[]{:S(2)}) collective-permute-start(f32[1200,128]{1,0:T(8,128)S(1)} %get-tuple-element.28), channel_id=1, source_target_pairs={{4,8},{8,4},{12,16},{16,12},{20,24},{24,20},{28,32},{32,28},{36,40... | collective-permute-start | bytes 1843208 | tf_op jit(solution)/shard_map/ppermute | solution.py:484
  6.9 4.9 %collective-permute-start.1 = (f32[1200,128]{1,0:T(8,128)S(1)}, f32[1200,128]{1,0:T(8,128)S(1)}, u32[]{:S(2)}, u32[]{:S(2)}) collective-permute-start(f32[1200,128]{1,0:T(8,128)S(1)} %get-tuple-element.29), channel_id=1, source_target_pairs={{0,4},{4,0},{8,12},{12,8},{16,20},{20,16},{24,28},{28,24},{32,36},... | collective-permute-start | bytes 1843208 | tf_op jit(solution)/shard_map/ppermute | solution.py:484
  11.8 4.7 %forward_start.1 = (bf16[3,128,1536]{2,1,0:T(8,128)(2,1)S(1)}, f32[3,128,1536]{2,1,0:T(8,128)S(1)}, bf16[3,128,1536]{2,1,0:T(8,128)(2,1)S(1)}, f32[3,128,1536]{2...) custom-call(f32[36,32,128]{2,1,0:T(8,128)} %bitcast.14, ...), custom_call_target="tpu_custom_call" | custom-call | flops 226492416 | bytes 9000000 | tf_op jit(solution)/shard_map/forward_start/pallas_call | solution.py:237
  16.6 0.0 collective-permute-done.far.far_tail
  16.6 0.0 collective-permute-done.1.near.near_tail
  16.6 0.0 copy-done.3
  16.6 0.0 copy-done.2
  16.6 0.0 copy-done.1
  16.6 0.0 copy-done
  16.6 0.0 copy-done.4
  16.6 0.0 copy-done.5
  16.6 0.0 copy-done.9
  16.7 0.0 copy-done.6
  16.7 0.0 copy-done.8
  16.7 0.0 copy-done.7
  16.7 7.4 %both_adjoints.1 = (f32[36,32,128]{2,1,0:T(8,128)S(1)}, f32[36,32,128]{2,1,0:T(8,128)S(1)}, f32[256,128]{1,0:T(8,128)}) custom-call(f32[36,32,128]{2,1,0:T(8,128)S(1)} %bitcast.15, f32[36,32,128]{2,1,0:T(8,128)S(1)} %bitcast.17, f32[36,128]{1,0:T(8,128)S(1)} %copy-done.2, s32[36,128]{1,0:T(8,128)S(1)} %copy-done.3, ...), custom_call_target="tpu_custom_call" | custom-call | flops 1132462080 | bytes 14000000 | tf_op jit(solution)/shard_map/both_adjoints/pallas_call | solution.py:336
  24.1 4.5 %all-to-all-start = ((f32[8,32,128]{2,1,0:T(8,128)}), f32[8,32,128]{2,1,0:T(8,128)S(1)}, u32[]{:S(2)}, u32[]{:S(2)}) async-start(f32[8,32,128]{2,1,0:T(8,128)} %bitcast.6), calls=%async_computation | async-start | bytes 262144 | tf_op jit(solution)/shard_map/all_to_all | solution.py:449
  28.6 0.9 pack_edges.1
  29.5 3.5 %collective-permute-start.2 = (f32[36,16,128]{2,1,0:T(8,128)}, f32[36,16,128]{2,1,0:T(8,128)S(1)}, u32[]{:S(2)}, u32[]{:S(2)}) collective-permute-start(f32[36,16,128]{2,1,0:T(8,128)} %get-tuple-element.40), channel_id=1, source_target_pairs={{4,8},{8,4},{12,16},{16,12},{20,24},{24,20},{28,32},{32,28},{36,40... | collective-permute-start | bytes 884744 | tf_op jit(solution)/shard_map/ppermute | solution.py:484
  33.0 1.9 %collective-permute-start.3 = (f32[36,16,128]{2,1,0:T(8,128)S(1)}, f32[36,16,128]{2,1,0:T(8,128)S(1)}, u32[]{:S(2)}, u32[]{:S(2)}) collective-permute-start(f32[36,16,128]{2,1,0:T(8,128)S(1)} %get-tuple-element.41), channel_id=1, source_target_pairs={{0,4},{4,0},{8,12},{12,8},{16,20},{20,16},{24,28},{28,24},{32,36},... | collective-permute-start | bytes 884744 | tf_op jit(solution)/shard_map/ppermute | solution.py:484
  35.0 0.0 all-to-all-done
  35.0 9.9 %all_to_all.30 = f32[4,8,128]{2,1,0:T(8,128)S(1)} all-to-all(f32[4,8,128]{2,1,0:T(8,128)S(1)} %bitcast.27), channel_id=1, replica_groups={{0,32,64,96},{1,33,65,97},{2,34,66,98},{3,35,67,99},{4,36,68,100},{5,37..., dimensions={0} | all-to-all | bytes 32768 | tf_op jit(solution)/shard_map/all_to_all | solution.py:449
  44.9 11.8 %all_to_all.31 = f32[4,8,128]{2,1,0:T(8,128)S(1)} all-to-all(f32[4,8,128]{2,1,0:T(8,128)S(1)} %broadcast_in_dim.37), channel_id=1, replica_groups={{0,128,256,384},{1,129,257,385},{2,130,258,386},{3,131,259,387},{4,132,..., dimensions={0} | all-to-all | bytes 32768 | tf_op jit(solution)/shard_map/all_to_all | solution.py:449
  56.6 24.2 %all_to_all.32 = f32[4,8,128]{2,1,0:T(8,128)S(1)} all-to-all(f32[4,8,128]{2,1,0:T(8,128)S(1)} %broadcast_in_dim.38), channel_id=1, replica_groups={{0,1,2,3},{4,5,6,7},{8,9,10,11},{12,13,14,15},{16,17,18,19},{20,21,22,2..., dimensions={0} | all-to-all | bytes 32768 | tf_op jit(solution)/shard_map/all_to_all | solution.py:449
  80.9 6.5 %all_to_all.33 = f32[4,8,128]{2,1,0:T(8,128)S(1)} all-to-all(f32[4,8,128]{2,1,0:T(8,128)S(1)} %broadcast_in_dim.39), channel_id=1, replica_groups={{0,32,64,96},{1,33,65,97},{2,34,66,98},{3,35,67,99},{4,36,68,100},{5,37..., dimensions={0} | all-to-all | bytes 32768 | tf_op jit(solution)/shard_map/all_to_all | solution.py:449
  87.4 0.6 broadcast_in_dim.41
  88.1 8.4 %all-to-all-start.5 = ((f32[8,32,128]{2,1,0:T(8,128)}), f32[8,32,128]{2,1,0:T(8,128)S(1)}, u32[]{:S(2)}, u32[]{:S(2)}) async-start(f32[8,32,128]{2,1,0:T(8,128)} %broadcast_in_dim.41), calls=%async_computation.5 | async-start | bytes 262144 | tf_op jit(solution)/shard_map/all_to_all | solution.py:449
  96.5 0.0 collective-permute-done.2.far
  96.5 0.0 collective-permute-done.3.near
  96.5 2.4 %last_state.1 = f32[1,36,32,128]{3,2,1,0:T(8,128)} custom-call(f32[36,32,128]{2,1,0:T(8,128)S(1)} %get-tuple-element.38.rest, f32[36,32,128]{2,1,0:T(8,128)S(1)} %get-tuple-element.39.middle, f32[36,128]{1,0:T(8,128)S(1)} %copy-done.2, s32[36,128]{1,0:T(8,128)S(1)} %copy-done.3, f32[36,16,128]{2,1,0:T(8,128)S(1)} %collective-permute-done.2.far, ...), custom_call_target="tpu_custom_call" | custom-call | flops 150994944 | bytes 2400000 | tf_op jit(solution)/shard_map/last_state/pallas_call | solution.py:403
  98.9 2.9 %all-to-all-done.5 = f32[8,32,128]{2,1,0:T(8,128)S(1)} async-done(((f32[8,32,128]{2,1,0:T(8,128)}), f32[8,32,128]{2,1,0:T(8,128)S(1)}, u32[]{:S(2)}, u32[]{:S(2)}) %all-to-all-start.5) | async-done | bytes 131104 | tf_op jit(solution)/shard_map/all_to_all | solution.py:449
  101.8 0.8 clip.1
  (7 shorter events, 0.0 us)
Async XLA Ops:
  0.6 16.0 %copy-start.3 = (s32[36,128]{1,0:T(8,128)S(1)}, s32[36,128]{1,0:T(8,128)}, u32[]{:S(2)}) copy-start(s32[36,128]{1,0:T(8,128)} %upwind.7) | copy-start | bytes 55300
  0.6 16.0 %copy-start.2 = (f32[36,128]{1,0:T(8,128)S(1)}, f32[36,128]{1,0:T(8,128)}, u32[]{:S(2)}) copy-start(f32[36,128]{1,0:T(8,128)} %courant.7) | copy-start | bytes 55300
  0.7 16.0 %copy-start.1 = (f32[1,36,32,128]{3,2,1,0:T(8,128)S(1)}, f32[1,36,32,128]{3,2,1,0:T(8,128)}, u32[]{:S(2)}) copy-start(f32[1,36,32,128]{3,2,1,0:T(8,128)} %cot.1) | copy-start | bytes 1769476
  0.7 15.9 %copy-start = (f32[1,36,32,128]{3,2,1,0:T(8,128)S(1)}, f32[1,36,32,128]{3,2,1,0:T(8,128)}, u32[]{:S(2)}) copy-start(f32[1,36,32,128]{3,2,1,0:T(8,128)} %spec.1) | copy-start | bytes 1769476
  0.7 15.9 %copy-start.4 = (bf16[128,128]{1,0:T(8,128)(2,1)S(1)}, bf16[128,128]{1,0:T(8,128)(2,1)}, u32[]{:S(2)}) copy-start(bf16[128,128]{1,0:T(8,128)(2,1)} %w_mid.3) | copy-start | bytes 98308
  0.7 15.9 %copy-start.5 = (bf16[32,128]{1,0:T(8,128)(2,1)S(1)}, bf16[32,128]{1,0:T(8,128)(2,1)}, u32[]{:S(2)}) copy-start(bf16[32,128]{1,0:T(8,128)(2,1)} %w_in.3) | copy-start | bytes 24580
  0.7 15.9 %copy-start.9 = (f32[32]{0:T(128)S(1)}, f32[32]{0:T(128)}, u32[]{:S(2)}) copy-start(f32[32]{0:T(128)} %param.19) | copy-start | bytes 388
  0.7 15.9 %copy-start.6 = (bf16[128,32]{0,1:T(8,128)(2,1)S(1)}, bf16[128,32]{0,1:T(8,128)(2,1)}, u32[]{:S(2)}) copy-start(bf16[128,32]{0,1:T(8,128)(2,1)} %param.18) | copy-start | bytes 24580
  0.7 15.9 %copy-start.8 = (f32[128]{0:T(128)S(1)}, f32[128]{0:T(128)}, u32[]{:S(2)}) copy-start(f32[128]{0:T(128)} %param.17) | copy-start | bytes 1540
  0.7 15.9 %copy-start.7 = (f32[128]{0:T(128)S(1)}, f32[128]{0:T(128)}, u32[]{:S(2)}) copy-start(f32[128]{0:T(128)} %param.15) | copy-start | bytes 1540
  2.3 14.3 %collective-permute-start = (f32[1200,128]{1,0:T(8,128)S(1)}, f32[1200,128]{1,0:T(8,128)S(1)}, u32[]{:S(2)}, u32[]{:S(2)}) collective-permute-start(f32[1200,128]{1,0:T(8,128)S(1)} %get-tuple-element.28), channel_id=1, source_target_pairs={{4,8},{8,4},{12,16},{16,12},{20,24},{24,20},{28,32},{32,28},{36,40... | collective-permute-start | bytes 1843208 | tf_op jit(solution)/shard_map/ppermute | solution.py:484
  6.9 9.7 %collective-permute-start.1 = (f32[1200,128]{1,0:T(8,128)S(1)}, f32[1200,128]{1,0:T(8,128)S(1)}, u32[]{:S(2)}, u32[]{:S(2)}) collective-permute-start(f32[1200,128]{1,0:T(8,128)S(1)} %get-tuple-element.29), channel_id=1, source_target_pairs={{0,4},{4,0},{8,12},{12,8},{16,20},{20,16},{24,28},{28,24},{32,36},... | collective-permute-start | bytes 1843208 | tf_op jit(solution)/shard_map/ppermute | solution.py:484
  24.1 10.9 %all-to-all-start = ((f32[8,32,128]{2,1,0:T(8,128)}), f32[8,32,128]{2,1,0:T(8,128)S(1)}, u32[]{:S(2)}, u32[]{:S(2)}) async-start(f32[8,32,128]{2,1,0:T(8,128)} %bitcast.6), calls=%async_computation | async-start | bytes 262144 | tf_op jit(solution)/shard_map/all_to_all | solution.py:449
  29.5 67.0 %collective-permute-start.2 = (f32[36,16,128]{2,1,0:T(8,128)}, f32[36,16,128]{2,1,0:T(8,128)S(1)}, u32[]{:S(2)}, u32[]{:S(2)}) collective-permute-start(f32[36,16,128]{2,1,0:T(8,128)} %get-tuple-element.40), channel_id=1, source_target_pairs={{4,8},{8,4},{12,16},{16,12},{20,24},{24,20},{28,32},{32,28},{36,40... | collective-permute-start | bytes 884744 | tf_op jit(solution)/shard_map/ppermute | solution.py:484
  33.0 63.5 %collective-permute-start.3 = (f32[36,16,128]{2,1,0:T(8,128)S(1)}, f32[36,16,128]{2,1,0:T(8,128)S(1)}, u32[]{:S(2)}, u32[]{:S(2)}) collective-permute-start(f32[36,16,128]{2,1,0:T(8,128)S(1)} %get-tuple-element.41), channel_id=1, source_target_pairs={{0,4},{4,0},{8,12},{12,8},{16,20},{20,16},{24,28},{28,24},{32,36},... | collective-permute-start | bytes 884744 | tf_op jit(solution)/shard_map/ppermute | solution.py:484
  88.1 13.7 %all-to-all-start.5 = ((f32[8,32,128]{2,1,0:T(8,128)}), f32[8,32,128]{2,1,0:T(8,128)S(1)}, u32[]{:S(2)}, u32[]{:S(2)}) async-start(f32[8,32,128]{2,1,0:T(8,128)} %broadcast_in_dim.41), calls=%async_computation.5 | async-start | bytes 262144 | tf_op jit(solution)/shard_map/all_to_all | solution.py:449

commit v2 on v1

--- a/solution.py
+++ b/solution.py
@@ -458,22 +458,18 @@
 
 def device_groups():
     spaces, cases = lax.axis_size("space"), lax.axis_size("case")
-    grid = np.arange(spaces * cases).reshape(spaces // 32, 4, 8, cases)
-    along = lambda axis: np.moveaxis(grid, axis, -1).reshape(-1, grid.shape[axis]).tolist()
-    return [along(axis) for axis in range(4)]
+    grid = np.arange(spaces * cases).reshape(spaces // 32, 32, cases)
+    layers = grid.transpose(0, 2, 1).reshape(-1, 32)
+    columns = grid.transpose(1, 0, 2).reshape(32, -1)
+    return layers.tolist(), columns.tolist()
 
 
 def summed_everywhere(parts):
-    z_lo, x, y_core, z_hi = device_groups()
-    first, second = len(y_core[0]), len(x[0])
-    rows = ROWS // first
-    parts = exchanged(parts.reshape(first, rows, WIDTH), y_core)
-    parts = exchanged(jnp.sum(parts, axis=0).reshape(second, rows // second, WIDTH), x)
-    parts = exchanged(copied(parts, len(z_lo[0])), z_lo)
-    parts = exchanged(copied(parts, len(z_hi[0])), z_hi)
-    parts = exchanged(copied(parts, second), x)
-    whole = jnp.broadcast_to(parts.reshape(1, rows, WIDTH), (first, rows, WIDTH))
-    return exchanged(whole, y_core).reshape(ROWS, WIDTH)
+    layers, columns = device_groups()
+    wide, deep = len(layers[0]), len(columns[0])
+    parts = exchanged(parts.reshape(wide, ROWS // wide, WIDTH), layers)
+    parts = exchanged(copied(parts, deep), columns)
+    return exchanged(copied(parts, wide), layers).reshape(ROWS, WIDTH)
 
 
 def by_pairs(far, near):

time: 103 us -> 82.5 us (0.80)
  blocking collectives: 52.4 us -> 16.5 us
  waiting for transfers between devices: 2.93 us -> 11.6 us
  starting transfers between devices: 27.9 us -> 34.5 us
    all_to_all x4 -> x1, blocking collectives: 52.4 us -> 16.5 us  [exchanged(): lax.all_to_all(blocks, ('space', 'case'), 0, 0, axis_index_groups=groups,...]
    all_to_all x2, waiting for transfers between devices: 2.91 us -> 11.6 us  [exchanged(): lax.all_to_all(blocks, ('space', 'case'), 0, 0, axis_index_groups=groups,...]
    all_to_all x2, starting transfers between devices: 13 us -> 20.4 us  [exchanged(): lax.all_to_all(blocks, ('space', 'case'), 0, 0, axis_index_groups=groups,...]
    broadcast_in_dim x3 -> x2, local copies, waits for them, and re-layouts: 0.02 us -> 1.3 us  [copied(): return jnp.broadcast_to(total[None], (copies,) + total.shape)]
  transfers between devices with their start and end apart: 6 -> 6, of which waited for: 1 -> 2; matrix products, arithmetic and copies ran while one was open for 1% -> 1% of each run, Pallas kernels for 8% -> 10%
where the time goes in v2:
time: 82.5 us; the launch traced here: 82.1 us
  starting transfers between devices  34.5 us (42%)
  Pallas kernels  17.2 us (21%)
  blocking collectives  16.5 us (20%)
  waiting for transfers between devices  11.6 us (14%)
  local copies, waits for them, and re-layouts  1.37 us (2%)
  between operations  0.89 us (1%)
    all_to_all x2, starting transfers between devices, exchanged(): lax.all_to_all(blocks, ('space', 'case'), 0, 0, axis_index_groups=groups,...  20.4 us
    all_to_all x1, blocking collectives, exchanged(): lax.all_to_all(blocks, ('space', 'case'), 0, 0, axis_index_groups=groups,...  16.5 us
    all_to_all x2, waiting for transfers between devices, exchanged(): lax.all_to_all(blocks, ('space', 'case'), 0, 0, axis_index_groups=groups,...  11.6 us
    ppermute x2, starting transfers between devices, by_pairs(): lax.ppermute(far, 'space', swapped(1))  7.3 us
    ppermute x2, starting transfers between devices, by_pairs(): lax.ppermute(near, 'space', swapped(0))  6.81 us
    pallas_call x1, Pallas kernels, both_adjoints(): pl.pallas_call(main_kernel, grid=(DIRS // BLOCK,), in_specs=[directions()...  6.73 us
    pallas_call x1, Pallas kernels, forward_saved(): pl.pallas_call(forward_kernel, grid=(DIRS // BLOCK,), in_specs=[direction...  4.74 us
    pallas_call x1, Pallas kernels, last_state(): pl.pallas_call(last_kernel, grid=(DIRS // BLOCK,), in_specs=[directions()...  2.38 us
  transfers between devices with their start and end apart: 6, of which 2 were waited for; matrix products, arithmetic and copies ran while one was open for 1% of the time, Pallas kernels for 10%

profile of v2, /device:TPU:1, one launch (start us, length us, event | category | flops | bytes accessed | tf_op | source)
XLA Modules:
  0.0 82.1 jit_solution(2014127883996500630)
XLA Ops:
  0.6 0.0 copy-start.3
  0.6 0.0 copy-start.2
  0.7 0.0 copy-start.1
  0.7 0.0 copy-start
  0.7 0.0 copy-start.4
  0.7 0.0 copy-start.5
  0.7 0.0 copy-start.9
  0.7 0.0 copy-start.6
  0.7 0.0 copy-start.8
  0.7 0.0 copy-start.7
  0.8 1.5 %pack_halo.1 = (f32[1200,128]{1,0:T(8,128)S(1)}, f32[1200,128]{1,0:T(8,128)S(1)}) custom-call(f32[1,36,32,128]{3,2,1,0:T(8,128)} %spec.1, f32[1,36,32,128]{3,2,1,0:T(8,128)} %cot.1, f32[36,128]{1,0:T(8,128)} %courant.7, s32[36,128]{1,0:T(8,128)} %upwind.7), custom_call_target="tpu_custom_call" | custom-call | tf_op jit(solution)/shard_map/pack_halo/pallas_call | solution.py:74
  2.3 4.6 %collective-permute-start = (f32[1200,128]{1,0:T(8,128)S(1)}, f32[1200,128]{1,0:T(8,128)S(1)}, u32[]{:S(2)}, u32[]{:S(2)}) collective-permute-start(f32[1200,128]{1,0:T(8,128)S(1)} %get-tuple-element.28), channel_id=1, source_target_pairs={{4,8},{8,4},{12,16},{16,12},{20,24},{24,20},{28,32},{32,28},{36,40... | collective-permute-start | bytes 1843208 | tf_op jit(solution)/shard_map/ppermute | solution.py:480
  6.9 4.9 %collective-permute-start.1 = (f32[1200,128]{1,0:T(8,128)S(1)}, f32[1200,128]{1,0:T(8,128)S(1)}, u32[]{:S(2)}, u32[]{:S(2)}) collective-permute-start(f32[1200,128]{1,0:T(8,128)S(1)} %get-tuple-element.29), channel_id=1, source_target_pairs={{0,4},{4,0},{8,12},{12,8},{16,20},{20,16},{24,28},{28,24},{32,36},... | collective-permute-start | bytes 1843208 | tf_op jit(solution)/shard_map/ppermute | solution.py:480
  11.8 4.7 %forward_start.1 = (bf16[3,128,1536]{2,1,0:T(8,128)(2,1)S(1)}, f32[3,128,1536]{2,1,0:T(8,128)S(1)}, bf16[3,128,1536]{2,1,0:T(8,128)(2,1)S(1)}, f32[3,128,1536]{2...) custom-call(f32[36,32,128]{2,1,0:T(8,128)} %bitcast.12, ...), custom_call_target="tpu_custom_call" | custom-call | flops 226492416 | bytes 9000000 | tf_op jit(solution)/shard_map/forward_start/pallas_call | solution.py:237
  16.6 0.0 collective-permute-done.far.far_tail
  16.6 0.0 collective-permute-done.1.near.near_tail
  16.6 0.0 copy-done.3
  16.6 0.0 copy-done.2
  16.6 0.0 copy-done.1
  16.6 0.0 copy-done
  16.6 0.0 copy-done.4
  16.6 0.0 copy-done.5
  16.6 0.0 copy-done.9
  16.7 0.0 copy-done.6
  16.7 0.0 copy-done.8
  16.7 0.0 copy-done.7
  16.7 6.7 %both_adjoints.1 = (f32[36,32,128]{2,1,0:T(8,128)S(1)}, f32[36,32,128]{2,1,0:T(8,128)S(1)}, f32[256,128]{1,0:T(8,128)S(1)}) custom-call(f32[36,32,128]{2,1,0:T(8,128)S(1)} %bitcast.13, f32[36,32,128]{2,1,0:T(8,128)S(1)} %bitcast.15, f32[36,128]{1,0:T(8,128)S(1)} %copy-done.2, s32[36,128]{1,0:T(8,128)S(1)} %copy-done.3, ...), custom_call_target="tpu_custom_call" | custom-call | flops 1132462080 | bytes 14000000 | tf_op jit(solution)/shard_map/both_adjoints/pallas_call | solution.py:336
  23.4 16.5 %all_to_all.15 = f32[32,8,128]{2,1,0:T(8,128)S(1)} all-to-all(f32[32,8,128]{2,1,0:T(8,128)S(1)} %bitcast.17), channel_id=1, replica_groups={{0,4,8,12,16,20,24,28,32,36,40,44,48,52,56,60,64,68,72,76,80,84,88,92,9..., dimensions={0} | all-to-all | bytes 262144 | tf_op jit(solution)/shard_map/all_to_all | solution.py:449
  39.9 0.6 broadcast_in_dim.24
  40.6 14.9 %all-to-all-start.1 = ((f32[16,8,128]{2,1,0:T(8,128)}), f32[16,8,128]{2,1,0:T(8,128)S(1)}, u32[]{:S(2)}, u32[]{:S(2)}) async-start(f32[16,8,128]{2,1,0:T(8,128)} %broadcast_in_dim.24), calls=%async_computation.1 | async-start | bytes 131072 | tf_op jit(solution)/shard_map/all_to_all | solution.py:449
  55.5 0.9 %pack_edges.1 = (f32[36,16,128]{2,1,0:T(8,128)}, f32[36,16,128]{2,1,0:T(8,128)S(1)}) custom-call(f32[36,32,128]{2,1,0:T(8,128)S(1)} %get-tuple-element.39.middle), custom_call_target="tpu_custom_call" | custom-call | flops 1000000 | bytes 1200000 | tf_op jit(solution)/shard_map/pack_edges/pallas_call | solution.py:370
  56.4 2.7 %collective-permute-start.2 = (f32[36,16,128]{2,1,0:T(8,128)}, f32[36,16,128]{2,1,0:T(8,128)S(1)}, u32[]{:S(2)}, u32[]{:S(2)}) collective-permute-start(f32[36,16,128]{2,1,0:T(8,128)} %get-tuple-element.40), channel_id=1, source_target_pairs={{4,8},{8,4},{12,16},{16,12},{20,24},{24,20},{28,32},{32,28},{36,40... | collective-permute-start | bytes 884744 | tf_op jit(solution)/shard_map/ppermute | solution.py:480
  59.2 1.9 %collective-permute-start.3 = (f32[36,16,128]{2,1,0:T(8,128)S(1)}, f32[36,16,128]{2,1,0:T(8,128)S(1)}, u32[]{:S(2)}, u32[]{:S(2)}) collective-permute-start(f32[36,16,128]{2,1,0:T(8,128)S(1)} %get-tuple-element.41), channel_id=1, source_target_pairs={{0,4},{4,0},{8,12},{12,8},{16,20},{20,16},{24,28},{28,24},{32,36},... | collective-permute-start | bytes 884744 | tf_op jit(solution)/shard_map/ppermute | solution.py:480
  61.1 6.2 %all-to-all-done.1 = f32[16,8,128]{2,1,0:T(8,128)S(1)} async-done(((f32[16,8,128]{2,1,0:T(8,128)}), f32[16,8,128]{2,1,0:T(8,128)S(1)}, u32[]{:S(2)}, u32[]{:S(2)}) %all-to-all-start.1) | async-done | bytes 65568 | tf_op jit(solution)/shard_map/all_to_all | solution.py:449
  67.3 0.7 broadcast_in_dim.25
  68.0 5.5 %all-to-all-start.2 = ((f32[32,8,128]{2,1,0:T(8,128)}), f32[32,8,128]{2,1,0:T(8,128)S(1)}, u32[]{:S(2)}, u32[]{:S(2)}) async-start(f32[32,8,128]{2,1,0:T(8,128)} %broadcast_in_dim.25), calls=%async_computation.2 | async-start | bytes 262144 | tf_op jit(solution)/shard_map/all_to_all | solution.py:449
  73.5 0.0 collective-permute-done.2.far
  73.5 0.0 collective-permute-done.3.near
  73.5 2.4 %last_state.1 = f32[1,36,32,128]{3,2,1,0:T(8,128)} custom-call(f32[36,32,128]{2,1,0:T(8,128)S(1)} %get-tuple-element.38.rest, f32[36,32,128]{2,1,0:T(8,128)S(1)} %get-tuple-element.39.middle, f32[36,128]{1,0:T(8,128)S(1)} %copy-done.2, s32[36,128]{1,0:T(8,128)S(1)} %copy-done.3, f32[36,16,128]{2,1,0:T(8,128)S(1)} %collective-permute-done.2.far, ...), custom_call_target="tpu_custom_call" | custom-call | flops 150994944 | bytes 2400000 | tf_op jit(solution)/shard_map/last_state/pallas_call | solution.py:403
  75.9 5.4 %all-to-all-done.2 = f32[32,8,128]{2,1,0:T(8,128)S(1)} async-done(((f32[32,8,128]{2,1,0:T(8,128)}), f32[32,8,128]{2,1,0:T(8,128)S(1)}, u32[]{:S(2)}, u32[]{:S(2)}) %all-to-all-start.2) | async-done | bytes 131104 | tf_op jit(solution)/shard_map/all_to_all | solution.py:449
  81.3 0.8 clip.1
  (2 shorter events, 0.1 us)
Async XLA Ops:
  0.6 16.0 %copy-start.3 = (s32[36,128]{1,0:T(8,128)S(1)}, s32[36,128]{1,0:T(8,128)}, u32[]{:S(2)}) copy-start(s32[36,128]{1,0:T(8,128)} %upwind.7) | copy-start | bytes 55300
  0.6 16.0 %copy-start.2 = (f32[36,128]{1,0:T(8,128)S(1)}, f32[36,128]{1,0:T(8,128)}, u32[]{:S(2)}) copy-start(f32[36,128]{1,0:T(8,128)} %courant.7) | copy-start | bytes 55300
  0.7 15.9 %copy-start.1 = (f32[1,36,32,128]{3,2,1,0:T(8,128)S(1)}, f32[1,36,32,128]{3,2,1,0:T(8,128)}, u32[]{:S(2)}) copy-start(f32[1,36,32,128]{3,2,1,0:T(8,128)} %cot.1) | copy-start | bytes 1769476
  0.7 15.9 %copy-start = (f32[1,36,32,128]{3,2,1,0:T(8,128)S(1)}, f32[1,36,32,128]{3,2,1,0:T(8,128)}, u32[]{:S(2)}) copy-start(f32[1,36,32,128]{3,2,1,0:T(8,128)} %spec.1) | copy-start | bytes 1769476
  0.7 15.9 %copy-start.4 = (bf16[128,128]{1,0:T(8,128)(2,1)S(1)}, bf16[128,128]{1,0:T(8,128)(2,1)}, u32[]{:S(2)}) copy-start(bf16[128,128]{1,0:T(8,128)(2,1)} %w_mid.3) | copy-start | bytes 98308
  0.7 15.9 %copy-start.5 = (bf16[32,128]{1,0:T(8,128)(2,1)S(1)}, bf16[32,128]{1,0:T(8,128)(2,1)}, u32[]{:S(2)}) copy-start(bf16[32,128]{1,0:T(8,128)(2,1)} %w_in.3) | copy-start | bytes 24580
  0.7 15.9 %copy-start.9 = (f32[32]{0:T(128)S(1)}, f32[32]{0:T(128)}, u32[]{:S(2)}) copy-start(f32[32]{0:T(128)} %param.19) | copy-start | bytes 388
  0.7 15.9 %copy-start.6 = (bf16[128,32]{0,1:T(8,128)(2,1)S(1)}, bf16[128,32]{0,1:T(8,128)(2,1)}, u32[]{:S(2)}) copy-start(bf16[128,32]{0,1:T(8,128)(2,1)} %param.18) | copy-start | bytes 24580
  0.7 15.9 %copy-start.8 = (f32[128]{0:T(128)S(1)}, f32[128]{0:T(128)}, u32[]{:S(2)}) copy-start(f32[128]{0:T(128)} %param.17) | copy-start | bytes 1540
  0.7 15.9 %copy-start.7 = (f32[128]{0:T(128)S(1)}, f32[128]{0:T(128)}, u32[]{:S(2)}) copy-start(f32[128]{0:T(128)} %param.15) | copy-start | bytes 1540
  2.3 14.3 %collective-permute-start = (f32[1200,128]{1,0:T(8,128)S(1)}, f32[1200,128]{1,0:T(8,128)S(1)}, u32[]{:S(2)}, u32[]{:S(2)}) collective-permute-start(f32[1200,128]{1,0:T(8,128)S(1)} %get-tuple-element.28), channel_id=1, source_target_pairs={{4,8},{8,4},{12,16},{16,12},{20,24},{24,20},{28,32},{32,28},{36,40... | collective-permute-start | bytes 1843208 | tf_op jit(solution)/shard_map/ppermute | solution.py:480
  6.9 9.7 %collective-permute-start.1 = (f32[1200,128]{1,0:T(8,128)S(1)}, f32[1200,128]{1,0:T(8,128)S(1)}, u32[]{:S(2)}, u32[]{:S(2)}) collective-permute-start(f32[1200,128]{1,0:T(8,128)S(1)} %get-tuple-element.29), channel_id=1, source_target_pairs={{0,4},{4,0},{8,12},{12,8},{16,20},{20,16},{24,28},{28,24},{32,36},... | collective-permute-start | bytes 1843208 | tf_op jit(solution)/shard_map/ppermute | solution.py:480
  40.6 26.7 %all-to-all-start.1 = ((f32[16,8,128]{2,1,0:T(8,128)}), f32[16,8,128]{2,1,0:T(8,128)S(1)}, u32[]{:S(2)}, u32[]{:S(2)}) async-start(f32[16,8,128]{2,1,0:T(8,128)} %broadcast_in_dim.24), calls=%async_computation.1 | async-start | bytes 131072 | tf_op jit(solution)/shard_map/all_to_all | solution.py:449
  56.4 17.0 %collective-permute-start.2 = (f32[36,16,128]{2,1,0:T(8,128)}, f32[36,16,128]{2,1,0:T(8,128)S(1)}, u32[]{:S(2)}, u32[]{:S(2)}) collective-permute-start(f32[36,16,128]{2,1,0:T(8,128)} %get-tuple-element.40), channel_id=1, source_target_pairs={{4,8},{8,4},{12,16},{16,12},{20,24},{24,20},{28,32},{32,28},{36,40... | collective-permute-start | bytes 884744 | tf_op jit(solution)/shard_map/ppermute | solution.py:480
  59.2 14.3 %collective-permute-start.3 = (f32[36,16,128]{2,1,0:T(8,128)S(1)}, f32[36,16,128]{2,1,0:T(8,128)S(1)}, u32[]{:S(2)}, u32[]{:S(2)}) collective-permute-start(f32[36,16,128]{2,1,0:T(8,128)S(1)} %get-tuple-element.41), channel_id=1, source_target_pairs={{0,4},{4,0},{8,12},{12,8},{16,20},{20,16},{24,28},{28,24},{32,36},... | collective-permute-start | bytes 884744 | tf_op jit(solution)/shard_map/ppermute | solution.py:480
  68.0 13.3 %all-to-all-start.2 = ((f32[32,8,128]{2,1,0:T(8,128)}), f32[32,8,128]{2,1,0:T(8,128)S(1)}, u32[]{:S(2)}, u32[]{:S(2)}) async-start(f32[32,8,128]{2,1,0:T(8,128)} %broadcast_in_dim.25), calls=%async_computation.2 | async-start | bytes 262144 | tf_op jit(solution)/shard_map/all_to_all | solution.py:449

commit v3 on v2

--- a/solution.py
+++ b/solution.py
@@ -249,31 +249,19 @@
     )(*in_hbm(field, cotangent, courant, upwind, *weights))
 
 
-def adjoint(incoming, rounded, driven, a1, s1, a2, s2, w_in, w_mid, w_out, grads, b_out_sum):
-    width = incoming.shape[1]
-    ones = jnp.ones((16, width), BF16)
+def adjoint(incoming, driven, slope_one, slope_two, w_mid, w_out):
     g_source = (incoming * driven).astype(BF16)
-    grads[160:192] += dot_nt(g_source, a2)
-    b_out_sum[...] += sum(
-        g_source[:, i * WIDTH : (i + 1) * WIDTH].astype(F32) for i in range(width // WIDTH)
-    )
-    back_two = (dot(w_out, g_source) * s2).astype(BF16)
-    grad = dot_nt(jnp.concatenate([a1, ones], axis=0), back_two)
-    grads[:128] += grad[:128]
-    grads[193:194] += grad[128:129]
-    back_one = (dot(w_mid, back_two) * s1).astype(BF16)
-    grad = dot_nt(jnp.concatenate([rounded, ones], axis=0), back_one)
-    grads[128:160] += grad[:32]
-    grads[192:193] += grad[32:33]
-    return dot(w_in, back_one)
+    back_two = (dot(w_out, g_source) * slope_two).astype(BF16)
+    back_one = (dot(w_mid, back_two) * slope_one).astype(BF16)
+    return g_source, back_two, back_one
 
 
 def main_kernel(
     spec, cot, courant, upwind, far, near, far_tail, near_tail,
     act_one, slope_one, act_two, slope_two, damped, driven, inside, sent,
     w_in, b_in, w_mid, b_mid, w_out_t, b_out,
-    middle_out, rest_out, grads,
-    w_in_t, b_in_c, w_mid_t, b_mid_c, b_out_c, w_out, b_out_sum, rim_cs, rim_us,
+    middle_out, back_out, grads,
+    w_in_t, b_in_c, w_mid_t, b_mid_c, b_out_c, w_out, b_out_sum, rim_cs, rim_us, inner_sum, outer_sum,
 ):
     step = pl.program_id(0)
 
@@ -283,7 +271,8 @@
             w_in, b_in, w_mid, b_mid, w_out_t, b_out, w_in_t, b_in_c, w_mid_t, b_mid_c, b_out_c, w_out
         )
         set_rim(far_tail, near_tail, rim_cs, rim_us)
-        grads[...] = jnp.zeros_like(grads)
+        inner_sum[...] = jnp.zeros_like(inner_sum)
+        outer_sum[...] = jnp.zeros_like(outer_sum)
         b_out_sum[...] = jnp.zeros_like(b_out_sum)
 
     odd = is_odd()
@@ -310,43 +299,71 @@
         rounded, a1, s1, a2, s2, damping, logistic = forward(
             field, w_in_t[...], b_in_c[...], w_mid_t[...], b_mid_c[...], w_out_t[...], b_out_c[...]
         )
-        back = adjoint(
-            g, rounded, (-time_step) * field * logistic, a1, s1, a2, s2,
-            w_in[...], w_mid[...], w_out[...], grads, b_out_sum,
-        )
+        gs, q2, q1 = adjoint(g, (-time_step) * field * logistic, s1, s2, w_mid[...], w_out[...])
         middle = (
-            g * (1.0 - c - time_step * damping) + back + sent[part] + jnp.concatenate(from_rim, axis=1)
-        )
-        back = adjoint(
-            middle, x.astype(BF16), driven[part], act_one[part], slope_one[part], act_two[part],
-            slope_two[part], w_in[...], w_mid[...], w_out[...], grads, b_out_sum,
+            g * (1.0 - c - time_step * damping)
+            + dot(w_in[...], q1)
+            + sent[part]
+            + jnp.concatenate(from_rim, axis=1)
+        )
+        gs_0, q2_0, q1_0 = adjoint(
+            middle, driven[part], slope_one[part], slope_two[part], w_mid[...], w_out[...]
         )
         put_apart(middle_out, at, middle)
-        put_apart(rest_out, at, middle * (1.0 - c - damped[part]) + back)
+        back_out[part] = q1_0
+        ones = jnp.ones((16, SPAN), BF16)
+        left = jnp.concatenate([a1, rounded, ones], axis=0)
+        left_0 = jnp.concatenate([act_one[part], x.astype(BF16), ones], axis=0)
+        right, right_0 = jnp.concatenate([q2, q1], axis=0), jnp.concatenate([q2_0, q1_0], axis=0)
+        inner_sum[...] += dot_nt(
+            jnp.concatenate([left, left_0], axis=1), jnp.concatenate([right, right_0], axis=1)
+        )
+        outer_sum[...] += dot_nt(
+            jnp.concatenate([gs, gs_0], axis=0), jnp.concatenate([a2, act_two[part]], axis=0)
+        )
+        b_out_sum[...] += sum(
+            value[:, i * WIDTH : (i + 1) * WIDTH].astype(F32) for i in range(CHUNK) for value in (gs, gs_0)
+        )
 
     @pl.when(step == pl.num_programs(0) - 1)
     def _():
+        grads[:128] = inner_sum[:128, :HID]
+        grads[128:160] = inner_sum[128:160, HID:]
+        grads[160:192] = outer_sum[:FREQS, :HID] + outer_sum[FREQS:, HID:]
+        grads[192:] = jnp.zeros((ROWS - 192, WIDTH), F32)
+        grads[192:193] = inner_sum[160:161, HID:]
+        grads[193:194] = inner_sum[160:161, :HID]
         grads[194:195, :FREQS] = jnp.sum(b_out_sum[...].T, axis=0, keepdims=True)
 
 
 def both_adjoints(field, cotangent, courant, upwind, far, near, saved, weights):
     halo = pl.BlockSpec((BLOCK * FREQS, WIDTH), lambda i: (i, 0))
     tail = pl.BlockSpec((TAIL, WIDTH), lambda i: (DIRS * FREQS // TAIL, 0))
-    state = jax.ShapeDtypeStruct((DIRS, FREQS, WIDTH), F32)
+    per = BLOCK // CHUNK
     return pl.pallas_call(
         main_kernel,
         grid=(DIRS // BLOCK,),
         in_specs=[directions(), directions(), whole_rows(), whole_rows(), halo, halo, tail, tail]
         + saved_specs()
         + weight_specs(),
-        out_specs=[directions(), directions(), pl.BlockSpec((ROWS, WIDTH), lambda i: (0, 0))],
-        out_shape=[state, state, jax.ShapeDtypeStruct((ROWS, WIDTH), F32)],
+        out_specs=[
+            directions(),
+            pl.BlockSpec((per, HID, SPAN), lambda i: (i, 0, 0)),
+            pl.BlockSpec((ROWS, WIDTH), lambda i: (0, 0)),
+        ],
+        out_shape=[
+            jax.ShapeDtypeStruct((DIRS, FREQS, WIDTH), F32),
+            pltpu.HBM((PARTS, HID, SPAN), BF16),
+            jax.ShapeDtypeStruct((ROWS, WIDTH), F32),
+        ],
         scratch_shapes=weight_scratch()
         + [
             pltpu.VMEM((HID, FREQS), BF16),
             pltpu.VMEM((FREQS, WIDTH), F32),
             pltpu.VMEM((TAIL, WIDTH), F32),
             pltpu.VMEM((TAIL, WIDTH), jnp.int32),
+            pltpu.VMEM((HID + FREQS + 16, 2 * HID), F32),
+            pltpu.VMEM((2 * FREQS, 2 * HID), F32),
         ],
         compiler_params=pltpu.CompilerParams(vmem_limit_bytes=LIMIT),
         cost_estimate=pl.CostEstimate(
@@ -376,7 +393,9 @@
     )(middle)
 
 
-def last_kernel(rest, middle, courant, upwind, far, near, far_tail, near_tail, out, rim_cs, rim_us):
+def last_kernel(
+    middle, back, damped, w_in, courant, upwind, far, near, far_tail, near_tail, out, rim_cs, rim_us
+):
     step = pl.program_id(0)
 
     @pl.when(step == 0)
@@ -384,35 +403,43 @@
         set_rim(far_tail, near_tail, rim_cs, rim_us)
 
     odd = is_odd()
-    for i in range(BLOCK):
-        d = step * BLOCK + i
-        low, high = jnp.where(odd, near[i], far[i]), jnp.where(odd, far[i], near[i])
-        rim = jnp.concatenate([low_lanes(high, turned(low)), low_lanes(turned(high), low)], axis=0)
-        rim_c, rim_u = rim_cs[pl.ds(d, 1), :], rim_us[pl.ds(d, 1), :]
-        own_u = upwind[pl.ds(d, 1), :] - HALO
-        hot = jnp.concatenate(
-            [one_hot(jnp.broadcast_to(u, (WIDTH, WIDTH))) for u in (own_u, rim_u)], axis=1
-        )
-        moved = jnp.concatenate([courant[pl.ds(d, 1), :] * middle[i], rim_c * rim], axis=1)
-        out[0, i] = rest[i] + spread(moved, hot)
-
-
-def last_state(rest, middle, courant, upwind, far, near, far_first, near_first):
+    for part in range(BLOCK // CHUNK):
+        state_back = dot(w_in[...], back[part])
+        for k in range(CHUNK):
+            i = part * CHUNK + k
+            d = step * BLOCK + i
+            columns = slice(k * WIDTH, (k + 1) * WIDTH)
+            low, high = jnp.where(odd, near[i], far[i]), jnp.where(odd, far[i], near[i])
+            rim = jnp.concatenate([low_lanes(high, turned(low)), low_lanes(turned(high), low)], axis=0)
+            rim_c, rim_u = rim_cs[pl.ds(d, 1), :], rim_us[pl.ds(d, 1), :]
+            own_u = upwind[pl.ds(d, 1), :] - HALO
+            hot = jnp.concatenate(
+                [one_hot(jnp.broadcast_to(u, (WIDTH, WIDTH))) for u in (own_u, rim_u)], axis=1
+            )
+            c, m = courant[pl.ds(d, 1), :], middle[i]
+            moved = jnp.concatenate([c * m, rim_c * rim], axis=1)
+            kept = m * (1.0 - c - damped[part, :, columns])
+            out[0, i] = kept + state_back[:, columns] + spread(moved, hot)
+
+
+def last_state(middle, back, damped, w_in, courant, upwind, far, near, far_first, near_first):
     tail = pl.BlockSpec((TAIL, WIDTH), lambda i: (DIRS * FREQS // TAIL, 0))
     edges = directions(FREQS // 2)
+    hid, freq = saved_specs()[0], saved_specs()[4]
     return pl.pallas_call(
         last_kernel,
         grid=(DIRS // BLOCK,),
-        in_specs=[directions(), directions(), whole_rows(), whole_rows(), edges, edges, tail, tail],
+        in_specs=[directions(), hid, freq, weight_specs()[0], whole_rows(), whole_rows()]
+        + [edges, edges, tail, tail],
         out_specs=pl.BlockSpec((1, BLOCK, FREQS, WIDTH), lambda i: (0, i, 0, 0)),
         out_shape=jax.ShapeDtypeStruct((1, DIRS, FREQS, WIDTH), F32),
         scratch_shapes=[pltpu.VMEM((TAIL, WIDTH), F32), pltpu.VMEM((TAIL, WIDTH), jnp.int32)],
         compiler_params=pltpu.CompilerParams(vmem_limit_bytes=LIMIT),
         cost_estimate=pl.CostEstimate(
-            flops=8 * FREQS * WIDTH * WIDTH * DIRS, bytes_accessed=2_400_000, transcendentals=0
+            flops=8 * FREQS * WIDTH * WIDTH * DIRS, bytes_accessed=4_000_000, transcendentals=0
         ),
         name="last_state",
-    )(rest, middle, courant, upwind, far, near, far_first, near_first)
+    )(middle, *in_hbm(back), damped, w_in, courant, upwind, far, near, far_first, near_first)
 
 
 def clip_kernel(whole, w_in, b_in, w_mid, b_mid, w_out_t, b_out):
@@ -485,12 +512,14 @@
     field, incoming = spectrum[0], cotangent[0]
     far, near = by_pairs(*packed_halo(spectrum, cotangent, courant, upwind))
     saved = forward_saved(field, incoming, courant, upwind, weights)
-    middle, rest, grads = both_adjoints(
+    middle, back, grads = both_adjoints(
         field, incoming, courant, upwind, far, near, saved, weights
     )
     totals = clipped(summed_everywhere(grads))
     far_mid, near_mid = by_pairs(*packed_edges(middle))
-    state = last_state(rest, middle, courant, upwind, far_mid, near_mid, far, near)
+    state = last_state(
+        middle, back, saved[4], w_in, courant, upwind, far_mid, near_mid, far, near
+    )
     return (state, *totals)
 
 

time: 82.5 us -> 84.2 us (1.021)
  Pallas kernels: 17.2 us -> 20.1 us
  waiting for transfers between devices: 11.6 us -> 10.2 us
    pallas_call x1, Pallas kernels: 6.73 us -> 8.31 us  [both_adjoints(): pl.pallas_call(main_kernel, grid=(DIRS // BLOCK,), in_specs=[directions()...]
    pallas_call x1, Pallas kernels: 2.38 us -> 3.78 us  [last_state(): pl.pallas_call(last_kernel, grid=(DIRS // BLOCK,), in_specs=[directions()...]
    all_to_all x2, waiting for transfers between devices: 11.6 us -> 10.2 us  [exchanged(): lax.all_to_all(blocks, ('space', 'case'), 0, 0, axis_index_groups=groups,...]
  transfers between devices with their start and end apart: 6 -> 6, of which waited for: 2 -> 2; matrix products, arithmetic and copies ran while one was open for 1% -> 1% of each run, Pallas kernels for 10% -> 11%
where the time goes in v3:
time: 84.2 us; the launch traced here: 83.7 us
  starting transfers between devices  34.7 us (41%)
  Pallas kernels  20.1 us (24%)
  blocking collectives  16.5 us (20%)
  waiting for transfers between devices  10.2 us (12%)
  local copies, waits for them, and re-layouts  1.36 us (2%)
  between operations  0.88 us (1%)
    all_to_all x2, starting transfers between devices, exchanged(): lax.all_to_all(blocks, ('space', 'case'), 0, 0, axis_index_groups=groups,...  20.4 us
    all_to_all x1, blocking collectives, exchanged(): lax.all_to_all(blocks, ('space', 'case'), 0, 0, axis_index_groups=groups,...  16.5 us
    all_to_all x2, waiting for transfers between devices, exchanged(): lax.all_to_all(blocks, ('space', 'case'), 0, 0, axis_index_groups=groups,...  10.2 us
    pallas_call x1, Pallas kernels, both_adjoints(): pl.pallas_call(main_kernel, grid=(DIRS // BLOCK,), in_specs=[directions()...  8.31 us
    ppermute x2, starting transfers between devices, by_pairs(): lax.ppermute(far, 'space', swapped(1))  7.44 us
    ppermute x2, starting transfers between devices, by_pairs(): lax.ppermute(near, 'space', swapped(0))  6.81 us
    pallas_call x1, Pallas kernels, forward_saved(): pl.pallas_call(forward_kernel, grid=(DIRS // BLOCK,), in_specs=[direction...  4.74 us
    pallas_call x1, Pallas kernels, last_state(): pl.pallas_call(last_kernel, grid=(DIRS // BLOCK,), in_specs=[directions()...  3.78 us
  transfers between devices with their start and end apart: 6, of which 2 were waited for; matrix products, arithmetic and copies ran while one was open for 1% of the time, Pallas kernels for 11%

profile of v3, /device:TPU:1, one launch (start us, length us, event | category | flops | bytes accessed | tf_op | source)
XLA Modules:
  0.0 83.7 jit_solution(6057471792883048529)
XLA Ops:
  0.6 1.5 %pack_halo.1 = (f32[1200,128]{1,0:T(8,128)S(1)}, f32[1200,128]{1,0:T(8,128)S(1)}) custom-call(f32[1,36,32,128]{3,2,1,0:T(8,128)} %spec.1, f32[1,36,32,128]{3,2,1,0:T(8,128)} %cot.1, f32[36,128]{1,0:T(8,128)} %courant.7, s32[36,128]{1,0:T(8,128)} %upwind.7), custom_call_target="tpu_custom_call" | custom-call | tf_op jit(solution)/shard_map/pack_halo/pallas_call | solution.py:74
  2.1 0.0 copy-start
  2.1 0.0 copy-start.1
  2.1 0.0 copy-start.2
  2.1 0.0 copy-start.3
  2.2 0.0 copy-start.4
  2.2 0.0 copy-start.5
  2.2 0.0 copy-start.6
  2.2 0.0 copy-start.7
  2.2 0.0 copy-start.8
  2.2 0.0 copy-start.9
  2.2 4.7 %collective-permute-start = (f32[1200,128]{1,0:T(8,128)S(1)}, f32[1200,128]{1,0:T(8,128)S(1)}, u32[]{:S(2)}, u32[]{:S(2)}) collective-permute-start(f32[1200,128]{1,0:T(8,128)S(1)} %get-tuple-element.28), channel_id=1, source_target_pairs={{4,8},{8,4},{12,16},{16,12},{20,24},{24,20},{28,32},{32,28},{36,40... | collective-permute-start | bytes 1843208 | tf_op jit(solution)/shard_map/ppermute | solution.py:507
  7.0 4.9 %collective-permute-start.1 = (f32[1200,128]{1,0:T(8,128)S(1)}, f32[1200,128]{1,0:T(8,128)S(1)}, u32[]{:S(2)}, u32[]{:S(2)}) collective-permute-start(f32[1200,128]{1,0:T(8,128)S(1)} %get-tuple-element.29), channel_id=1, source_target_pairs={{0,4},{4,0},{8,12},{12,8},{16,20},{20,16},{24,28},{28,24},{32,36},... | collective-permute-start | bytes 1843208 | tf_op jit(solution)/shard_map/ppermute | solution.py:507
  11.9 4.7 %forward_start.1 = (bf16[3,128,1536]{2,1,0:T(8,128)(2,1)S(1)}, f32[3,128,1536]{2,1,0:T(8,128)S(1)}, bf16[3,128,1536]{2,1,0:T(8,128)(2,1)S(1)}, f32[3,128,1536]{2...) custom-call(f32[36,32,128]{2,1,0:T(8,128)} %bitcast.12, ...), custom_call_target="tpu_custom_call" | custom-call | flops 226492416 | bytes 9000000 | tf_op jit(solution)/shard_map/forward_start/pallas_call | solution.py:237
  16.6 0.0 collective-permute-done.far.far_tail
  16.6 0.0 collective-permute-done.1.near.near_tail
  16.6 0.0 copy-done
  16.6 0.0 copy-done.1
  16.7 0.0 copy-done.2
  16.7 0.0 copy-done.3
  16.7 0.0 copy-done.4
  16.7 0.0 copy-done.5
  16.7 0.0 copy-done.6
  16.7 0.0 copy-done.7
  16.7 0.0 copy-done.8
  16.7 0.0 copy-done.9
  16.7 8.3 %both_adjoints.1 = (f32[36,32,128]{2,1,0:T(8,128)S(1)}, bf16[3,128,1536]{2,1,0:T(8,128)(2,1)}, f32[256,128]{1,0:T(8,128)S(1)}) custom-call(f32[36,32,128]{2,1,0:T(8,128)S(1)} %bitcast.13, f32[36,32,128]{2,1,0:T(8,128)S(1)} %bitcast.15, f32[36,128]{1,0:T(8,128)S(1)} %copy-done.2, s32[36,128]{1,0:T(8,128)S(1)} %copy-done.3, ...), custom_call_target="tpu_custom_call" | custom-call | flops 1132462080 | bytes 14000000 | tf_op jit(solution)/shard_map/both_adjoints/pallas_call | solution.py:343
  25.1 16.5 %all_to_all.15 = f32[32,8,128]{2,1,0:T(8,128)S(1)} all-to-all(f32[32,8,128]{2,1,0:T(8,128)S(1)} %bitcast.17), channel_id=1, replica_groups={{0,4,8,12,16,20,24,28,32,36,40,44,48,52,56,60,64,68,72,76,80,84,88,92,9..., dimensions={0} | all-to-all | bytes 262144 | tf_op jit(solution)/shard_map/all_to_all | solution.py:476
  41.6 0.6 broadcast_in_dim.24
  42.2 14.9 %all-to-all-start.1 = ((f32[16,8,128]{2,1,0:T(8,128)}), f32[16,8,128]{2,1,0:T(8,128)S(1)}, u32[]{:S(2)}, u32[]{:S(2)}) async-start(f32[16,8,128]{2,1,0:T(8,128)} %broadcast_in_dim.24), calls=%async_computation.1 | async-start | bytes 131072 | tf_op jit(solution)/shard_map/all_to_all | solution.py:476
  57.1 0.9 %pack_edges.1 = (f32[36,16,128]{2,1,0:T(8,128)}, f32[36,16,128]{2,1,0:T(8,128)S(1)}) custom-call(f32[36,32,128]{2,1,0:T(8,128)S(1)} %get-tuple-element.38.middle), custom_call_target="tpu_custom_call" | custom-call | flops 1000000 | bytes 1200000 | tf_op jit(solution)/shard_map/pack_edges/pallas_call | solution.py:387
  58.1 2.7 %collective-permute-start.2 = (f32[36,16,128]{2,1,0:T(8,128)}, f32[36,16,128]{2,1,0:T(8,128)S(1)}, u32[]{:S(2)}, u32[]{:S(2)}) collective-permute-start(f32[36,16,128]{2,1,0:T(8,128)} %get-tuple-element.40), channel_id=1, source_target_pairs={{4,8},{8,4},{12,16},{16,12},{20,24},{24,20},{28,32},{32,28},{36,40... | collective-permute-start | bytes 884744 | tf_op jit(solution)/shard_map/ppermute | solution.py:507
  60.8 1.9 %collective-permute-start.3 = (f32[36,16,128]{2,1,0:T(8,128)S(1)}, f32[36,16,128]{2,1,0:T(8,128)S(1)}, u32[]{:S(2)}, u32[]{:S(2)}) collective-permute-start(f32[36,16,128]{2,1,0:T(8,128)S(1)} %get-tuple-element.41), channel_id=1, source_target_pairs={{0,4},{4,0},{8,12},{12,8},{16,20},{20,16},{24,28},{28,24},{32,36},... | collective-permute-start | bytes 884744 | tf_op jit(solution)/shard_map/ppermute | solution.py:507
  62.7 6.2 %all-to-all-done.1 = f32[16,8,128]{2,1,0:T(8,128)S(1)} async-done(((f32[16,8,128]{2,1,0:T(8,128)}), f32[16,8,128]{2,1,0:T(8,128)S(1)}, u32[]{:S(2)}, u32[]{:S(2)}) %all-to-all-start.1) | async-done | bytes 65568 | tf_op jit(solution)/shard_map/all_to_all | solution.py:476
  68.9 0.7 broadcast_in_dim.25
  69.6 5.5 %all-to-all-start.2 = ((f32[32,8,128]{2,1,0:T(8,128)}), f32[32,8,128]{2,1,0:T(8,128)S(1)}, u32[]{:S(2)}, u32[]{:S(2)}) async-start(f32[32,8,128]{2,1,0:T(8,128)} %broadcast_in_dim.25), calls=%async_computation.2 | async-start | bytes 262144 | tf_op jit(solution)/shard_map/all_to_all | solution.py:476
  75.1 0.0 collective-permute-done.2.far
  75.1 0.0 collective-permute-done.3.near
  75.1 3.8 %last_state.1 = f32[1,36,32,128]{3,2,1,0:T(8,128)} custom-call(f32[36,32,128]{2,1,0:T(8,128)S(1)} %get-tuple-element.38.middle, bf16[3,128,1536]{2,1,0:T(8,128)(2,1)} %get-tuple-element.39.back, f32[3,32,1536]{2,1,0:T(8,128)S(1)} %get-tuple-element.34.damped, bf16[32,128]{1,0:T(8,128)(2,1)S(1)} %copy-done.5, f32[36,128]{1,0:T(8,128)S(1)} %copy-done.2, ...), custom_call_target="tpu_custom_call" | custom-call | flops 150994944 | bytes 4000000 | tf_op jit(solution)/shard_map/last_state/pallas_call | solution.py:429
  78.9 4.0 %all-to-all-done.2 = f32[32,8,128]{2,1,0:T(8,128)S(1)} async-done(((f32[32,8,128]{2,1,0:T(8,128)}), f32[32,8,128]{2,1,0:T(8,128)S(1)}, u32[]{:S(2)}, u32[]{:S(2)}) %all-to-all-start.2) | async-done | bytes 131104 | tf_op jit(solution)/shard_map/all_to_all | solution.py:476
  82.9 0.8 clip.1
  (2 shorter events, 0.1 us)
Async XLA Ops:
  2.1 14.5 %copy-start = (f32[1,36,32,128]{3,2,1,0:T(8,128)S(1)}, f32[1,36,32,128]{3,2,1,0:T(8,128)}, u32[]{:S(2)}) copy-start(f32[1,36,32,128]{3,2,1,0:T(8,128)} %spec.1) | copy-start | bytes 1769476
  2.1 14.5 %copy-start.1 = (f32[1,36,32,128]{3,2,1,0:T(8,128)S(1)}, f32[1,36,32,128]{3,2,1,0:T(8,128)}, u32[]{:S(2)}) copy-start(f32[1,36,32,128]{3,2,1,0:T(8,128)} %cot.1) | copy-start | bytes 1769476
  2.1 14.5 %copy-start.2 = (f32[36,128]{1,0:T(8,128)S(1)}, f32[36,128]{1,0:T(8,128)}, u32[]{:S(2)}) copy-start(f32[36,128]{1,0:T(8,128)} %courant.7) | copy-start | bytes 55300
  2.1 14.5 %copy-start.3 = (s32[36,128]{1,0:T(8,128)S(1)}, s32[36,128]{1,0:T(8,128)}, u32[]{:S(2)}) copy-start(s32[36,128]{1,0:T(8,128)} %upwind.7) | copy-start | bytes 55300
  2.2 14.5 %copy-start.4 = (bf16[128,128]{1,0:T(8,128)(2,1)S(1)}, bf16[128,128]{1,0:T(8,128)(2,1)}, u32[]{:S(2)}) copy-start(bf16[128,128]{1,0:T(8,128)(2,1)} %w_mid.3) | copy-start | bytes 98308
  2.2 14.5 %copy-start.5 = (bf16[32,128]{1,0:T(8,128)(2,1)S(1)}, bf16[32,128]{1,0:T(8,128)(2,1)}, u32[]{:S(2)}) copy-start(bf16[32,128]{1,0:T(8,128)(2,1)} %w_in.5) | copy-start | bytes 24580
  2.2 14.5 %copy-start.6 = (bf16[128,32]{0,1:T(8,128)(2,1)S(1)}, bf16[128,32]{0,1:T(8,128)(2,1)}, u32[]{:S(2)}) copy-start(bf16[128,32]{0,1:T(8,128)(2,1)} %param.18) | copy-start | bytes 24580
  2.2 14.5 %copy-start.7 = (f32[128]{0:T(128)S(1)}, f32[128]{0:T(128)}, u32[]{:S(2)}) copy-start(f32[128]{0:T(128)} %param.15) | copy-start | bytes 1540
  2.2 14.5 %copy-start.8 = (f32[128]{0:T(128)S(1)}, f32[128]{0:T(128)}, u32[]{:S(2)}) copy-start(f32[128]{0:T(128)} %param.17) | copy-start | bytes 1540
  2.2 14.5 %copy-start.9 = (f32[32]{0:T(128)S(1)}, f32[32]{0:T(128)}, u32[]{:S(2)}) copy-start(f32[32]{0:T(128)} %param.19) | copy-start | bytes 388
  2.2 14.4 %collective-permute-start = (f32[1200,128]{1,0:T(8,128)S(1)}, f32[1200,128]{1,0:T(8,128)S(1)}, u32[]{:S(2)}, u32[]{:S(2)}) collective-permute-start(f32[1200,128]{1,0:T(8,128)S(1)} %get-tuple-element.28), channel_id=1, source_target_pairs={{4,8},{8,4},{12,16},{16,12},{20,24},{24,20},{28,32},{32,28},{36,40... | collective-permute-start | bytes 1843208 | tf_op jit(solution)/shard_map/ppermute | solution.py:507
  7.0 9.7 %collective-permute-start.1 = (f32[1200,128]{1,0:T(8,128)S(1)}, f32[1200,128]{1,0:T(8,128)S(1)}, u32[]{:S(2)}, u32[]{:S(2)}) collective-permute-start(f32[1200,128]{1,0:T(8,128)S(1)} %get-tuple-element.29), channel_id=1, source_target_pairs={{0,4},{4,0},{8,12},{12,8},{16,20},{20,16},{24,28},{28,24},{32,36},... | collective-permute-start | bytes 1843208 | tf_op jit(solution)/shard_map/ppermute | solution.py:507
  42.2 26.7 %all-to-all-start.1 = ((f32[16,8,128]{2,1,0:T(8,128)}), f32[16,8,128]{2,1,0:T(8,128)S(1)}, u32[]{:S(2)}, u32[]{:S(2)}) async-start(f32[16,8,128]{2,1,0:T(8,128)} %broadcast_in_dim.24), calls=%async_computation.1 | async-start | bytes 131072 | tf_op jit(solution)/shard_map/all_to_all | solution.py:476
  58.1 17.0 %collective-permute-start.2 = (f32[36,16,128]{2,1,0:T(8,128)}, f32[36,16,128]{2,1,0:T(8,128)S(1)}, u32[]{:S(2)}, u32[]{:S(2)}) collective-permute-start(f32[36,16,128]{2,1,0:T(8,128)} %get-tuple-element.40), channel_id=1, source_target_pairs={{4,8},{8,4},{12,16},{16,12},{20,24},{24,20},{28,32},{32,28},{36,40... | collective-permute-start | bytes 884744 | tf_op jit(solution)/shard_map/ppermute | solution.py:507
  60.8 14.3 %collective-permute-start.3 = (f32[36,16,128]{2,1,0:T(8,128)S(1)}, f32[36,16,128]{2,1,0:T(8,128)S(1)}, u32[]{:S(2)}, u32[]{:S(2)}) collective-permute-start(f32[36,16,128]{2,1,0:T(8,128)S(1)} %get-tuple-element.41), channel_id=1, source_target_pairs={{0,4},{4,0},{8,12},{12,8},{16,20},{20,16},{24,28},{28,24},{32,36},... | collective-permute-start | bytes 884744 | tf_op jit(solution)/shard_map/ppermute | solution.py:507
  69.6 13.3 %all-to-all-start.2 = ((f32[32,8,128]{2,1,0:T(8,128)}), f32[32,8,128]{2,1,0:T(8,128)S(1)}, u32[]{:S(2)}, u32[]{:S(2)}) async-start(f32[32,8,128]{2,1,0:T(8,128)} %broadcast_in_dim.25), calls=%async_computation.2 | async-start | bytes 262144 | tf_op jit(solution)/shard_map/all_to_all | solution.py:476

commit v4 on v3

--- a/solution.py
+++ b/solution.py
@@ -249,19 +249,31 @@
     )(*in_hbm(field, cotangent, courant, upwind, *weights))
 
 
-def adjoint(incoming, driven, slope_one, slope_two, w_mid, w_out):
+def adjoint(incoming, rounded, driven, a1, s1, a2, s2, w_mid, w_out, grads, b_out_sum):
+    width = incoming.shape[1]
+    ones = jnp.ones((16, width), BF16)
     g_source = (incoming * driven).astype(BF16)
-    back_two = (dot(w_out, g_source) * slope_two).astype(BF16)
-    back_one = (dot(w_mid, back_two) * slope_one).astype(BF16)
-    return g_source, back_two, back_one
+    grads[160:192] += dot_nt(g_source, a2)
+    b_out_sum[...] += sum(
+        g_source[:, i * WIDTH : (i + 1) * WIDTH].astype(F32) for i in range(width // WIDTH)
+    )
+    back_two = (dot(w_out, g_source) * s2).astype(BF16)
+    grad = dot_nt(jnp.concatenate([a1, ones], axis=0), back_two)
+    grads[:128] += grad[:128]
+    grads[193:194] += grad[128:129]
+    back_one = (dot(w_mid, back_two) * s1).astype(BF16)
+    grad = dot_nt(jnp.concatenate([rounded, ones], axis=0), back_one)
+    grads[128:160] += grad[:32]
+    grads[192:193] += grad[32:33]
+    return back_one
 
 
 def main_kernel(
-    spec, cot, courant, upwind, far, near, far_tail, near_tail,
+    spec, cot, courant, upwind, far, near,
     act_one, slope_one, act_two, slope_two, damped, driven, inside, sent,
     w_in, b_in, w_mid, b_mid, w_out_t, b_out,
     middle_out, back_out, grads,
-    w_in_t, b_in_c, w_mid_t, b_mid_c, b_out_c, w_out, b_out_sum, rim_cs, rim_us, inner_sum, outer_sum,
+    w_in_t, b_in_c, w_mid_t, b_mid_c, b_out_c, w_out, b_out_sum, rim_cs, rim_us,
 ):
     step = pl.program_id(0)
 
@@ -270,22 +282,25 @@
         set_weights(
             w_in, b_in, w_mid, b_mid, w_out_t, b_out, w_in_t, b_in_c, w_mid_t, b_mid_c, b_out_c, w_out
         )
-        set_rim(far_tail, near_tail, rim_cs, rim_us)
-        inner_sum[...] = jnp.zeros_like(inner_sum)
-        outer_sum[...] = jnp.zeros_like(outer_sum)
+        tail = pl.ds(DIRS * FREQS, TAIL)
+        set_rim(far.at[tail], near.at[tail], rim_cs, rim_us)
+        grads[...] = jnp.zeros_like(grads)
         b_out_sum[...] = jnp.zeros_like(b_out_sum)
 
     odd = is_odd()
     sides = (lanes((FREQS, WIDTH)) < HALO).astype(jnp.int32)
-    far_side = jnp.where(odd, 1 - sides, sides) == 1
-    for part in range(BLOCK // CHUNK):
+
+    for k in range(BLOCK // CHUNK):
+        part = step * (BLOCK // CHUNK) + k
+        far_side = jnp.where(odd, 1 - sides, sides) == 1
         at = part * CHUNK
         outside, courants, from_rim = [], [], []
         for i in range(CHUNK):
-            d = step * BLOCK + at + i
-            rows = slice((at + i) * FREQS, (at + i + 1) * FREQS)
-            rim_x = jnp.where(far_side, far[rows], near[rows])
-            rim_g = jnp.where(far_side, near[rows], far[rows])
+            d = at + i
+            rows = pl.ds(pl.multiple_of(d * FREQS, FREQS), FREQS)
+            far_d, near_d = far[rows, :], near[rows, :]
+            rim_x = jnp.where(far_side, far_d, near_d)
+            rim_g = jnp.where(far_side, near_d, far_d)
             index = jnp.broadcast_to(upwind[pl.ds(d, 1), :], (FREQS, WIDTH))
             c = jnp.broadcast_to(courant[pl.ds(d, 1), :], (FREQS, WIDTH))
             outside.append(jnp.where(from_inside(index), 0.0, c * gathered(rim_x, index)))
@@ -299,56 +314,35 @@
         rounded, a1, s1, a2, s2, damping, logistic = forward(
             field, w_in_t[...], b_in_c[...], w_mid_t[...], b_mid_c[...], w_out_t[...], b_out_c[...]
         )
-        gs, q2, q1 = adjoint(g, (-time_step) * field * logistic, s1, s2, w_mid[...], w_out[...])
+        q1 = adjoint(
+            g, rounded, (-time_step) * field * logistic, a1, s1, a2, s2,
+            w_mid[...], w_out[...], grads, b_out_sum,
+        )
         middle = (
             g * (1.0 - c - time_step * damping)
             + dot(w_in[...], q1)
             + sent[part]
             + jnp.concatenate(from_rim, axis=1)
         )
-        gs_0, q2_0, q1_0 = adjoint(
-            middle, driven[part], slope_one[part], slope_two[part], w_mid[...], w_out[...]
-        )
-        put_apart(middle_out, at, middle)
-        back_out[part] = q1_0
-        ones = jnp.ones((16, SPAN), BF16)
-        left = jnp.concatenate([a1, rounded, ones], axis=0)
-        left_0 = jnp.concatenate([act_one[part], x.astype(BF16), ones], axis=0)
-        right, right_0 = jnp.concatenate([q2, q1], axis=0), jnp.concatenate([q2_0, q1_0], axis=0)
-        inner_sum[...] += dot_nt(
-            jnp.concatenate([left, left_0], axis=1), jnp.concatenate([right, right_0], axis=1)
-        )
-        outer_sum[...] += dot_nt(
-            jnp.concatenate([gs, gs_0], axis=0), jnp.concatenate([a2, act_two[part]], axis=0)
-        )
-        b_out_sum[...] += sum(
-            value[:, i * WIDTH : (i + 1) * WIDTH].astype(F32) for i in range(CHUNK) for value in (gs, gs_0)
+        put_apart(middle_out, k * CHUNK, middle)
+        back_out[k] = adjoint(
+            middle, x.astype(BF16), driven[part], act_one[part], slope_one[part], act_two[part],
+            slope_two[part], w_mid[...], w_out[...], grads, b_out_sum,
         )
 
     @pl.when(step == pl.num_programs(0) - 1)
     def _():
-        grads[:128] = inner_sum[:128, :HID]
-        grads[128:160] = inner_sum[128:160, HID:]
-        grads[160:192] = outer_sum[:FREQS, :HID] + outer_sum[FREQS:, HID:]
-        grads[192:] = jnp.zeros((ROWS - 192, WIDTH), F32)
-        grads[192:193] = inner_sum[160:161, HID:]
-        grads[193:194] = inner_sum[160:161, :HID]
         grads[194:195, :FREQS] = jnp.sum(b_out_sum[...].T, axis=0, keepdims=True)
 
 
 def both_adjoints(field, cotangent, courant, upwind, far, near, saved, weights):
-    halo = pl.BlockSpec((BLOCK * FREQS, WIDTH), lambda i: (i, 0))
-    tail = pl.BlockSpec((TAIL, WIDTH), lambda i: (DIRS * FREQS // TAIL, 0))
-    per = BLOCK // CHUNK
     return pl.pallas_call(
         main_kernel,
         grid=(DIRS // BLOCK,),
-        in_specs=[directions(), directions(), whole_rows(), whole_rows(), halo, halo, tail, tail]
-        + saved_specs()
-        + weight_specs(),
+        in_specs=[pl.BlockSpec(memory_space=pltpu.VMEM)] * 20,
         out_specs=[
             directions(),
-            pl.BlockSpec((per, HID, SPAN), lambda i: (i, 0, 0)),
+            pl.BlockSpec((BLOCK // CHUNK, HID, SPAN), lambda i: (i, 0, 0)),
             pl.BlockSpec((ROWS, WIDTH), lambda i: (0, 0)),
         ],
         out_shape=[
@@ -362,15 +356,13 @@
             pltpu.VMEM((FREQS, WIDTH), F32),
             pltpu.VMEM((TAIL, WIDTH), F32),
             pltpu.VMEM((TAIL, WIDTH), jnp.int32),
-            pltpu.VMEM((HID + FREQS + 16, 2 * HID), F32),
-            pltpu.VMEM((2 * FREQS, 2 * HID), F32),
         ],
         compiler_params=pltpu.CompilerParams(vmem_limit_bytes=LIMIT),
         cost_estimate=pl.CostEstimate(
             flops=10 * 24576 * DIRS * WIDTH, bytes_accessed=14_000_000, transcendentals=2 * HID * DIRS * WIDTH
         ),
         name="both_adjoints",
-    )(field, cotangent, courant, upwind, far, near, far, near, *saved, *weights)
+    )(field, cotangent, courant, upwind, far, near, *saved, *weights)
 
 
 def edge_kernel(middle, to_far, to_near):
@@ -485,18 +477,9 @@
 
 def device_groups():
     spaces, cases = lax.axis_size("space"), lax.axis_size("case")
-    grid = np.arange(spaces * cases).reshape(spaces // 32, 32, cases)
-    layers = grid.transpose(0, 2, 1).reshape(-1, 32)
-    columns = grid.transpose(1, 0, 2).reshape(32, -1)
-    return layers.tolist(), columns.tolist()
-
-
-def summed_everywhere(parts):
-    layers, columns = device_groups()
-    wide, deep = len(layers[0]), len(columns[0])
-    parts = exchanged(parts.reshape(wide, ROWS // wide, WIDTH), layers)
-    parts = exchanged(copied(parts, deep), columns)
-    return exchanged(copied(parts, wide), layers).reshape(ROWS, WIDTH)
+    ids = np.arange(spaces * cases).reshape(4, 2, 2, 2, 2, 2, cases)
+    ids = ids.transpose(1, 3, 6, 0, 2, 4, 5).reshape(-1, 32)
+    return ids.tolist(), ids.reshape(2, 2, cases, 32).reshape(-1, 32).T.tolist()
 
 
 def by_pairs(far, near):
@@ -515,8 +498,13 @@
     middle, back, grads = both_adjoints(
         field, incoming, courant, upwind, far, near, saved, weights
     )
-    totals = clipped(summed_everywhere(grads))
+    blocks, alike = device_groups()
+    parts = exchanged(grads.reshape(len(blocks[0]), -1, WIDTH), blocks)
+    parts = exchanged(copied(parts, len(alike[0])), alike)
     far_mid, near_mid = by_pairs(*packed_edges(middle))
+    parts = copied(parts, len(blocks[0]))
+    parts, far_mid, near_mid = lax.optimization_barrier((parts, far_mid, near_mid))
+    totals = clipped(exchanged(parts, blocks).reshape(ROWS, WIDTH))
     state = last_state(
         middle, back, saved[4], w_in, courant, upwind, far_mid, near_mid, far, near
     )

time: 84.2 us -> 90.9 us (1.080)
  blocking collectives: 16.5 us -> 34.2 us
  starting transfers between devices: 34.7 us -> 29.2 us
  waiting for transfers between devices: 10.2 us -> 6.31 us
  Pallas kernels: 20.1 us -> 19.1 us
    all_to_all x1, blocking collectives: 16.5 us -> 34.2 us  [exchanged(): lax.all_to_all(blocks, ('space', 'case'), 0, 0, axis_index_groups=groups,...]
    all_to_all x2, starting transfers between devices: 20.4 us -> 14.1 us  [exchanged(): lax.all_to_all(blocks, ('space', 'case'), 0, 0, axis_index_groups=groups,...]
    all_to_all x2, waiting for transfers between devices: 10.2 us -> 6.29 us  [exchanged(): lax.all_to_all(blocks, ('space', 'case'), 0, 0, axis_index_groups=groups,...]
  transfers between devices with their start and end apart: 6 -> 6, of which waited for: 2 -> 2; matrix products, arithmetic and copies ran while one was open for 1% -> 0% of each run, Pallas kernels for 11% -> 10%
where the time goes in v4:
time: 90.9 us; the launch traced here: 90.4 us
  blocking collectives  34.2 us (38%)
  starting transfers between devices  29.2 us (32%)
  Pallas kernels  19.1 us (21%)
  waiting for transfers between devices  6.31 us (7%)
    all_to_all x1, blocking collectives, exchanged(): lax.all_to_all(blocks, ('space', 'case'), 0, 0, axis_index_groups=groups,...  34.2 us
    all_to_all x2, starting transfers between devices, exchanged(): lax.all_to_all(blocks, ('space', 'case'), 0, 0, axis_index_groups=groups,...  14.1 us
    ppermute x2, starting transfers between devices, by_pairs(): lax.ppermute(far, 'space', swapped(1))  8.25 us
    pallas_call x1, Pallas kernels, both_adjoints(): pl.pallas_call(main_kernel, grid=(DIRS // BLOCK,), in_specs=[pl.BlockSpec...  7.41 us
    ppermute x2, starting transfers between devices, by_pairs(): lax.ppermute(near, 'space', swapped(0))  6.81 us
    all_to_all x2, waiting for transfers between devices, exchanged(): lax.all_to_all(blocks, ('space', 'case'), 0, 0, axis_index_groups=groups,...  6.29 us
    pallas_call x1, Pallas kernels, forward_saved(): pl.pallas_call(forward_kernel, grid=(DIRS // BLOCK,), in_specs=[direction...  4.74 us
    pallas_call x1, Pallas kernels, last_state(): pl.pallas_call(last_kernel, grid=(DIRS // BLOCK,), in_specs=[directions()...  3.77 us
  transfers between devices with their start and end apart: 6, of which 2 were waited for; matrix products, arithmetic and copies ran while one was open for 0% of the time, Pallas kernels for 10%

profile of v4, /device:TPU:1, one launch (start us, length us, event | category | flops | bytes accessed | tf_op | source)
XLA Modules:
  0.0 90.4 jit_solution(11698453061596242622)
XLA Ops:
  0.6 1.5 %pack_halo.1 = (f32[1200,128]{1,0:T(8,128)S(1)}, f32[1200,128]{1,0:T(8,128)S(1)}) custom-call(f32[1,36,32,128]{3,2,1,0:T(8,128)} %spec.1, f32[1,36,32,128]{3,2,1,0:T(8,128)} %cot.1, f32[36,128]{1,0:T(8,128)} %courant.7, s32[36,128]{1,0:T(8,128)} %upwind.7), custom_call_target="tpu_custom_call" | custom-call | tf_op jit(solution)/shard_map/pack_halo/pallas_call | solution.py:74
  2.1 0.0 copy-start
  2.1 0.0 copy-start.1
  2.1 0.0 copy-start.2
  2.1 0.0 copy-start.3
  2.2 0.0 copy-start.4
  2.2 0.0 copy-start.5
  2.2 0.0 copy-start.6
  2.2 0.0 copy-start.7
  2.2 0.0 copy-start.8
  2.2 0.0 copy-start.9
  2.2 4.7 %collective-permute-start = (f32[1200,128]{1,0:T(8,128)S(1)}, f32[1200,128]{1,0:T(8,128)S(1)}, u32[]{:S(2)}, u32[]{:S(2)}) collective-permute-start(f32[1200,128]{1,0:T(8,128)S(1)} %get-tuple-element.31), channel_id=1, source_target_pairs={{4,8},{8,4},{12,16},{16,12},{20,24},{24,20},{28,32},{32,28},{36,40... | collective-permute-start | bytes 1843208 | tf_op jit(solution)/shard_map/ppermute | solution.py:490
  7.0 4.9 %collective-permute-start.1 = (f32[1200,128]{1,0:T(8,128)S(1)}, f32[1200,128]{1,0:T(8,128)S(1)}, u32[]{:S(2)}, u32[]{:S(2)}) collective-permute-start(f32[1200,128]{1,0:T(8,128)S(1)} %get-tuple-element.32), channel_id=1, source_target_pairs={{0,4},{4,0},{8,12},{12,8},{16,20},{20,16},{24,28},{28,24},{32,36},... | collective-permute-start | bytes 1843208 | tf_op jit(solution)/shard_map/ppermute | solution.py:490
  11.9 4.7 %forward_start.1 = (bf16[3,128,1536]{2,1,0:T(8,128)(2,1)S(1)}, f32[3,128,1536]{2,1,0:T(8,128)S(1)}, bf16[3,128,1536]{2,1,0:T(8,128)(2,1)S(1)}, f32[3,128,1536]{2...) custom-call(f32[36,32,128]{2,1,0:T(8,128)} %bitcast.12, ...), custom_call_target="tpu_custom_call" | custom-call | flops 226492416 | bytes 9000000 | tf_op jit(solution)/shard_map/forward_start/pallas_call | solution.py:237
  16.6 0.0 collective-permute-done.far.far_tail
  16.6 0.0 collective-permute-done.1.near.near_tail
  16.6 0.0 copy-done
  16.6 0.0 copy-done.1
  16.7 0.0 copy-done.2
  16.7 0.0 copy-done.3
  16.7 0.0 copy-done.4
  16.7 0.0 copy-done.5
  16.7 0.0 copy-done.6
  16.7 0.0 copy-done.7
  16.7 0.0 copy-done.8
  16.7 0.0 copy-done.9
  16.7 7.4 %both_adjoints.1 = (f32[36,32,128]{2,1,0:T(8,128)S(1)}, bf16[3,128,1536]{2,1,0:T(8,128)(2,1)}, f32[256,128]{1,0:T(8,128)}) custom-call(f32[36,32,128]{2,1,0:T(8,128)S(1)} %bitcast.13, f32[36,32,128]{2,1,0:T(8,128)S(1)} %bitcast.15, f32[36,128]{1,0:T(8,128)S(1)} %copy-done.2, s32[36,128]{1,0:T(8,128)S(1)} %copy-done.3, ...), custom_call_target="tpu_custom_call" | custom-call | flops 1132462080 | bytes 14000000 | tf_op jit(solution)/shard_map/both_adjoints/pallas_call | solution.py:339
  24.1 9.0 %all-to-all-start = ((f32[32,8,128]{2,1,0:T(8,128)}), f32[32,8,128]{2,1,0:T(8,128)S(1)}, u32[]{:S(2)}, u32[]{:S(2)}) async-start(f32[32,8,128]{2,1,0:T(8,128)} %bitcast.6), calls=%async_computation | async-start | bytes 262144 | tf_op jit(solution)/shard_map/all_to_all | solution.py:468
  33.1 0.9 %pack_edges.1 = (f32[36,16,128]{2,1,0:T(8,128)}, f32[36,16,128]{2,1,0:T(8,128)S(1)}) custom-call(f32[36,32,128]{2,1,0:T(8,128)S(1)} %get-tuple-element.41.middle), custom_call_target="tpu_custom_call" | custom-call | flops 1000000 | bytes 1200000 | tf_op jit(solution)/shard_map/pack_edges/pallas_call | solution.py:379
  34.0 3.5 %collective-permute-start.2 = (f32[36,16,128]{2,1,0:T(8,128)}, f32[36,16,128]{2,1,0:T(8,128)S(1)}, u32[]{:S(2)}, u32[]{:S(2)}) collective-permute-start(f32[36,16,128]{2,1,0:T(8,128)} %get-tuple-element.44), channel_id=1, source_target_pairs={{4,8},{8,4},{12,16},{16,12},{20,24},{24,20},{28,32},{32,28},{36,40... | collective-permute-start | bytes 884744 | tf_op jit(solution)/shard_map/ppermute | solution.py:490
  37.6 1.9 %collective-permute-start.3 = (f32[36,16,128]{2,1,0:T(8,128)S(1)}, f32[36,16,128]{2,1,0:T(8,128)S(1)}, u32[]{:S(2)}, u32[]{:S(2)}) collective-permute-start(f32[36,16,128]{2,1,0:T(8,128)S(1)} %get-tuple-element.45), channel_id=1, source_target_pairs={{0,4},{4,0},{8,12},{12,8},{16,20},{20,16},{24,28},{28,24},{32,36},... | collective-permute-start | bytes 884744 | tf_op jit(solution)/shard_map/ppermute | solution.py:490
  39.5 1.8 %all-to-all-done = f32[32,8,128]{2,1,0:T(8,128)S(1)} async-done(((f32[32,8,128]{2,1,0:T(8,128)}), f32[32,8,128]{2,1,0:T(8,128)S(1)}, u32[]{:S(2)}, u32[]{:S(2)}) %all-to-all-start) | async-done | bytes 131104 | tf_op jit(solution)/shard_map/all_to_all | solution.py:468
  41.3 34.2 %all_to_all.15 = f32[16,8,128]{2,1,0:T(8,128)S(1)} all-to-all(f32[16,8,128]{2,1,0:T(8,128)S(1)} %broadcast_in_dim.24), channel_id=1, replica_groups={{0,1,2,3,16,17,18,19,64,65,66,67,80,81,82,83},{4,5,6,7,20,21,22,23,68,6..., dimensions={0} | all-to-all | bytes 131072 | tf_op jit(solution)/shard_map/all_to_all | solution.py:468
  75.5 0.0 collective-permute-done.2.far
  75.5 0.0 collective-permute-done.3.near
  75.5 0.7 broadcast_in_dim.25
  76.2 5.1 %all-to-all-start.2 = ((f32[32,8,128]{2,1,0:T(8,128)}), f32[32,8,128]{2,1,0:T(8,128)S(1)}, u32[]{:S(2)}, u32[]{:S(2)}) async-start(f32[32,8,128]{2,1,0:T(8,128)} %broadcast_in_dim.25), calls=%async_computation.2 | async-start | bytes 262144 | tf_op jit(solution)/shard_map/all_to_all | solution.py:468
  81.3 3.8 %last_state.1 = f32[1,36,32,128]{3,2,1,0:T(8,128)} custom-call(f32[36,32,128]{2,1,0:T(8,128)S(1)} %get-tuple-element.41.middle, bf16[3,128,1536]{2,1,0:T(8,128)(2,1)} %get-tuple-element.42.back, f32[3,32,1536]{2,1,0:T(8,128)S(1)} %get-tuple-element.37.damped, bf16[32,128]{1,0:T(8,128)(2,1)S(1)} %copy-done.5, f32[36,128]{1,0:T(8,128)S(1)} %copy-done.2, ...), custom_call_target="tpu_custom_call" | custom-call | flops 150994944 | bytes 4000000 | tf_op jit(solution)/shard_map/last_state/pallas_call | solution.py:421
  85.1 4.5 %all-to-all-done.2 = f32[32,8,128]{2,1,0:T(8,128)S(1)} async-done(((f32[32,8,128]{2,1,0:T(8,128)}), f32[32,8,128]{2,1,0:T(8,128)S(1)}, u32[]{:S(2)}, u32[]{:S(2)}) %all-to-all-start.2) | async-done | bytes 131104 | tf_op jit(solution)/shard_map/all_to_all | solution.py:468
  89.6 0.8 clip.1
  (3 shorter events, 0.1 us)
Async XLA Ops:
  2.1 14.5 %copy-start = (f32[1,36,32,128]{3,2,1,0:T(8,128)S(1)}, f32[1,36,32,128]{3,2,1,0:T(8,128)}, u32[]{:S(2)}) copy-start(f32[1,36,32,128]{3,2,1,0:T(8,128)} %spec.1) | copy-start | bytes 1769476
  2.1 14.5 %copy-start.1 = (f32[1,36,32,128]{3,2,1,0:T(8,128)S(1)}, f32[1,36,32,128]{3,2,1,0:T(8,128)}, u32[]{:S(2)}) copy-start(f32[1,36,32,128]{3,2,1,0:T(8,128)} %cot.1) | copy-start | bytes 1769476
  2.1 14.5 %copy-start.2 = (f32[36,128]{1,0:T(8,128)S(1)}, f32[36,128]{1,0:T(8,128)}, u32[]{:S(2)}) copy-start(f32[36,128]{1,0:T(8,128)} %courant.7) | copy-start | bytes 55300
  2.1 14.5 %copy-start.3 = (s32[36,128]{1,0:T(8,128)S(1)}, s32[36,128]{1,0:T(8,128)}, u32[]{:S(2)}) copy-start(s32[36,128]{1,0:T(8,128)} %upwind.7) | copy-start | bytes 55300
  2.2 14.5 %copy-start.4 = (bf16[128,128]{1,0:T(8,128)(2,1)S(1)}, bf16[128,128]{1,0:T(8,128)(2,1)}, u32[]{:S(2)}) copy-start(bf16[128,128]{1,0:T(8,128)(2,1)} %w_mid.3) | copy-start | bytes 98308
  2.2 14.5 %copy-start.5 = (bf16[32,128]{1,0:T(8,128)(2,1)S(1)}, bf16[32,128]{1,0:T(8,128)(2,1)}, u32[]{:S(2)}) copy-start(bf16[32,128]{1,0:T(8,128)(2,1)} %w_in.5) | copy-start | bytes 24580
  2.2 14.5 %copy-start.6 = (bf16[128,32]{0,1:T(8,128)(2,1)S(1)}, bf16[128,32]{0,1:T(8,128)(2,1)}, u32[]{:S(2)}) copy-start(bf16[128,32]{0,1:T(8,128)(2,1)} %param.18) | copy-start | bytes 24580
  2.2 14.5 %copy-start.7 = (f32[128]{0:T(128)S(1)}, f32[128]{0:T(128)}, u32[]{:S(2)}) copy-start(f32[128]{0:T(128)} %param.15) | copy-start | bytes 1540
  2.2 14.5 %copy-start.8 = (f32[128]{0:T(128)S(1)}, f32[128]{0:T(128)}, u32[]{:S(2)}) copy-start(f32[128]{0:T(128)} %param.17) | copy-start | bytes 1540
  2.2 14.5 %copy-start.9 = (f32[32]{0:T(128)S(1)}, f32[32]{0:T(128)}, u32[]{:S(2)}) copy-start(f32[32]{0:T(128)} %param.19) | copy-start | bytes 388
  2.2 14.4 %collective-permute-start = (f32[1200,128]{1,0:T(8,128)S(1)}, f32[1200,128]{1,0:T(8,128)S(1)}, u32[]{:S(2)}, u32[]{:S(2)}) collective-permute-start(f32[1200,128]{1,0:T(8,128)S(1)} %get-tuple-element.31), channel_id=1, source_target_pairs={{4,8},{8,4},{12,16},{16,12},{20,24},{24,20},{28,32},{32,28},{36,40... | collective-permute-start | bytes 1843208 | tf_op jit(solution)/shard_map/ppermute | solution.py:490
  7.0 9.7 %collective-permute-start.1 = (f32[1200,128]{1,0:T(8,128)S(1)}, f32[1200,128]{1,0:T(8,128)S(1)}, u32[]{:S(2)}, u32[]{:S(2)}) collective-permute-start(f32[1200,128]{1,0:T(8,128)S(1)} %get-tuple-element.32), channel_id=1, source_target_pairs={{0,4},{4,0},{8,12},{12,8},{16,20},{20,16},{24,28},{28,24},{32,36},... | collective-permute-start | bytes 1843208 | tf_op jit(solution)/shard_map/ppermute | solution.py:490
  24.1 17.1 %all-to-all-start = ((f32[32,8,128]{2,1,0:T(8,128)}), f32[32,8,128]{2,1,0:T(8,128)S(1)}, u32[]{:S(2)}, u32[]{:S(2)}) async-start(f32[32,8,128]{2,1,0:T(8,128)} %bitcast.6), calls=%async_computation | async-start | bytes 262144 | tf_op jit(solution)/shard_map/all_to_all | solution.py:468
  34.0 41.5 %collective-permute-start.2 = (f32[36,16,128]{2,1,0:T(8,128)}, f32[36,16,128]{2,1,0:T(8,128)S(1)}, u32[]{:S(2)}, u32[]{:S(2)}) collective-permute-start(f32[36,16,128]{2,1,0:T(8,128)} %get-tuple-element.44), channel_id=1, source_target_pairs={{4,8},{8,4},{12,16},{16,12},{20,24},{24,20},{28,32},{32,28},{36,40... | collective-permute-start | bytes 884744 | tf_op jit(solution)/shard_map/ppermute | solution.py:490
  37.6 37.9 %collective-permute-start.3 = (f32[36,16,128]{2,1,0:T(8,128)S(1)}, f32[36,16,128]{2,1,0:T(8,128)S(1)}, u32[]{:S(2)}, u32[]{:S(2)}) collective-permute-start(f32[36,16,128]{2,1,0:T(8,128)S(1)} %get-tuple-element.45), channel_id=1, source_target_pairs={{0,4},{4,0},{8,12},{12,8},{16,20},{20,16},{24,28},{28,24},{32,36},... | collective-permute-start | bytes 884744 | tf_op jit(solution)/shard_map/ppermute | solution.py:490
  76.2 13.4 %all-to-all-start.2 = ((f32[32,8,128]{2,1,0:T(8,128)}), f32[32,8,128]{2,1,0:T(8,128)S(1)}, u32[]{:S(2)}, u32[]{:S(2)}) async-start(f32[32,8,128]{2,1,0:T(8,128)} %broadcast_in_dim.25), calls=%async_computation.2 | async-start | bytes 262144 | tf_op jit(solution)/shard_map/all_to_all | solution.py:468

commit v5 on v3

--- a/solution.py
+++ b/solution.py
@@ -13,6 +13,7 @@
 WIDTH = 128
 TAIL = 48
 CHUNK = 12
+HALF = 6
 BLOCK = 12
 ROWS = 256
 
@@ -123,14 +124,18 @@
     return act.astype(BF16), logistic + act * (1.0 - logistic)
 
 
+def damping_of(source):
+    damping = jnp.maximum(source, 0.0) + jnp.log(1.0 + jnp.exp(-jnp.abs(source)))
+    return damping, 0.5 + 0.5 * jnp.tanh(0.5 * source)
+
+
 def forward(x, w_in_t, b_in, w_mid_t, b_mid, w_out_t, b_out):
     width = x.shape[1]
     rounded = x.astype(BF16)
     act_one, slope_one = activated(dot(w_in_t, rounded) + wide(b_in, width))
     act_two, slope_two = activated(dot(w_mid_t, act_one) + wide(b_mid, width))
     source = dot(w_out_t, act_two) + wide(b_out, width)
-    damping = jnp.maximum(source, 0.0) + jnp.log(1.0 + jnp.exp(-jnp.abs(source)))
-    logistic = 0.5 + 0.5 * jnp.tanh(0.5 * source)
+    damping, logistic = damping_of(source)
     return rounded, act_one, slope_one, act_two, slope_two, damping, logistic
 
 
@@ -249,11 +254,14 @@
     )(*in_hbm(field, cotangent, courant, upwind, *weights))
 
 
-def adjoint(incoming, driven, slope_one, slope_two, w_mid, w_out):
-    g_source = (incoming * driven).astype(BF16)
-    back_two = (dot(w_out, g_source) * slope_two).astype(BF16)
-    back_one = (dot(w_mid, back_two) * slope_one).astype(BF16)
-    return g_source, back_two, back_one
+def alternated(chains):
+    waiting, running = list(chains), []
+    while waiting or running:
+        if waiting:
+            running.append(waiting.pop(0))
+        for chain in list(running):
+            if next(chain, "done") == "done":
+                running.remove(chain)
 
 
 def main_kernel(
@@ -261,7 +269,7 @@
     act_one, slope_one, act_two, slope_two, damped, driven, inside, sent,
     w_in, b_in, w_mid, b_mid, w_out_t, b_out,
     middle_out, back_out, grads,
-    w_in_t, b_in_c, w_mid_t, b_mid_c, b_out_c, w_out, b_out_sum, rim_cs, rim_us, inner_sum, outer_sum,
+    w_in_t, b_in_c, w_mid_t, b_mid_c, b_out_c, w_out, b_out_sum, rim_cs, rim_us,
 ):
     step = pl.program_id(0)
 
@@ -271,68 +279,93 @@
             w_in, b_in, w_mid, b_mid, w_out_t, b_out, w_in_t, b_in_c, w_mid_t, b_mid_c, b_out_c, w_out
         )
         set_rim(far_tail, near_tail, rim_cs, rim_us)
-        inner_sum[...] = jnp.zeros_like(inner_sum)
-        outer_sum[...] = jnp.zeros_like(outer_sum)
+        grads[...] = jnp.zeros_like(grads)
         b_out_sum[...] = jnp.zeros_like(b_out_sum)
 
     odd = is_odd()
     sides = (lanes((FREQS, WIDTH)) < HALO).astype(jnp.int32)
     far_side = jnp.where(odd, 1 - sides, sides) == 1
-    for part in range(BLOCK // CHUNK):
-        at = part * CHUNK
+    ones = jnp.ones((16, HALF * WIDTH), BF16)
+
+    def adjoint(incoming, rounded, driven_by, a1, s1, a2, s2, keep):
+        g_source = (incoming * driven_by).astype(BF16)
+        b_out_sum[...] += sum(
+            g_source[:, i * WIDTH : (i + 1) * WIDTH].astype(F32) for i in range(HALF)
+        )
+        yield
+        back = dot(w_out[...], g_source)
+        grads[160:192] += dot_nt(g_source, a2)
+        yield
+        back_two = (back * s2).astype(BF16)
+        yield
+        back = dot(w_mid[...], back_two)
+        grad = dot_nt(jnp.concatenate([a1, ones], axis=0), back_two)
+        grads[:128] += grad[:128]
+        grads[193:194] += grad[128:129]
+        yield
+        back_one = (back * s1).astype(BF16)
+        yield
+        grad = dot_nt(jnp.concatenate([rounded, ones], axis=0), back_one)
+        grads[128:160] += grad[:32]
+        grads[192:193] += grad[32:33]
+        keep.append(back_one)
+
+    def chain(at):
+        columns = slice(at * WIDTH, (at + HALF) * WIDTH)
         outside, courants, from_rim = [], [], []
-        for i in range(CHUNK):
+        for i in range(HALF):
             d = step * BLOCK + at + i
             rows = slice((at + i) * FREQS, (at + i + 1) * FREQS)
             rim_x = jnp.where(far_side, far[rows], near[rows])
-            rim_g = jnp.where(far_side, near[rows], far[rows])
             index = jnp.broadcast_to(upwind[pl.ds(d, 1), :], (FREQS, WIDTH))
             c = jnp.broadcast_to(courant[pl.ds(d, 1), :], (FREQS, WIDTH))
             outside.append(jnp.where(from_inside(index), 0.0, c * gathered(rim_x, index)))
             courants.append(c)
+        c = jnp.concatenate(courants, axis=1)
+        field = inside[0, :, columns] + jnp.concatenate(outside, axis=1)
+        rounded = field.astype(BF16)
+        yield
+        pre = dot(w_in_t[...], rounded)
+        yield
+        a1, s1 = activated(pre + wide(b_in_c[...], HALF * WIDTH))
+        yield
+        pre = dot(w_mid_t[...], a1)
+        yield
+        a2, s2 = activated(pre + wide(b_mid_c[...], HALF * WIDTH))
+        yield
+        source = dot(w_out_t[...], a2)
+        for i in range(HALF):
+            d = step * BLOCK + at + i
+            rows = slice((at + i) * FREQS, (at + i + 1) * FREQS)
+            rim_g = jnp.where(far_side, near[rows], far[rows])
             rim_c, rim_u = rim_cs[pl.ds(d, 1), :], rim_us[pl.ds(d, 1), :]
             from_rim.append(spread(rim_c * rim_g, one_hot(jnp.broadcast_to(rim_u, (WIDTH, WIDTH)))))
-        x = side_by_side(spec, at)
-        g = side_by_side(cot, at)
-        c = jnp.concatenate(courants, axis=1)
-        field = inside[part] + jnp.concatenate(outside, axis=1)
-        rounded, a1, s1, a2, s2, damping, logistic = forward(
-            field, w_in_t[...], b_in_c[...], w_mid_t[...], b_mid_c[...], w_out_t[...], b_out_c[...]
-        )
-        gs, q2, q1 = adjoint(g, (-time_step) * field * logistic, s1, s2, w_mid[...], w_out[...])
+        yield
+        damping, logistic = damping_of(source + wide(b_out_c[...], HALF * WIDTH))
+        g = jnp.concatenate([cot[at + i] for i in range(HALF)], axis=1)
+        kept = []
+        yield from adjoint(g, rounded, (-time_step) * field * logistic, a1, s1, a2, s2, kept)
+        back = dot(w_in[...], kept[0])
+        yield
         middle = (
             g * (1.0 - c - time_step * damping)
-            + dot(w_in[...], q1)
-            + sent[part]
+            + back
+            + sent[0, :, columns]
             + jnp.concatenate(from_rim, axis=1)
         )
-        gs_0, q2_0, q1_0 = adjoint(
-            middle, driven[part], slope_one[part], slope_two[part], w_mid[...], w_out[...]
+        for i in range(HALF):
+            middle_out[at + i] = middle[:, i * WIDTH : (i + 1) * WIDTH]
+        x = jnp.concatenate([spec[at + i] for i in range(HALF)], axis=1)
+        yield from adjoint(
+            middle, x.astype(BF16), driven[0, :, columns], act_one[0, :, columns],
+            slope_one[0, :, columns], act_two[0, :, columns], slope_two[0, :, columns], kept,
         )
-        put_apart(middle_out, at, middle)
-        back_out[part] = q1_0
-        ones = jnp.ones((16, SPAN), BF16)
-        left = jnp.concatenate([a1, rounded, ones], axis=0)
-        left_0 = jnp.concatenate([act_one[part], x.astype(BF16), ones], axis=0)
-        right, right_0 = jnp.concatenate([q2, q1], axis=0), jnp.concatenate([q2_0, q1_0], axis=0)
-        inner_sum[...] += dot_nt(
-            jnp.concatenate([left, left_0], axis=1), jnp.concatenate([right, right_0], axis=1)
-        )
-        outer_sum[...] += dot_nt(
-            jnp.concatenate([gs, gs_0], axis=0), jnp.concatenate([a2, act_two[part]], axis=0)
-        )
-        b_out_sum[...] += sum(
-            value[:, i * WIDTH : (i + 1) * WIDTH].astype(F32) for i in range(CHUNK) for value in (gs, gs_0)
-        )
+        back_out[0, :, columns] = kept[1]
+
+    alternated(chain(at) for at in range(0, BLOCK, HALF))
 
     @pl.when(step == pl.num_programs(0) - 1)
     def _():
-        grads[:128] = inner_sum[:128, :HID]
-        grads[128:160] = inner_sum[128:160, HID:]
-        grads[160:192] = outer_sum[:FREQS, :HID] + outer_sum[FREQS:, HID:]
-        grads[192:] = jnp.zeros((ROWS - 192, WIDTH), F32)
-        grads[192:193] = inner_sum[160:161, HID:]
-        grads[193:194] = inner_sum[160:161, :HID]
         grads[194:195, :FREQS] = jnp.sum(b_out_sum[...].T, axis=0, keepdims=True)
 
 
@@ -362,8 +395,6 @@
             pltpu.VMEM((FREQS, WIDTH), F32),
             pltpu.VMEM((TAIL, WIDTH), F32),
             pltpu.VMEM((TAIL, WIDTH), jnp.int32),
-            pltpu.VMEM((HID + FREQS + 16, 2 * HID), F32),
-            pltpu.VMEM((2 * FREQS, 2 * HID), F32),
         ],
         compiler_params=pltpu.CompilerParams(vmem_limit_bytes=LIMIT),
         cost_estimate=pl.CostEstimate(

time: 84.2 us -> 83.3 us (0.989)
  Pallas kernels: 20.1 us -> 19.2 us
where the time goes in v5:
time: 83.3 us; the launch traced here: 82.9 us
  starting transfers between devices  34.7 us (42%)
  Pallas kernels  19.2 us (23%)
  blocking collectives  16.5 us (20%)
  waiting for transfers between devices  10.2 us (12%)
  local copies, waits for them, and re-layouts  1.36 us (2%)
  between operations  0.88 us (1%)
    all_to_all x2, starting transfers between devices, exchanged(): lax.all_to_all(blocks, ('space', 'case'), 0, 0, axis_index_groups=groups,...  20.4 us
    all_to_all x1, blocking collectives, exchanged(): lax.all_to_all(blocks, ('space', 'case'), 0, 0, axis_index_groups=groups,...  16.5 us
    all_to_all x2, waiting for transfers between devices, exchanged(): lax.all_to_all(blocks, ('space', 'case'), 0, 0, axis_index_groups=groups,...  10.2 us
    pallas_call x1, Pallas kernels, both_adjoints(): pl.pallas_call(main_kernel, grid=(DIRS // BLOCK,), in_specs=[directions()...  7.48 us
    ppermute x2, starting transfers between devices, by_pairs(): lax.ppermute(far, 'space', swapped(1))  7.44 us
    ppermute x2, starting transfers between devices, by_pairs(): lax.ppermute(near, 'space', swapped(0))  6.81 us
    pallas_call x1, Pallas kernels, forward_saved(): pl.pallas_call(forward_kernel, grid=(DIRS // BLOCK,), in_specs=[direction...  4.74 us
    pallas_call x1, Pallas kernels, last_state(): pl.pallas_call(last_kernel, grid=(DIRS // BLOCK,), in_specs=[directions()...  3.78 us
  transfers between devices with their start and end apart: 6, of which 2 were waited for; matrix products, arithmetic and copies ran while one was open for 1% of the time, Pallas kernels for 11%

profile of v5, /device:TPU:1, one launch (start us, length us, event | category | flops | bytes accessed | tf_op | source)
XLA Modules:
  0.0 82.9 jit_solution(3459974759439141323)
XLA Ops:
  0.6 1.5 %pack_halo.1 = (f32[1200,128]{1,0:T(8,128)S(1)}, f32[1200,128]{1,0:T(8,128)S(1)}) custom-call(f32[1,36,32,128]{3,2,1,0:T(8,128)} %spec.1, f32[1,36,32,128]{3,2,1,0:T(8,128)} %cot.1, f32[36,128]{1,0:T(8,128)} %courant.7, s32[36,128]{1,0:T(8,128)} %upwind.7), custom_call_target="tpu_custom_call" | custom-call | tf_op jit(solution)/shard_map/pack_halo/pallas_call | solution.py:75
  2.1 0.0 copy-start
  2.1 0.0 copy-start.1
  2.1 0.0 copy-start.2
  2.1 0.0 copy-start.3
  2.2 0.0 copy-start.4
  2.2 0.0 copy-start.5
  2.2 0.0 copy-start.6
  2.2 0.0 copy-start.7
  2.2 0.0 copy-start.8
  2.2 0.0 copy-start.9
  2.2 4.7 %collective-permute-start = (f32[1200,128]{1,0:T(8,128)S(1)}, f32[1200,128]{1,0:T(8,128)S(1)}, u32[]{:S(2)}, u32[]{:S(2)}) collective-permute-start(f32[1200,128]{1,0:T(8,128)S(1)} %get-tuple-element.28), channel_id=1, source_target_pairs={{4,8},{8,4},{12,16},{16,12},{20,24},{24,20},{28,32},{32,28},{36,40... | collective-permute-start | bytes 1843208 | tf_op jit(solution)/shard_map/ppermute | solution.py:538
  7.0 4.9 %collective-permute-start.1 = (f32[1200,128]{1,0:T(8,128)S(1)}, f32[1200,128]{1,0:T(8,128)S(1)}, u32[]{:S(2)}, u32[]{:S(2)}) collective-permute-start(f32[1200,128]{1,0:T(8,128)S(1)} %get-tuple-element.29), channel_id=1, source_target_pairs={{0,4},{4,0},{8,12},{12,8},{16,20},{20,16},{24,28},{28,24},{32,36},... | collective-permute-start | bytes 1843208 | tf_op jit(solution)/shard_map/ppermute | solution.py:538
  11.9 4.7 %forward_start.1 = (bf16[3,128,1536]{2,1,0:T(8,128)(2,1)S(1)}, f32[3,128,1536]{2,1,0:T(8,128)S(1)}, bf16[3,128,1536]{2,1,0:T(8,128)(2,1)S(1)}, f32[3,128,1536]{2...) custom-call(f32[36,32,128]{2,1,0:T(8,128)} %bitcast.12, ...), custom_call_target="tpu_custom_call" | custom-call | flops 226492416 | bytes 9000000 | tf_op jit(solution)/shard_map/forward_start/pallas_call | solution.py:242
  16.6 0.0 collective-permute-done.far.far_tail
  16.6 0.0 collective-permute-done.1.near.near_tail
  16.6 0.0 copy-done
  16.6 0.0 copy-done.1
  16.7 0.0 copy-done.2
  16.7 0.0 copy-done.3
  16.7 0.0 copy-done.4
  16.7 0.0 copy-done.5
  16.7 0.0 copy-done.6
  16.7 0.0 copy-done.7
  16.7 0.0 copy-done.8
  16.7 0.0 copy-done.9
  16.7 7.5 %both_adjoints.1 = (f32[36,32,128]{2,1,0:T(8,128)S(1)}, bf16[3,128,1536]{2,1,0:T(8,128)(2,1)}, f32[256,128]{1,0:T(8,128)S(1)}) custom-call(f32[36,32,128]{2,1,0:T(8,128)S(1)} %bitcast.13, f32[36,32,128]{2,1,0:T(8,128)S(1)} %bitcast.15, f32[36,128]{1,0:T(8,128)S(1)} %copy-done.2, s32[36,128]{1,0:T(8,128)S(1)} %copy-done.3, ...), custom_call_target="tpu_custom_call" | custom-call | flops 1132462080 | bytes 14000000 | tf_op jit(solution)/shard_map/both_adjoints/pallas_call | solution.py:376
  24.2 16.5 %all_to_all.15 = f32[32,8,128]{2,1,0:T(8,128)S(1)} all-to-all(f32[32,8,128]{2,1,0:T(8,128)S(1)} %bitcast.17), channel_id=1, replica_groups={{0,4,8,12,16,20,24,28,32,36,40,44,48,52,56,60,64,68,72,76,80,84,88,92,9..., dimensions={0} | all-to-all | bytes 262144 | tf_op jit(solution)/shard_map/all_to_all | solution.py:507
  40.7 0.6 broadcast_in_dim.24
  41.4 14.9 %all-to-all-start.1 = ((f32[16,8,128]{2,1,0:T(8,128)}), f32[16,8,128]{2,1,0:T(8,128)S(1)}, u32[]{:S(2)}, u32[]{:S(2)}) async-start(f32[16,8,128]{2,1,0:T(8,128)} %broadcast_in_dim.24), calls=%async_computation.1 | async-start | bytes 131072 | tf_op jit(solution)/shard_map/all_to_all | solution.py:507
  56.3 0.9 %pack_edges.1 = (f32[36,16,128]{2,1,0:T(8,128)}, f32[36,16,128]{2,1,0:T(8,128)S(1)}) custom-call(f32[36,32,128]{2,1,0:T(8,128)S(1)} %get-tuple-element.38.middle), custom_call_target="tpu_custom_call" | custom-call | flops 1000000 | bytes 1200000 | tf_op jit(solution)/shard_map/pack_edges/pallas_call | solution.py:418
  57.2 2.7 %collective-permute-start.2 = (f32[36,16,128]{2,1,0:T(8,128)}, f32[36,16,128]{2,1,0:T(8,128)S(1)}, u32[]{:S(2)}, u32[]{:S(2)}) collective-permute-start(f32[36,16,128]{2,1,0:T(8,128)} %get-tuple-element.40), channel_id=1, source_target_pairs={{4,8},{8,4},{12,16},{16,12},{20,24},{24,20},{28,32},{32,28},{36,40... | collective-permute-start | bytes 884744 | tf_op jit(solution)/shard_map/ppermute | solution.py:538
  60.0 1.9 %collective-permute-start.3 = (f32[36,16,128]{2,1,0:T(8,128)S(1)}, f32[36,16,128]{2,1,0:T(8,128)S(1)}, u32[]{:S(2)}, u32[]{:S(2)}) collective-permute-start(f32[36,16,128]{2,1,0:T(8,128)S(1)} %get-tuple-element.41), channel_id=1, source_target_pairs={{0,4},{4,0},{8,12},{12,8},{16,20},{20,16},{24,28},{28,24},{32,36},... | collective-permute-start | bytes 884744 | tf_op jit(solution)/shard_map/ppermute | solution.py:538
  61.9 6.2 %all-to-all-done.1 = f32[16,8,128]{2,1,0:T(8,128)S(1)} async-done(((f32[16,8,128]{2,1,0:T(8,128)}), f32[16,8,128]{2,1,0:T(8,128)S(1)}, u32[]{:S(2)}, u32[]{:S(2)}) %all-to-all-start.1) | async-done | bytes 65568 | tf_op jit(solution)/shard_map/all_to_all | solution.py:507
  68.1 0.7 broadcast_in_dim.25
  68.8 5.5 %all-to-all-start.2 = ((f32[32,8,128]{2,1,0:T(8,128)}), f32[32,8,128]{2,1,0:T(8,128)S(1)}, u32[]{:S(2)}, u32[]{:S(2)}) async-start(f32[32,8,128]{2,1,0:T(8,128)} %broadcast_in_dim.25), calls=%async_computation.2 | async-start | bytes 262144 | tf_op jit(solution)/shard_map/all_to_all | solution.py:507
  74.3 0.0 collective-permute-done.2.far
  74.3 0.0 collective-permute-done.3.near
  74.3 3.8 %last_state.1 = f32[1,36,32,128]{3,2,1,0:T(8,128)} custom-call(f32[36,32,128]{2,1,0:T(8,128)S(1)} %get-tuple-element.38.middle, bf16[3,128,1536]{2,1,0:T(8,128)(2,1)} %get-tuple-element.39.back, f32[3,32,1536]{2,1,0:T(8,128)S(1)} %get-tuple-element.34.damped, bf16[32,128]{1,0:T(8,128)(2,1)S(1)} %copy-done.5, f32[36,128]{1,0:T(8,128)S(1)} %copy-done.2, ...), custom_call_target="tpu_custom_call" | custom-call | flops 150994944 | bytes 4000000 | tf_op jit(solution)/shard_map/last_state/pallas_call | solution.py:460
  78.1 4.0 %all-to-all-done.2 = f32[32,8,128]{2,1,0:T(8,128)S(1)} async-done(((f32[32,8,128]{2,1,0:T(8,128)}), f32[32,8,128]{2,1,0:T(8,128)S(1)}, u32[]{:S(2)}, u32[]{:S(2)}) %all-to-all-start.2) | async-done | bytes 131104 | tf_op jit(solution)/shard_map/all_to_all | solution.py:507
  82.1 0.8 clip.1
  (2 shorter events, 0.1 us)
Async XLA Ops:
  2.1 14.5 %copy-start = (f32[1,36,32,128]{3,2,1,0:T(8,128)S(1)}, f32[1,36,32,128]{3,2,1,0:T(8,128)}, u32[]{:S(2)}) copy-start(f32[1,36,32,128]{3,2,1,0:T(8,128)} %spec.1) | copy-start | bytes 1769476
  2.1 14.5 %copy-start.1 = (f32[1,36,32,128]{3,2,1,0:T(8,128)S(1)}, f32[1,36,32,128]{3,2,1,0:T(8,128)}, u32[]{:S(2)}) copy-start(f32[1,36,32,128]{3,2,1,0:T(8,128)} %cot.1) | copy-start | bytes 1769476
  2.1 14.5 %copy-start.2 = (f32[36,128]{1,0:T(8,128)S(1)}, f32[36,128]{1,0:T(8,128)}, u32[]{:S(2)}) copy-start(f32[36,128]{1,0:T(8,128)} %courant.7) | copy-start | bytes 55300
  2.1 14.5 %copy-start.3 = (s32[36,128]{1,0:T(8,128)S(1)}, s32[36,128]{1,0:T(8,128)}, u32[]{:S(2)}) copy-start(s32[36,128]{1,0:T(8,128)} %upwind.7) | copy-start | bytes 55300
  2.2 14.5 %copy-start.4 = (bf16[128,128]{1,0:T(8,128)(2,1)S(1)}, bf16[128,128]{1,0:T(8,128)(2,1)}, u32[]{:S(2)}) copy-start(bf16[128,128]{1,0:T(8,128)(2,1)} %w_mid.3) | copy-start | bytes 98308
  2.2 14.5 %copy-start.5 = (bf16[32,128]{1,0:T(8,128)(2,1)S(1)}, bf16[32,128]{1,0:T(8,128)(2,1)}, u32[]{:S(2)}) copy-start(bf16[32,128]{1,0:T(8,128)(2,1)} %w_in.5) | copy-start | bytes 24580
  2.2 14.5 %copy-start.6 = (bf16[128,32]{0,1:T(8,128)(2,1)S(1)}, bf16[128,32]{0,1:T(8,128)(2,1)}, u32[]{:S(2)}) copy-start(bf16[128,32]{0,1:T(8,128)(2,1)} %param.18) | copy-start | bytes 24580
  2.2 14.5 %copy-start.7 = (f32[128]{0:T(128)S(1)}, f32[128]{0:T(128)}, u32[]{:S(2)}) copy-start(f32[128]{0:T(128)} %param.15) | copy-start | bytes 1540
  2.2 14.5 %copy-start.8 = (f32[128]{0:T(128)S(1)}, f32[128]{0:T(128)}, u32[]{:S(2)}) copy-start(f32[128]{0:T(128)} %param.17) | copy-start | bytes 1540
  2.2 14.5 %copy-start.9 = (f32[32]{0:T(128)S(1)}, f32[32]{0:T(128)}, u32[]{:S(2)}) copy-start(f32[32]{0:T(128)} %param.19) | copy-start | bytes 388
  2.2 14.4 %collective-permute-start = (f32[1200,128]{1,0:T(8,128)S(1)}, f32[1200,128]{1,0:T(8,128)S(1)}, u32[]{:S(2)}, u32[]{:S(2)}) collective-permute-start(f32[1200,128]{1,0:T(8,128)S(1)} %get-tuple-element.28), channel_id=1, source_target_pairs={{4,8},{8,4},{12,16},{16,12},{20,24},{24,20},{28,32},{32,28},{36,40... | collective-permute-start | bytes 1843208 | tf_op jit(solution)/shard_map/ppermute | solution.py:538
  7.0 9.7 %collective-permute-start.1 = (f32[1200,128]{1,0:T(8,128)S(1)}, f32[1200,128]{1,0:T(8,128)S(1)}, u32[]{:S(2)}, u32[]{:S(2)}) collective-permute-start(f32[1200,128]{1,0:T(8,128)S(1)} %get-tuple-element.29), channel_id=1, source_target_pairs={{0,4},{4,0},{8,12},{12,8},{16,20},{20,16},{24,28},{28,24},{32,36},... | collective-permute-start | bytes 1843208 | tf_op jit(solution)/shard_map/ppermute | solution.py:538
  41.4 26.7 %all-to-all-start.1 = ((f32[16,8,128]{2,1,0:T(8,128)}), f32[16,8,128]{2,1,0:T(8,128)S(1)}, u32[]{:S(2)}, u32[]{:S(2)}) async-start(f32[16,8,128]{2,1,0:T(8,128)} %broadcast_in_dim.24), calls=%async_computation.1 | async-start | bytes 131072 | tf_op jit(solution)/shard_map/all_to_all | solution.py:507
  57.2 17.0 %collective-permute-start.2 = (f32[36,16,128]{2,1,0:T(8,128)}, f32[36,16,128]{2,1,0:T(8,128)S(1)}, u32[]{:S(2)}, u32[]{:S(2)}) collective-permute-start(f32[36,16,128]{2,1,0:T(8,128)} %get-tuple-element.40), channel_id=1, source_target_pairs={{4,8},{8,4},{12,16},{16,12},{20,24},{24,20},{28,32},{32,28},{36,40... | collective-permute-start | bytes 884744 | tf_op jit(solution)/shard_map/ppermute | solution.py:538
  60.0 14.3 %collective-permute-start.3 = (f32[36,16,128]{2,1,0:T(8,128)S(1)}, f32[36,16,128]{2,1,0:T(8,128)S(1)}, u32[]{:S(2)}, u32[]{:S(2)}) collective-permute-start(f32[36,16,128]{2,1,0:T(8,128)S(1)} %get-tuple-element.41), channel_id=1, source_target_pairs={{0,4},{4,0},{8,12},{12,8},{16,20},{20,16},{24,28},{28,24},{32,36},... | collective-permute-start | bytes 884744 | tf_op jit(solution)/shard_map/ppermute | solution.py:538
  68.8 13.3 %all-to-all-start.2 = ((f32[32,8,128]{2,1,0:T(8,128)}), f32[32,8,128]{2,1,0:T(8,128)S(1)}, u32[]{:S(2)}, u32[]{:S(2)}) async-start(f32[32,8,128]{2,1,0:T(8,128)} %broadcast_in_dim.25), calls=%async_computation.2 | async-start | bytes 262144 | tf_op jit(solution)/shard_map/all_to_all | solution.py:507

commit v6 on v5

--- a/solution.py
+++ b/solution.py
@@ -12,9 +12,9 @@
 HALO = 64
 WIDTH = 128
 TAIL = 48
-CHUNK = 12
-HALF = 6
-BLOCK = 12
+CHUNK = 18
+HALF = 18
+BLOCK = 18
 ROWS = 256
 
 time_step = 0.3
@@ -139,15 +139,14 @@
     return rounded, act_one, slope_one, act_two, slope_two, damping, logistic
 
 
-def set_weights(w_in, b_in, w_mid, b_mid, w_out_t, b_out, w_in_t, b_in_c, w_mid_t, b_mid_c, b_out_c, w_out=None):
+def set_weights(w_in, b_in, w_mid, b_mid, w_out_t, b_out, w_in_t, b_in_c, w_mid_t, b_mid_c, b_out_c, w_out):
     w_in_t[...] = w_in[...].astype(F32).T.astype(BF16)
     w_mid_t[...] = w_mid[...].astype(F32).T.astype(BF16)
     b_in_c[...] = column(b_in[...])
     b_mid_c[...] = column(b_mid[...])
     row = jnp.broadcast_to(b_out[...], (HID, FREQS))
     b_out_c[...] = row.T
-    if w_out is not None:
-        w_out[...] = w_out_t[...].astype(F32).T.astype(BF16)
+    w_out[...] = w_out_t[...].astype(F32).T.astype(BF16)
 
 
 def side_by_side(ref, at):
@@ -162,13 +161,15 @@
 def forward_kernel(
     spec, cot, courant, upwind, w_in, b_in, w_mid, b_mid, w_out_t, b_out,
     act_one, slope_one, act_two, slope_two, damped, driven, inside, sent,
-    w_in_t, b_in_c, w_mid_t, b_mid_c, b_out_c,
+    w_in_t, b_in_c, w_mid_t, b_mid_c, b_out_c, w_out,
 ):
     step = pl.program_id(0)
 
     @pl.when(step == 0)
     def _():
-        set_weights(w_in, b_in, w_mid, b_mid, w_out_t, b_out, w_in_t, b_in_c, w_mid_t, b_mid_c, b_out_c)
+        set_weights(
+            w_in, b_in, w_mid, b_mid, w_out_t, b_out, w_in_t, b_in_c, w_mid_t, b_mid_c, b_out_c, w_out
+        )
 
     for part in range(BLOCK // CHUNK):
         at = part * CHUNK
@@ -207,14 +208,18 @@
     ]
 
 
-def weight_scratch():
-    return [
-        pltpu.VMEM((HID, FREQS), BF16),
-        pltpu.VMEM((HID, HID), F32),
-        pltpu.VMEM((HID, HID), BF16),
-        pltpu.VMEM((HID, HID), F32),
-        pltpu.VMEM((FREQS, HID), F32),
-    ]
+TURNED = (
+    ((HID, FREQS), BF16),
+    ((HID, HID), F32),
+    ((HID, HID), BF16),
+    ((HID, HID), F32),
+    ((FREQS, HID), F32),
+    ((HID, FREQS), BF16),
+)
+
+
+def turned_specs():
+    return [pl.BlockSpec(shape, lambda i: (0, 0)) for shape, _ in TURNED]
 
 
 PARTS = DIRS // CHUNK
@@ -243,9 +248,9 @@
         forward_kernel,
         grid=(DIRS // BLOCK,),
         in_specs=[directions(), directions(), whole_rows(), whole_rows()] + weight_specs(),
-        out_specs=saved_specs(),
-        out_shape=[hid(BF16), hid(F32), hid(BF16), hid(F32), freq, freq, freq, freq],
-        scratch_shapes=weight_scratch(),
+        out_specs=saved_specs() + turned_specs(),
+        out_shape=[hid(BF16), hid(F32), hid(BF16), hid(F32), freq, freq, freq, freq]
+        + [jax.ShapeDtypeStruct(*item) for item in TURNED],
         compiler_params=pltpu.CompilerParams(vmem_limit_bytes=LIMIT),
         cost_estimate=pl.CostEstimate(
             flops=2 * 24576 * DIRS * WIDTH, bytes_accessed=9_000_000, transcendentals=2 * HID * DIRS * WIDTH
@@ -267,17 +272,14 @@
 def main_kernel(
     spec, cot, courant, upwind, far, near, far_tail, near_tail,
     act_one, slope_one, act_two, slope_two, damped, driven, inside, sent,
-    w_in, b_in, w_mid, b_mid, w_out_t, b_out,
+    w_in_t, b_in_c, w_mid_t, b_mid_c, b_out_c, w_out, w_in, w_mid, w_out_t,
     middle_out, back_out, grads,
-    w_in_t, b_in_c, w_mid_t, b_mid_c, b_out_c, w_out, b_out_sum, rim_cs, rim_us,
+    b_out_sum, rim_cs, rim_us,
 ):
     step = pl.program_id(0)
 
     @pl.when(step == 0)
     def _():
-        set_weights(
-            w_in, b_in, w_mid, b_mid, w_out_t, b_out, w_in_t, b_in_c, w_mid_t, b_mid_c, b_out_c, w_out
-        )
         set_rim(far_tail, near_tail, rim_cs, rim_us)
         grads[...] = jnp.zeros_like(grads)
         b_out_sum[...] = jnp.zeros_like(b_out_sum)
@@ -369,7 +371,7 @@
         grads[194:195, :FREQS] = jnp.sum(b_out_sum[...].T, axis=0, keepdims=True)
 
 
-def both_adjoints(field, cotangent, courant, upwind, far, near, saved, weights):
+def both_adjoints(field, cotangent, courant, upwind, far, near, saved, w_in, w_mid, w_out_t):
     halo = pl.BlockSpec((BLOCK * FREQS, WIDTH), lambda i: (i, 0))
     tail = pl.BlockSpec((TAIL, WIDTH), lambda i: (DIRS * FREQS // TAIL, 0))
     per = BLOCK // CHUNK
@@ -378,7 +380,8 @@
         grid=(DIRS // BLOCK,),
         in_specs=[directions(), directions(), whole_rows(), whole_rows(), halo, halo, tail, tail]
         + saved_specs()
-        + weight_specs(),
+        + turned_specs()
+        + [weight_specs()[0], weight_specs()[2], weight_specs()[4]],
         out_specs=[
             directions(),
             pl.BlockSpec((per, HID, SPAN), lambda i: (i, 0, 0)),
@@ -389,9 +392,7 @@
             pltpu.HBM((PARTS, HID, SPAN), BF16),
             jax.ShapeDtypeStruct((ROWS, WIDTH), F32),
         ],
-        scratch_shapes=weight_scratch()
-        + [
-            pltpu.VMEM((HID, FREQS), BF16),
+        scratch_shapes=[
             pltpu.VMEM((FREQS, WIDTH), F32),
             pltpu.VMEM((TAIL, WIDTH), F32),
             pltpu.VMEM((TAIL, WIDTH), jnp.int32),
@@ -401,7 +402,7 @@
             flops=10 * 24576 * DIRS * WIDTH, bytes_accessed=14_000_000, transcendentals=2 * HID * DIRS * WIDTH
         ),
         name="both_adjoints",
-    )(field, cotangent, courant, upwind, far, near, far, near, *saved, *weights)
+    )(field, cotangent, courant, upwind, far, near, far, near, *saved, w_in, w_mid, w_out_t)
 
 
 def edge_kernel(middle, to_far, to_near):
@@ -544,7 +545,7 @@
     far, near = by_pairs(*packed_halo(spectrum, cotangent, courant, upwind))
     saved = forward_saved(field, incoming, courant, upwind, weights)
     middle, back, grads = both_adjoints(
-        field, incoming, courant, upwind, far, near, saved, weights
+        field, incoming, courant, upwind, far, near, saved, w_in, w_mid, w_out.T
     )
     totals = clipped(summed_everywhere(grads))
     far_mid, near_mid = by_pairs(*packed_edges(middle))

time: 83.3 us -> 83.1 us (level)
  Pallas kernels: 19.2 us -> 18 us
  transfers between devices with their start and end apart: 6 -> 6, of which waited for: 2 -> 2; matrix products, arithmetic and copies ran while one was open for 1% -> 1% of each run, Pallas kernels for 11% -> 10%
where the time goes in v6:
time: 83.1 us; the launch traced here: 82.6 us
  starting transfers between devices  34.6 us (42%)
  Pallas kernels  18 us (22%)
  blocking collectives  16.8 us (20%)
  waiting for transfers between devices  11 us (13%)
  local copies, waits for them, and re-layouts  1.36 us (2%)
    all_to_all x2, starting transfers between devices, exchanged(): lax.all_to_all(blocks, ('space', 'case'), 0, 0, axis_index_groups=groups,...  20.4 us
    all_to_all x1, blocking collectives, exchanged(): lax.all_to_all(blocks, ('space', 'case'), 0, 0, axis_index_groups=groups,...  16.8 us
    all_to_all x2, waiting for transfers between devices, exchanged(): lax.all_to_all(blocks, ('space', 'case'), 0, 0, axis_index_groups=groups,...  11 us
    ppermute x2, starting transfers between devices, by_pairs(): lax.ppermute(far, 'space', swapped(1))  7.44 us
    pallas_call x1, Pallas kernels, both_adjoints(): pl.pallas_call(main_kernel, grid=(DIRS // BLOCK,), in_specs=[directions()...  7.3 us
    ppermute x2, starting transfers between devices, by_pairs(): lax.ppermute(near, 'space', swapped(0))  6.81 us
    pallas_call x1, Pallas kernels, forward_saved(): pl.pallas_call(forward_kernel, grid=(DIRS // BLOCK,), in_specs=[direction...  4.43 us
    pallas_call x1, Pallas kernels, last_state(): pl.pallas_call(last_kernel, grid=(DIRS // BLOCK,), in_specs=[directions()...  3.03 us
  transfers between devices with their start and end apart: 6, of which 2 were waited for; matrix products, arithmetic and copies ran while one was open for 1% of the time, Pallas kernels for 10%

profile of v6, /device:TPU:1, one launch (start us, length us, event | category | flops | bytes accessed | tf_op | source)
XLA Modules:
  0.0 82.6 jit_solution(17159332098825050977)
XLA Ops:
  0.6 1.5 %pack_halo.1 = (f32[1200,128]{1,0:T(8,128)S(1)}, f32[1200,128]{1,0:T(8,128)S(1)}) custom-call(f32[1,36,32,128]{3,2,1,0:T(8,128)} %spec.1, f32[1,36,32,128]{3,2,1,0:T(8,128)} %cot.1, f32[36,128]{1,0:T(8,128)} %courant.7, s32[36,128]{1,0:T(8,128)} %upwind.7), custom_call_target="tpu_custom_call" | custom-call | tf_op jit(solution)/shard_map/pack_halo/pallas_call | solution.py:75
  2.1 0.0 copy-start
  2.1 0.0 copy-start.1
  2.1 0.0 copy-start.2
  2.1 0.0 copy-start.3
  2.2 0.0 copy-start.4
  2.2 0.0 copy-start.5
  2.2 0.0 copy-start.6
  2.2 4.7 %collective-permute-start = (f32[1200,128]{1,0:T(8,128)S(1)}, f32[1200,128]{1,0:T(8,128)S(1)}, u32[]{:S(2)}, u32[]{:S(2)}) collective-permute-start(f32[1200,128]{1,0:T(8,128)S(1)} %get-tuple-element.34), channel_id=1, source_target_pairs={{4,8},{8,4},{12,16},{16,12},{20,24},{24,20},{28,32},{32,28},{36,40... | collective-permute-start | bytes 1843208 | tf_op jit(solution)/shard_map/ppermute | solution.py:539
  6.9 4.9 %collective-permute-start.1 = (f32[1200,128]{1,0:T(8,128)S(1)}, f32[1200,128]{1,0:T(8,128)S(1)}, u32[]{:S(2)}, u32[]{:S(2)}) collective-permute-start(f32[1200,128]{1,0:T(8,128)S(1)} %get-tuple-element.35), channel_id=1, source_target_pairs={{0,4},{4,0},{8,12},{12,8},{16,20},{20,16},{24,28},{28,24},{32,36},... | collective-permute-start | bytes 1843208 | tf_op jit(solution)/shard_map/ppermute | solution.py:539
  11.8 4.4 %forward_start.1 = (bf16[2,128,2304]{2,1,0:T(8,128)(2,1)S(1)}, f32[2,128,2304]{2,1,0:T(8,128)S(1)}, bf16[2,128,2304]{2,1,0:T(8,128)(2,1)S(1)}, f32[2,128,2304]{2...) custom-call(f32[36,32,128]{2,1,0:T(8,128)} %bitcast.12, ...), custom_call_target="tpu_custom_call" | custom-call | flops 226492416 | bytes 9000000 | tf_op jit(solution)/shard_map/forward_start/pallas_call | solution.py:247
  16.3 0.0 collective-permute-done.far.far_tail
  16.3 0.0 collective-permute-done.1.near.near_tail
  16.3 0.0 copy-done
  16.3 0.0 copy-done.1
  16.3 0.0 copy-done.2
  16.3 0.0 copy-done.3
  16.3 0.0 copy-done.4
  16.3 0.0 copy-done.5
  16.4 0.0 copy-done.6
  16.4 7.3 %both_adjoints.1 = (f32[36,32,128]{2,1,0:T(8,128)S(1)}, bf16[2,128,2304]{2,1,0:T(8,128)(2,1)}, f32[256,128]{1,0:T(8,128)S(1)}) custom-call(f32[36,32,128]{2,1,0:T(8,128)S(1)} %bitcast.13, f32[36,32,128]{2,1,0:T(8,128)S(1)} %bitcast.15, f32[36,128]{1,0:T(8,128)S(1)} %copy-done.2, s32[36,128]{1,0:T(8,128)S(1)} %copy-done.3, ...), custom_call_target="tpu_custom_call" | custom-call | flops 1132462080 | bytes 14000000 | tf_op jit(solution)/shard_map/both_adjoints/pallas_call | solution.py:378
  23.7 16.8 %all_to_all.15 = f32[32,8,128]{2,1,0:T(8,128)S(1)} all-to-all(f32[32,8,128]{2,1,0:T(8,128)S(1)} %bitcast.17), channel_id=1, replica_groups={{0,4,8,12,16,20,24,28,32,36,40,44,48,52,56,60,64,68,72,76,80,84,88,92,9..., dimensions={0} | all-to-all | bytes 262144 | tf_op jit(solution)/shard_map/all_to_all | solution.py:508
  40.5 0.6 broadcast_in_dim.24
  41.1 14.9 %all-to-all-start.1 = ((f32[16,8,128]{2,1,0:T(8,128)}), f32[16,8,128]{2,1,0:T(8,128)S(1)}, u32[]{:S(2)}, u32[]{:S(2)}) async-start(f32[16,8,128]{2,1,0:T(8,128)} %broadcast_in_dim.24), calls=%async_computation.1 | async-start | bytes 131072 | tf_op jit(solution)/shard_map/all_to_all | solution.py:508
  56.0 0.9 %pack_edges.1 = (f32[36,16,128]{2,1,0:T(8,128)}, f32[36,16,128]{2,1,0:T(8,128)S(1)}) custom-call(f32[36,32,128]{2,1,0:T(8,128)S(1)} %get-tuple-element.50.middle), custom_call_target="tpu_custom_call" | custom-call | flops 1000000 | bytes 1200000 | tf_op jit(solution)/shard_map/pack_edges/pallas_call | solution.py:419
  57.0 2.7 %collective-permute-start.2 = (f32[36,16,128]{2,1,0:T(8,128)}, f32[36,16,128]{2,1,0:T(8,128)S(1)}, u32[]{:S(2)}, u32[]{:S(2)}) collective-permute-start(f32[36,16,128]{2,1,0:T(8,128)} %get-tuple-element.52), channel_id=1, source_target_pairs={{4,8},{8,4},{12,16},{16,12},{20,24},{24,20},{28,32},{32,28},{36,40... | collective-permute-start | bytes 884744 | tf_op jit(solution)/shard_map/ppermute | solution.py:539
  59.7 1.9 %collective-permute-start.3 = (f32[36,16,128]{2,1,0:T(8,128)S(1)}, f32[36,16,128]{2,1,0:T(8,128)S(1)}, u32[]{:S(2)}, u32[]{:S(2)}) collective-permute-start(f32[36,16,128]{2,1,0:T(8,128)S(1)} %get-tuple-element.53), channel_id=1, source_target_pairs={{0,4},{4,0},{8,12},{12,8},{16,20},{20,16},{24,28},{28,24},{32,36},... | collective-permute-start | bytes 884744 | tf_op jit(solution)/shard_map/ppermute | solution.py:539
  61.6 6.2 %all-to-all-done.1 = f32[16,8,128]{2,1,0:T(8,128)S(1)} async-done(((f32[16,8,128]{2,1,0:T(8,128)}), f32[16,8,128]{2,1,0:T(8,128)S(1)}, u32[]{:S(2)}, u32[]{:S(2)}) %all-to-all-start.1) | async-done | bytes 65568 | tf_op jit(solution)/shard_map/all_to_all | solution.py:508
  67.8 0.7 broadcast_in_dim.25
  68.5 5.5 %all-to-all-start.2 = ((f32[32,8,128]{2,1,0:T(8,128)}), f32[32,8,128]{2,1,0:T(8,128)S(1)}, u32[]{:S(2)}, u32[]{:S(2)}) async-start(f32[32,8,128]{2,1,0:T(8,128)} %broadcast_in_dim.25), calls=%async_computation.2 | async-start | bytes 262144 | tf_op jit(solution)/shard_map/all_to_all | solution.py:508
  74.0 0.0 collective-permute-done.2.far
  74.0 0.0 collective-permute-done.3.near
  74.0 3.0 %last_state.1 = f32[1,36,32,128]{3,2,1,0:T(8,128)} custom-call(f32[36,32,128]{2,1,0:T(8,128)S(1)} %get-tuple-element.50.middle, bf16[2,128,2304]{2,1,0:T(8,128)(2,1)} %get-tuple-element.51.back, f32[2,32,2304]{2,1,0:T(8,128)S(1)} %get-tuple-element.40.damped, bf16[32,128]{1,0:T(8,128)(2,1)S(1)} %copy-done.5, f32[36,128]{1,0:T(8,128)S(1)} %copy-done.2, ...), custom_call_target="tpu_custom_call" | custom-call | flops 150994944 | bytes 4000000 | tf_op jit(solution)/shard_map/last_state/pallas_call | solution.py:461
  77.0 4.8 %all-to-all-done.2 = f32[32,8,128]{2,1,0:T(8,128)S(1)} async-done(((f32[32,8,128]{2,1,0:T(8,128)}), f32[32,8,128]{2,1,0:T(8,128)S(1)}, u32[]{:S(2)}, u32[]{:S(2)}) %all-to-all-start.2) | async-done | bytes 131104 | tf_op jit(solution)/shard_map/all_to_all | solution.py:508
  81.8 0.8 clip.1
  (2 shorter events, 0.1 us)
Async XLA Ops:
  2.1 14.2 %copy-start = (f32[1,36,32,128]{3,2,1,0:T(8,128)S(1)}, f32[1,36,32,128]{3,2,1,0:T(8,128)}, u32[]{:S(2)}) copy-start(f32[1,36,32,128]{3,2,1,0:T(8,128)} %spec.1) | copy-start | bytes 1769476
  2.1 14.2 %copy-start.1 = (f32[1,36,32,128]{3,2,1,0:T(8,128)S(1)}, f32[1,36,32,128]{3,2,1,0:T(8,128)}, u32[]{:S(2)}) copy-start(f32[1,36,32,128]{3,2,1,0:T(8,128)} %cot.1) | copy-start | bytes 1769476
  2.1 14.2 %copy-start.2 = (f32[36,128]{1,0:T(8,128)S(1)}, f32[36,128]{1,0:T(8,128)}, u32[]{:S(2)}) copy-start(f32[36,128]{1,0:T(8,128)} %courant.7) | copy-start | bytes 55300
  2.1 14.2 %copy-start.3 = (s32[36,128]{1,0:T(8,128)S(1)}, s32[36,128]{1,0:T(8,128)}, u32[]{:S(2)}) copy-start(s32[36,128]{1,0:T(8,128)} %upwind.7) | copy-start | bytes 55300
  2.2 14.2 %copy-start.4 = (bf16[128,128]{1,0:T(8,128)(2,1)S(1)}, bf16[128,128]{1,0:T(8,128)(2,1)}, u32[]{:S(2)}) copy-start(bf16[128,128]{1,0:T(8,128)(2,1)} %w_mid.3) | copy-start | bytes 98308
  2.2 14.2 %copy-start.5 = (bf16[32,128]{1,0:T(8,128)(2,1)S(1)}, bf16[32,128]{1,0:T(8,128)(2,1)}, u32[]{:S(2)}) copy-start(bf16[32,128]{1,0:T(8,128)(2,1)} %w_in.5) | copy-start | bytes 24580
  2.2 14.2 %copy-start.6 = (bf16[128,32]{0,1:T(8,128)(2,1)S(1)}, bf16[128,32]{0,1:T(8,128)(2,1)}, u32[]{:S(2)}) copy-start(bf16[128,32]{0,1:T(8,128)(2,1)} %param.18) | copy-start | bytes 24580
  2.2 14.1 %collective-permute-start = (f32[1200,128]{1,0:T(8,128)S(1)}, f32[1200,128]{1,0:T(8,128)S(1)}, u32[]{:S(2)}, u32[]{:S(2)}) collective-permute-start(f32[1200,128]{1,0:T(8,128)S(1)} %get-tuple-element.34), channel_id=1, source_target_pairs={{4,8},{8,4},{12,16},{16,12},{20,24},{24,20},{28,32},{32,28},{36,40... | collective-permute-start | bytes 1843208 | tf_op jit(solution)/shard_map/ppermute | solution.py:539
  6.9 9.4 %collective-permute-start.1 = (f32[1200,128]{1,0:T(8,128)S(1)}, f32[1200,128]{1,0:T(8,128)S(1)}, u32[]{:S(2)}, u32[]{:S(2)}) collective-permute-start(f32[1200,128]{1,0:T(8,128)S(1)} %get-tuple-element.35), channel_id=1, source_target_pairs={{0,4},{4,0},{8,12},{12,8},{16,20},{20,16},{24,28},{28,24},{32,36},... | collective-permute-start | bytes 1843208 | tf_op jit(solution)/shard_map/ppermute | solution.py:539
  41.1 26.7 %all-to-all-start.1 = ((f32[16,8,128]{2,1,0:T(8,128)}), f32[16,8,128]{2,1,0:T(8,128)S(1)}, u32[]{:S(2)}, u32[]{:S(2)}) async-start(f32[16,8,128]{2,1,0:T(8,128)} %broadcast_in_dim.24), calls=%async_computation.1 | async-start | bytes 131072 | tf_op jit(solution)/shard_map/all_to_all | solution.py:508
  57.0 17.0 %collective-permute-start.2 = (f32[36,16,128]{2,1,0:T(8,128)}, f32[36,16,128]{2,1,0:T(8,128)S(1)}, u32[]{:S(2)}, u32[]{:S(2)}) collective-permute-start(f32[36,16,128]{2,1,0:T(8,128)} %get-tuple-element.52), channel_id=1, source_target_pairs={{4,8},{8,4},{12,16},{16,12},{20,24},{24,20},{28,32},{32,28},{36,40... | collective-permute-start | bytes 884744 | tf_op jit(solution)/shard_map/ppermute | solution.py:539
  59.7 14.3 %collective-permute-start.3 = (f32[36,16,128]{2,1,0:T(8,128)S(1)}, f32[36,16,128]{2,1,0:T(8,128)S(1)}, u32[]{:S(2)}, u32[]{:S(2)}) collective-permute-start(f32[36,16,128]{2,1,0:T(8,128)S(1)} %get-tuple-element.53), channel_id=1, source_target_pairs={{0,4},{4,0},{8,12},{12,8},{16,20},{20,16},{24,28},{28,24},{32,36},... | collective-permute-start | bytes 884744 | tf_op jit(solution)/shard_map/ppermute | solution.py:539
  68.5 13.3 %all-to-all-start.2 = ((f32[32,8,128]{2,1,0:T(8,128)}), f32[32,8,128]{2,1,0:T(8,128)S(1)}, u32[]{:S(2)}, u32[]{:S(2)}) async-start(f32[32,8,128]{2,1,0:T(8,128)} %broadcast_in_dim.25), calls=%async_computation.2 | async-start | bytes 262144 | tf_op jit(solution)/shard_map/all_to_all | solution.py:508

commit v7 on v2

--- a/solution.py
+++ b/solution.py
@@ -12,8 +12,8 @@
 HALO = 64
 WIDTH = 128
 TAIL = 48
-CHUNK = 12
-BLOCK = 12
+CHUNK = 18
+BLOCK = 18
 ROWS = 256
 
 time_step = 0.3
@@ -134,15 +134,14 @@
     return rounded, act_one, slope_one, act_two, slope_two, damping, logistic
 
 
-def set_weights(w_in, b_in, w_mid, b_mid, w_out_t, b_out, w_in_t, b_in_c, w_mid_t, b_mid_c, b_out_c, w_out=None):
+def set_weights(w_in, b_in, w_mid, b_mid, w_out_t, b_out, w_in_t, b_in_c, w_mid_t, b_mid_c, b_out_c, w_out):
     w_in_t[...] = w_in[...].astype(F32).T.astype(BF16)
     w_mid_t[...] = w_mid[...].astype(F32).T.astype(BF16)
     b_in_c[...] = column(b_in[...])
     b_mid_c[...] = column(b_mid[...])
     row = jnp.broadcast_to(b_out[...], (HID, FREQS))
     b_out_c[...] = row.T
-    if w_out is not None:
-        w_out[...] = w_out_t[...].astype(F32).T.astype(BF16)
+    w_out[...] = w_out_t[...].astype(F32).T.astype(BF16)
 
 
 def side_by_side(ref, at):
@@ -157,13 +156,15 @@
 def forward_kernel(
     spec, cot, courant, upwind, w_in, b_in, w_mid, b_mid, w_out_t, b_out,
     act_one, slope_one, act_two, slope_two, damped, driven, inside, sent,
-    w_in_t, b_in_c, w_mid_t, b_mid_c, b_out_c,
+    w_in_t, b_in_c, w_mid_t, b_mid_c, b_out_c, w_out,
 ):
     step = pl.program_id(0)
 
     @pl.when(step == 0)
     def _():
-        set_weights(w_in, b_in, w_mid, b_mid, w_out_t, b_out, w_in_t, b_in_c, w_mid_t, b_mid_c, b_out_c)
+        set_weights(
+            w_in, b_in, w_mid, b_mid, w_out_t, b_out, w_in_t, b_in_c, w_mid_t, b_mid_c, b_out_c, w_out
+        )
 
     for part in range(BLOCK // CHUNK):
         at = part * CHUNK
@@ -202,14 +203,18 @@
     ]
 
 
-def weight_scratch():
-    return [
-        pltpu.VMEM((HID, FREQS), BF16),
-        pltpu.VMEM((HID, HID), F32),
-        pltpu.VMEM((HID, HID), BF16),
-        pltpu.VMEM((HID, HID), F32),
-        pltpu.VMEM((FREQS, HID), F32),
-    ]
+TURNED = (
+    ((HID, FREQS), BF16),
+    ((HID, HID), F32),
+    ((HID, HID), BF16),
+    ((HID, HID), F32),
+    ((FREQS, HID), F32),
+    ((HID, FREQS), BF16),
+)
+
+
+def turned_specs():
+    return [pl.BlockSpec(shape, lambda i: (0, 0)) for shape, _ in TURNED]
 
 
 PARTS = DIRS // CHUNK
@@ -238,9 +243,9 @@
         forward_kernel,
         grid=(DIRS // BLOCK,),
         in_specs=[directions(), directions(), whole_rows(), whole_rows()] + weight_specs(),
-        out_specs=saved_specs(),
-        out_shape=[hid(BF16), hid(F32), hid(BF16), hid(F32), freq, freq, freq, freq],
-        scratch_shapes=weight_scratch(),
+        out_specs=saved_specs() + turned_specs(),
+        out_shape=[hid(BF16), hid(F32), hid(BF16), hid(F32), freq, freq, freq, freq]
+        + [jax.ShapeDtypeStruct(*item) for item in TURNED],
         compiler_params=pltpu.CompilerParams(vmem_limit_bytes=LIMIT),
         cost_estimate=pl.CostEstimate(
             flops=2 * 24576 * DIRS * WIDTH, bytes_accessed=9_000_000, transcendentals=2 * HID * DIRS * WIDTH
@@ -271,17 +276,14 @@
 def main_kernel(
     spec, cot, courant, upwind, far, near, far_tail, near_tail,
     act_one, slope_one, act_two, slope_two, damped, driven, inside, sent,
-    w_in, b_in, w_mid, b_mid, w_out_t, b_out,
+    w_in_t, b_in_c, w_mid_t, b_mid_c, b_out_c, w_out, w_in, w_mid, w_out_t,
     middle_out, rest_out, grads,
-    w_in_t, b_in_c, w_mid_t, b_mid_c, b_out_c, w_out, b_out_sum, rim_cs, rim_us,
+    b_out_sum, rim_cs, rim_us,
 ):
     step = pl.program_id(0)
 
     @pl.when(step == 0)
     def _():
-        set_weights(
-            w_in, b_in, w_mid, b_mid, w_out_t, b_out, w_in_t, b_in_c, w_mid_t, b_mid_c, b_out_c, w_out
-        )
         set_rim(far_tail, near_tail, rim_cs, rim_us)
         grads[...] = jnp.zeros_like(grads)
         b_out_sum[...] = jnp.zeros_like(b_out_sum)
@@ -329,7 +331,7 @@
         grads[194:195, :FREQS] = jnp.sum(b_out_sum[...].T, axis=0, keepdims=True)
 
 
-def both_adjoints(field, cotangent, courant, upwind, far, near, saved, weights):
+def both_adjoints(field, cotangent, courant, upwind, far, near, saved, w_in, w_mid, w_out_t):
     halo = pl.BlockSpec((BLOCK * FREQS, WIDTH), lambda i: (i, 0))
     tail = pl.BlockSpec((TAIL, WIDTH), lambda i: (DIRS * FREQS // TAIL, 0))
     state = jax.ShapeDtypeStruct((DIRS, FREQS, WIDTH), F32)
@@ -338,12 +340,11 @@
         grid=(DIRS // BLOCK,),
         in_specs=[directions(), directions(), whole_rows(), whole_rows(), halo, halo, tail, tail]
         + saved_specs()
-        + weight_specs(),
+        + turned_specs()
+        + [weight_specs()[0], weight_specs()[2], weight_specs()[4]],
         out_specs=[directions(), directions(), pl.BlockSpec((ROWS, WIDTH), lambda i: (0, 0))],
         out_shape=[state, state, jax.ShapeDtypeStruct((ROWS, WIDTH), F32)],
-        scratch_shapes=weight_scratch()
-        + [
-            pltpu.VMEM((HID, FREQS), BF16),
+        scratch_shapes=[
             pltpu.VMEM((FREQS, WIDTH), F32),
             pltpu.VMEM((TAIL, WIDTH), F32),
             pltpu.VMEM((TAIL, WIDTH), jnp.int32),
@@ -353,7 +354,7 @@
             flops=10 * 24576 * DIRS * WIDTH, bytes_accessed=14_000_000, transcendentals=2 * HID * DIRS * WIDTH
         ),
         name="both_adjoints",
-    )(field, cotangent, courant, upwind, far, near, far, near, *saved, *weights)
+    )(field, cotangent, courant, upwind, far, near, far, near, *saved, w_in, w_mid, w_out_t)
 
 
 def edge_kernel(middle, to_far, to_near):
@@ -486,7 +487,7 @@
     far, near = by_pairs(*packed_halo(spectrum, cotangent, courant, upwind))
     saved = forward_saved(field, incoming, courant, upwind, weights)
     middle, rest, grads = both_adjoints(
-        field, incoming, courant, upwind, far, near, saved, weights
+        field, incoming, courant, upwind, far, near, saved, w_in, w_mid, w_out.T
     )
     totals = clipped(summed_everywhere(grads))
     far_mid, near_mid = by_pairs(*packed_edges(middle))

time: 82.5 us -> 81.7 us (level)
  Pallas kernels: 17.2 us -> 15.8 us
  transfers between devices with their start and end apart: 6 -> 6, of which waited for: 2 -> 2; matrix products, arithmetic and copies ran while one was open for 1% -> 1% of each run, Pallas kernels for 10% -> 9%
where the time goes in v7:
time: 81.7 us; the launch traced here: 81.3 us
  starting transfers between devices  34.5 us (42%)
  blocking collectives  16.8 us (21%)
  Pallas kernels  15.8 us (19%)
  waiting for transfers between devices  12 us (15%)
  local copies, waits for them, and re-layouts  1.34 us (2%)
  between operations  0.84 us (1%)
    all_to_all x2, starting transfers between devices, exchanged(): lax.all_to_all(blocks, ('space', 'case'), 0, 0, axis_index_groups=groups,...  20.4 us
    all_to_all x1, blocking collectives, exchanged(): lax.all_to_all(blocks, ('space', 'case'), 0, 0, axis_index_groups=groups,...  16.8 us
    all_to_all x2, waiting for transfers between devices, exchanged(): lax.all_to_all(blocks, ('space', 'case'), 0, 0, axis_index_groups=groups,...  11.9 us
    ppermute x2, starting transfers between devices, by_pairs(): lax.ppermute(far, 'space', swapped(1))  7.3 us
    ppermute x2, starting transfers between devices, by_pairs(): lax.ppermute(near, 'space', swapped(0))  6.81 us
    pallas_call x1, Pallas kernels, both_adjoints(): pl.pallas_call(main_kernel, grid=(DIRS // BLOCK,), in_specs=[directions()...  6.03 us
    pallas_call x1, Pallas kernels, forward_saved(): pl.pallas_call(forward_kernel, grid=(DIRS // BLOCK,), in_specs=[direction...  4.38 us
    pallas_call x1, Pallas kernels, last_state(): pl.pallas_call(last_kernel, grid=(DIRS // BLOCK,), in_specs=[directions()...  2.04 us
  transfers between devices with their start and end apart: 6, of which 2 were waited for; matrix products, arithmetic and copies ran while one was open for 1% of the time, Pallas kernels for 9%

profile of v7, /device:TPU:1, one launch (start us, length us, event | category | flops | bytes accessed | tf_op | source)
XLA Modules:
  0.0 81.3 jit_solution(4407513230841693921)
XLA Ops:
  0.6 0.0 copy-start.3
  0.6 0.0 copy-start.2
  0.7 0.0 copy-start.1
  0.7 0.0 copy-start
  0.7 0.0 copy-start.4
  0.7 0.0 copy-start.5
  0.7 0.0 copy-start.6
  0.7 1.6 %pack_halo.1 = (f32[1200,128]{1,0:T(8,128)S(1)}, f32[1200,128]{1,0:T(8,128)S(1)}) custom-call(f32[1,36,32,128]{3,2,1,0:T(8,128)} %spec.1, f32[1,36,32,128]{3,2,1,0:T(8,128)} %cot.1, f32[36,128]{1,0:T(8,128)} %courant.7, s32[36,128]{1,0:T(8,128)} %upwind.7), custom_call_target="tpu_custom_call" | custom-call | tf_op jit(solution)/shard_map/pack_halo/pallas_call | solution.py:74
  2.3 4.6 %collective-permute-start = (f32[1200,128]{1,0:T(8,128)S(1)}, f32[1200,128]{1,0:T(8,128)S(1)}, u32[]{:S(2)}, u32[]{:S(2)}) collective-permute-start(f32[1200,128]{1,0:T(8,128)S(1)} %get-tuple-element.34), channel_id=1, source_target_pairs={{4,8},{8,4},{12,16},{16,12},{20,24},{24,20},{28,32},{32,28},{36,40... | collective-permute-start | bytes 1843208 | tf_op jit(solution)/shard_map/ppermute | solution.py:481
  6.9 4.9 %collective-permute-start.1 = (f32[1200,128]{1,0:T(8,128)S(1)}, f32[1200,128]{1,0:T(8,128)S(1)}, u32[]{:S(2)}, u32[]{:S(2)}) collective-permute-start(f32[1200,128]{1,0:T(8,128)S(1)} %get-tuple-element.35), channel_id=1, source_target_pairs={{0,4},{4,0},{8,12},{12,8},{16,20},{20,16},{24,28},{28,24},{32,36},... | collective-permute-start | bytes 1843208 | tf_op jit(solution)/shard_map/ppermute | solution.py:481
  11.8 4.4 %forward_start.1 = (bf16[2,128,2304]{2,1,0:T(8,128)(2,1)S(1)}, f32[2,128,2304]{2,1,0:T(8,128)S(1)}, bf16[2,128,2304]{2,1,0:T(8,128)(2,1)S(1)}, f32[2,128,2304]{2...) custom-call(f32[36,32,128]{2,1,0:T(8,128)} %bitcast.12, ...), custom_call_target="tpu_custom_call" | custom-call | flops 226492416 | bytes 9000000 | tf_op jit(solution)/shard_map/forward_start/pallas_call | solution.py:242
  16.2 0.0 collective-permute-done.far.far_tail
  16.2 0.0 collective-permute-done.1.near.near_tail
  16.2 0.0 copy-done.3
  16.2 0.0 copy-done.2
  16.2 0.0 copy-done.1
  16.2 0.0 copy-done
  16.2 0.0 copy-done.4
  16.2 0.0 copy-done.5
  16.3 0.0 copy-done.6
  16.3 6.0 %both_adjoints.1 = (f32[36,32,128]{2,1,0:T(8,128)S(1)}, f32[36,32,128]{2,1,0:T(8,128)S(1)}, f32[256,128]{1,0:T(8,128)S(1)}) custom-call(f32[36,32,128]{2,1,0:T(8,128)S(1)} %bitcast.13, f32[36,32,128]{2,1,0:T(8,128)S(1)} %bitcast.15, f32[36,128]{1,0:T(8,128)S(1)} %copy-done.2, s32[36,128]{1,0:T(8,128)S(1)} %copy-done.3, ...), custom_call_target="tpu_custom_call" | custom-call | flops 1132462080 | bytes 14000000 | tf_op jit(solution)/shard_map/both_adjoints/pallas_call | solution.py:338
  22.3 16.8 %all_to_all.15 = f32[32,8,128]{2,1,0:T(8,128)S(1)} all-to-all(f32[32,8,128]{2,1,0:T(8,128)S(1)} %bitcast.17), channel_id=1, replica_groups={{0,4,8,12,16,20,24,28,32,36,40,44,48,52,56,60,64,68,72,76,80,84,88,92,9..., dimensions={0} | all-to-all | bytes 262144 | tf_op jit(solution)/shard_map/all_to_all | solution.py:450
  39.2 0.6 broadcast_in_dim.24
  39.8 14.9 %all-to-all-start.1 = ((f32[16,8,128]{2,1,0:T(8,128)}), f32[16,8,128]{2,1,0:T(8,128)S(1)}, u32[]{:S(2)}, u32[]{:S(2)}) async-start(f32[16,8,128]{2,1,0:T(8,128)} %broadcast_in_dim.24), calls=%async_computation.1 | async-start | bytes 131072 | tf_op jit(solution)/shard_map/all_to_all | solution.py:450
  54.7 0.9 %pack_edges.1 = (f32[36,16,128]{2,1,0:T(8,128)}, f32[36,16,128]{2,1,0:T(8,128)S(1)}) custom-call(f32[36,32,128]{2,1,0:T(8,128)S(1)} %get-tuple-element.51.middle), custom_call_target="tpu_custom_call" | custom-call | flops 1000000 | bytes 1200000 | tf_op jit(solution)/shard_map/pack_edges/pallas_call | solution.py:371
  55.7 2.7 %collective-permute-start.2 = (f32[36,16,128]{2,1,0:T(8,128)}, f32[36,16,128]{2,1,0:T(8,128)S(1)}, u32[]{:S(2)}, u32[]{:S(2)}) collective-permute-start(f32[36,16,128]{2,1,0:T(8,128)} %get-tuple-element.52), channel_id=1, source_target_pairs={{4,8},{8,4},{12,16},{16,12},{20,24},{24,20},{28,32},{32,28},{36,40... | collective-permute-start | bytes 884744 | tf_op jit(solution)/shard_map/ppermute | solution.py:481
  58.4 1.9 %collective-permute-start.3 = (f32[36,16,128]{2,1,0:T(8,128)S(1)}, f32[36,16,128]{2,1,0:T(8,128)S(1)}, u32[]{:S(2)}, u32[]{:S(2)}) collective-permute-start(f32[36,16,128]{2,1,0:T(8,128)S(1)} %get-tuple-element.53), channel_id=1, source_target_pairs={{0,4},{4,0},{8,12},{12,8},{16,20},{20,16},{24,28},{28,24},{32,36},... | collective-permute-start | bytes 884744 | tf_op jit(solution)/shard_map/ppermute | solution.py:481
  60.3 6.2 %all-to-all-done.1 = f32[16,8,128]{2,1,0:T(8,128)S(1)} async-done(((f32[16,8,128]{2,1,0:T(8,128)}), f32[16,8,128]{2,1,0:T(8,128)S(1)}, u32[]{:S(2)}, u32[]{:S(2)}) %all-to-all-start.1) | async-done | bytes 65568 | tf_op jit(solution)/shard_map/all_to_all | solution.py:450
  66.5 0.7 broadcast_in_dim.25
  67.2 5.5 %all-to-all-start.2 = ((f32[32,8,128]{2,1,0:T(8,128)}), f32[32,8,128]{2,1,0:T(8,128)S(1)}, u32[]{:S(2)}, u32[]{:S(2)}) async-start(f32[32,8,128]{2,1,0:T(8,128)} %broadcast_in_dim.25), calls=%async_computation.2 | async-start | bytes 262144 | tf_op jit(solution)/shard_map/all_to_all | solution.py:450
  72.7 0.0 collective-permute-done.2.far
  72.7 0.0 collective-permute-done.3.near
  72.7 2.0 %last_state.1 = f32[1,36,32,128]{3,2,1,0:T(8,128)} custom-call(f32[36,32,128]{2,1,0:T(8,128)S(1)} %get-tuple-element.50.rest, f32[36,32,128]{2,1,0:T(8,128)S(1)} %get-tuple-element.51.middle, f32[36,128]{1,0:T(8,128)S(1)} %copy-done.2, s32[36,128]{1,0:T(8,128)S(1)} %copy-done.3, f32[36,16,128]{2,1,0:T(8,128)S(1)} %collective-permute-done.2.far, ...), custom_call_target="tpu_custom_call" | custom-call | flops 150994944 | bytes 2400000 | tf_op jit(solution)/shard_map/last_state/pallas_call | solution.py:404
  74.8 5.8 %all-to-all-done.2 = f32[32,8,128]{2,1,0:T(8,128)S(1)} async-done(((f32[32,8,128]{2,1,0:T(8,128)}), f32[32,8,128]{2,1,0:T(8,128)S(1)}, u32[]{:S(2)}, u32[]{:S(2)}) %all-to-all-start.2) | async-done | bytes 131104 | tf_op jit(solution)/shard_map/all_to_all | solution.py:450
  80.5 0.8 %clip.1 = (f32[32,128]{1,0:T(8,128)}, f32[1,128]{1,0:T(1,128)}, f32[128,128]{1,0:T(8,128)}, f32[1,128]{1,0:T(1,128)}, f32[32,128]{1,0:T(8,128)}, /*index=5*/f32[1,32]{1,0:T(1,128)}) custom-call(f32[256,128]{1,0:T(8,128)S(1)} %bitcast.16), custom_call_target="tpu_custom_call" | custom-call | tf_op jit(solution)/shard_map/clip/pallas_call | solution.py:433
  (2 shorter events, 0.1 us)
Async XLA Ops:
  0.6 15.6 %copy-start.3 = (s32[36,128]{1,0:T(8,128)S(1)}, s32[36,128]{1,0:T(8,128)}, u32[]{:S(2)}) copy-start(s32[36,128]{1,0:T(8,128)} %upwind.7) | copy-start | bytes 55300
  0.6 15.6 %copy-start.2 = (f32[36,128]{1,0:T(8,128)S(1)}, f32[36,128]{1,0:T(8,128)}, u32[]{:S(2)}) copy-start(f32[36,128]{1,0:T(8,128)} %courant.7) | copy-start | bytes 55300
  0.7 15.6 %copy-start.1 = (f32[1,36,32,128]{3,2,1,0:T(8,128)S(1)}, f32[1,36,32,128]{3,2,1,0:T(8,128)}, u32[]{:S(2)}) copy-start(f32[1,36,32,128]{3,2,1,0:T(8,128)} %cot.1) | copy-start | bytes 1769476
  0.7 15.6 %copy-start = (f32[1,36,32,128]{3,2,1,0:T(8,128)S(1)}, f32[1,36,32,128]{3,2,1,0:T(8,128)}, u32[]{:S(2)}) copy-start(f32[1,36,32,128]{3,2,1,0:T(8,128)} %spec.1) | copy-start | bytes 1769476
  0.7 15.6 %copy-start.4 = (bf16[128,128]{1,0:T(8,128)(2,1)S(1)}, bf16[128,128]{1,0:T(8,128)(2,1)}, u32[]{:S(2)}) copy-start(bf16[128,128]{1,0:T(8,128)(2,1)} %w_mid.3) | copy-start | bytes 98308
  0.7 15.6 %copy-start.5 = (bf16[32,128]{1,0:T(8,128)(2,1)S(1)}, bf16[32,128]{1,0:T(8,128)(2,1)}, u32[]{:S(2)}) copy-start(bf16[32,128]{1,0:T(8,128)(2,1)} %w_in.3) | copy-start | bytes 24580
  0.7 15.6 %copy-start.6 = (bf16[128,32]{0,1:T(8,128)(2,1)S(1)}, bf16[128,32]{0,1:T(8,128)(2,1)}, u32[]{:S(2)}) copy-start(bf16[128,32]{0,1:T(8,128)(2,1)} %param.18) | copy-start | bytes 24580
  2.3 13.9 %collective-permute-start = (f32[1200,128]{1,0:T(8,128)S(1)}, f32[1200,128]{1,0:T(8,128)S(1)}, u32[]{:S(2)}, u32[]{:S(2)}) collective-permute-start(f32[1200,128]{1,0:T(8,128)S(1)} %get-tuple-element.34), channel_id=1, source_target_pairs={{4,8},{8,4},{12,16},{16,12},{20,24},{24,20},{28,32},{32,28},{36,40... | collective-permute-start | bytes 1843208 | tf_op jit(solution)/shard_map/ppermute | solution.py:481
  6.9 9.3 %collective-permute-start.1 = (f32[1200,128]{1,0:T(8,128)S(1)}, f32[1200,128]{1,0:T(8,128)S(1)}, u32[]{:S(2)}, u32[]{:S(2)}) collective-permute-start(f32[1200,128]{1,0:T(8,128)S(1)} %get-tuple-element.35), channel_id=1, source_target_pairs={{0,4},{4,0},{8,12},{12,8},{16,20},{20,16},{24,28},{28,24},{32,36},... | collective-permute-start | bytes 1843208 | tf_op jit(solution)/shard_map/ppermute | solution.py:481
  39.8 26.7 %all-to-all-start.1 = ((f32[16,8,128]{2,1,0:T(8,128)}), f32[16,8,128]{2,1,0:T(8,128)S(1)}, u32[]{:S(2)}, u32[]{:S(2)}) async-start(f32[16,8,128]{2,1,0:T(8,128)} %broadcast_in_dim.24), calls=%async_computation.1 | async-start | bytes 131072 | tf_op jit(solution)/shard_map/all_to_all | solution.py:450
  55.7 17.0 %collective-permute-start.2 = (f32[36,16,128]{2,1,0:T(8,128)}, f32[36,16,128]{2,1,0:T(8,128)S(1)}, u32[]{:S(2)}, u32[]{:S(2)}) collective-permute-start(f32[36,16,128]{2,1,0:T(8,128)} %get-tuple-element.52), channel_id=1, source_target_pairs={{4,8},{8,4},{12,16},{16,12},{20,24},{24,20},{28,32},{32,28},{36,40... | collective-permute-start | bytes 884744 | tf_op jit(solution)/shard_map/ppermute | solution.py:481
  58.4 14.3 %collective-permute-start.3 = (f32[36,16,128]{2,1,0:T(8,128)S(1)}, f32[36,16,128]{2,1,0:T(8,128)S(1)}, u32[]{:S(2)}, u32[]{:S(2)}) collective-permute-start(f32[36,16,128]{2,1,0:T(8,128)S(1)} %get-tuple-element.53), channel_id=1, source_target_pairs={{0,4},{4,0},{8,12},{12,8},{16,20},{20,16},{24,28},{28,24},{32,36},... | collective-permute-start | bytes 884744 | tf_op jit(solution)/shard_map/ppermute | solution.py:481
  67.2 13.3 %all-to-all-start.2 = ((f32[32,8,128]{2,1,0:T(8,128)}), f32[32,8,128]{2,1,0:T(8,128)S(1)}, u32[]{:S(2)}, u32[]{:S(2)}) async-start(f32[32,8,128]{2,1,0:T(8,128)} %broadcast_in_dim.25), calls=%async_computation.2 | async-start | bytes 262144 | tf_op jit(solution)/shard_map/all_to_all | solution.py:450

commit v8 on v7

--- a/solution.py
+++ b/solution.py
@@ -460,9 +460,11 @@
 def device_groups():
     spaces, cases = lax.axis_size("space"), lax.axis_size("case")
     grid = np.arange(spaces * cases).reshape(spaces // 32, 32, cases)
-    layers = grid.transpose(0, 2, 1).reshape(-1, 32)
-    columns = grid.transpose(1, 0, 2).reshape(32, -1)
-    return layers.tolist(), columns.tolist()
+    grid = grid.transpose(2, 0, 1).reshape(-1, 32)
+    farther = lambda at, size: abs(2 * at - size + 1)
+    deep = sorted(range(grid.shape[0]), key=lambda z: -farther(z, grid.shape[0]))
+    wide = sorted(range(32), key=lambda i: -farther(i // 8, 4) - farther(i // 2 % 4, 4))
+    return grid[:, wide].tolist(), grid[deep].T.tolist()
 
 
 def summed_everywhere(parts):

time: 81.7 us -> 82.6 us (1.011)
  waiting for transfers between devices: 12 us -> 12.9 us
    all_to_all x2, waiting for transfers between devices: 11.9 us -> 12.9 us  [exchanged(): lax.all_to_all(blocks, ('space', 'case'), 0, 0, axis_index_groups=groups,...]
where the time goes in v8:
time: 82.6 us; the launch traced here: 82.2 us
  starting transfers between devices  34.3 us (42%)
  blocking collectives  17 us (21%)
  Pallas kernels  15.8 us (19%)
  waiting for transfers between devices  12.9 us (16%)
  local copies, waits for them, and re-layouts  1.34 us (2%)
  between operations  0.84 us (1%)
    all_to_all x2, starting transfers between devices, exchanged(): lax.all_to_all(blocks, ('space', 'case'), 0, 0, axis_index_groups=groups,...  20.5 us
    all_to_all x1, blocking collectives, exchanged(): lax.all_to_all(blocks, ('space', 'case'), 0, 0, axis_index_groups=groups,...  17 us
    all_to_all x2, waiting for transfers between devices, exchanged(): lax.all_to_all(blocks, ('space', 'case'), 0, 0, axis_index_groups=groups,...  12.9 us
    ppermute x2, starting transfers between devices, by_pairs(): lax.ppermute(far, 'space', swapped(1))  6.94 us
    ppermute x2, starting transfers between devices, by_pairs(): lax.ppermute(near, 'space', swapped(0))  6.81 us
    pallas_call x1, Pallas kernels, both_adjoints(): pl.pallas_call(main_kernel, grid=(DIRS // BLOCK,), in_specs=[directions()...  6.03 us
    pallas_call x1, Pallas kernels, forward_saved(): pl.pallas_call(forward_kernel, grid=(DIRS // BLOCK,), in_specs=[direction...  4.38 us
    pallas_call x1, Pallas kernels, last_state(): pl.pallas_call(last_kernel, grid=(DIRS // BLOCK,), in_specs=[directions()...  2.05 us
  transfers between devices with their start and end apart: 6, of which 2 were waited for; matrix products, arithmetic and copies ran while one was open for 1% of the time, Pallas kernels for 9%

profile of v8, /device:TPU:1, one launch (start us, length us, event | category | flops | bytes accessed | tf_op | source)
XLA Modules:
  0.0 82.2 jit_solution(15677778631133684550)
XLA Ops:
  0.6 0.0 copy-start.3
  0.6 0.0 copy-start.2
  0.7 0.0 copy-start.1
  0.7 0.0 copy-start
  0.7 0.0 copy-start.4
  0.7 0.0 copy-start.5
  0.7 0.0 copy-start.6
  0.7 1.6 %pack_halo.1 = (f32[1200,128]{1,0:T(8,128)S(1)}, f32[1200,128]{1,0:T(8,128)S(1)}) custom-call(f32[1,36,32,128]{3,2,1,0:T(8,128)} %spec.1, f32[1,36,32,128]{3,2,1,0:T(8,128)} %cot.1, f32[36,128]{1,0:T(8,128)} %courant.7, s32[36,128]{1,0:T(8,128)} %upwind.7), custom_call_target="tpu_custom_call" | custom-call | tf_op jit(solution)/shard_map/pack_halo/pallas_call | solution.py:74
  2.3 4.6 %collective-permute-start = (f32[1200,128]{1,0:T(8,128)S(1)}, f32[1200,128]{1,0:T(8,128)S(1)}, u32[]{:S(2)}, u32[]{:S(2)}) collective-permute-start(f32[1200,128]{1,0:T(8,128)S(1)} %get-tuple-element.34), channel_id=1, source_target_pairs={{4,8},{8,4},{12,16},{16,12},{20,24},{24,20},{28,32},{32,28},{36,40... | collective-permute-start | bytes 1843208 | tf_op jit(solution)/shard_map/ppermute | solution.py:483
  6.9 4.9 %collective-permute-start.1 = (f32[1200,128]{1,0:T(8,128)S(1)}, f32[1200,128]{1,0:T(8,128)S(1)}, u32[]{:S(2)}, u32[]{:S(2)}) collective-permute-start(f32[1200,128]{1,0:T(8,128)S(1)} %get-tuple-element.35), channel_id=1, source_target_pairs={{0,4},{4,0},{8,12},{12,8},{16,20},{20,16},{24,28},{28,24},{32,36},... | collective-permute-start | bytes 1843208 | tf_op jit(solution)/shard_map/ppermute | solution.py:483
  11.8 4.4 %forward_start.1 = (bf16[2,128,2304]{2,1,0:T(8,128)(2,1)S(1)}, f32[2,128,2304]{2,1,0:T(8,128)S(1)}, bf16[2,128,2304]{2,1,0:T(8,128)(2,1)S(1)}, f32[2,128,2304]{2...) custom-call(f32[36,32,128]{2,1,0:T(8,128)} %bitcast.12, ...), custom_call_target="tpu_custom_call" | custom-call | flops 226492416 | bytes 9000000 | tf_op jit(solution)/shard_map/forward_start/pallas_call | solution.py:242
  16.2 0.0 collective-permute-done.far.far_tail
  16.2 0.0 collective-permute-done.1.near.near_tail
  16.2 0.0 copy-done.3
  16.2 0.0 copy-done.2
  16.2 0.0 copy-done.1
  16.2 0.0 copy-done
  16.2 0.0 copy-done.4
  16.2 0.0 copy-done.5
  16.3 0.0 copy-done.6
  16.3 6.0 %both_adjoints.1 = (f32[36,32,128]{2,1,0:T(8,128)S(1)}, f32[36,32,128]{2,1,0:T(8,128)S(1)}, f32[256,128]{1,0:T(8,128)S(1)}) custom-call(f32[36,32,128]{2,1,0:T(8,128)S(1)} %bitcast.13, f32[36,32,128]{2,1,0:T(8,128)S(1)} %bitcast.15, f32[36,128]{1,0:T(8,128)S(1)} %copy-done.2, s32[36,128]{1,0:T(8,128)S(1)} %copy-done.3, ...), custom_call_target="tpu_custom_call" | custom-call | flops 1132462080 | bytes 14000000 | tf_op jit(solution)/shard_map/both_adjoints/pallas_call | solution.py:338
  22.3 17.0 %all_to_all.15 = f32[32,8,128]{2,1,0:T(8,128)S(1)} all-to-all(f32[32,8,128]{2,1,0:T(8,128)S(1)} %bitcast.17), channel_id=1, replica_groups={{0,4,24,28,96,100,120,124,8,12,16,20,32,36,56,60,64,68,88,92,104,108,11..., dimensions={0} | all-to-all | bytes 262144 | tf_op jit(solution)/shard_map/all_to_all | solution.py:450
  39.3 0.6 broadcast_in_dim.24
  40.0 14.9 %all-to-all-start.1 = ((f32[16,8,128]{2,1,0:T(8,128)}), f32[16,8,128]{2,1,0:T(8,128)S(1)}, u32[]{:S(2)}, u32[]{:S(2)}) async-start(f32[16,8,128]{2,1,0:T(8,128)} %broadcast_in_dim.24), calls=%async_computation.1 | async-start | bytes 131072 | tf_op jit(solution)/shard_map/all_to_all | solution.py:450
  54.9 0.9 %pack_edges.1 = (f32[36,16,128]{2,1,0:T(8,128)}, f32[36,16,128]{2,1,0:T(8,128)S(1)}) custom-call(f32[36,32,128]{2,1,0:T(8,128)S(1)} %get-tuple-element.51.middle), custom_call_target="tpu_custom_call" | custom-call | flops 1000000 | bytes 1200000 | tf_op jit(solution)/shard_map/pack_edges/pallas_call | solution.py:371
  55.8 2.3 %collective-permute-start.2 = (f32[36,16,128]{2,1,0:T(8,128)}, f32[36,16,128]{2,1,0:T(8,128)S(1)}, u32[]{:S(2)}, u32[]{:S(2)}) collective-permute-start(f32[36,16,128]{2,1,0:T(8,128)} %get-tuple-element.52), channel_id=1, source_target_pairs={{4,8},{8,4},{12,16},{16,12},{20,24},{24,20},{28,32},{32,28},{36,40... | collective-permute-start | bytes 884744 | tf_op jit(solution)/shard_map/ppermute | solution.py:483
  58.2 1.9 %collective-permute-start.3 = (f32[36,16,128]{2,1,0:T(8,128)S(1)}, f32[36,16,128]{2,1,0:T(8,128)S(1)}, u32[]{:S(2)}, u32[]{:S(2)}) collective-permute-start(f32[36,16,128]{2,1,0:T(8,128)S(1)} %get-tuple-element.53), channel_id=1, source_target_pairs={{0,4},{4,0},{8,12},{12,8},{16,20},{20,16},{24,28},{28,24},{32,36},... | collective-permute-start | bytes 884744 | tf_op jit(solution)/shard_map/ppermute | solution.py:483
  60.1 7.0 %all-to-all-done.1 = f32[16,8,128]{2,1,0:T(8,128)S(1)} async-done(((f32[16,8,128]{2,1,0:T(8,128)}), f32[16,8,128]{2,1,0:T(8,128)S(1)}, u32[]{:S(2)}, u32[]{:S(2)}) %all-to-all-start.1) | async-done | bytes 65568 | tf_op jit(solution)/shard_map/all_to_all | solution.py:450
  67.2 0.7 broadcast_in_dim.25
  67.8 5.6 %all-to-all-start.2 = ((f32[32,8,128]{2,1,0:T(8,128)}), f32[32,8,128]{2,1,0:T(8,128)S(1)}, u32[]{:S(2)}, u32[]{:S(2)}) async-start(f32[32,8,128]{2,1,0:T(8,128)} %broadcast_in_dim.25), calls=%async_computation.2 | async-start | bytes 262144 | tf_op jit(solution)/shard_map/all_to_all | solution.py:450
  73.4 0.0 collective-permute-done.2.far
  73.4 0.0 collective-permute-done.3.near
  73.5 2.0 %last_state.1 = f32[1,36,32,128]{3,2,1,0:T(8,128)} custom-call(f32[36,32,128]{2,1,0:T(8,128)S(1)} %get-tuple-element.50.rest, f32[36,32,128]{2,1,0:T(8,128)S(1)} %get-tuple-element.51.middle, f32[36,128]{1,0:T(8,128)S(1)} %copy-done.2, s32[36,128]{1,0:T(8,128)S(1)} %copy-done.3, f32[36,16,128]{2,1,0:T(8,128)S(1)} %collective-permute-done.2.far, ...), custom_call_target="tpu_custom_call" | custom-call | flops 150994944 | bytes 2400000 | tf_op jit(solution)/shard_map/last_state/pallas_call | solution.py:404
  75.5 5.9 %all-to-all-done.2 = f32[32,8,128]{2,1,0:T(8,128)S(1)} async-done(((f32[32,8,128]{2,1,0:T(8,128)}), f32[32,8,128]{2,1,0:T(8,128)S(1)}, u32[]{:S(2)}, u32[]{:S(2)}) %all-to-all-start.2) | async-done | bytes 131104 | tf_op jit(solution)/shard_map/all_to_all | solution.py:450
  81.4 0.8 clip.1
  (2 shorter events, 0.1 us)
Async XLA Ops:
  0.6 15.6 %copy-start.3 = (s32[36,128]{1,0:T(8,128)S(1)}, s32[36,128]{1,0:T(8,128)}, u32[]{:S(2)}) copy-start(s32[36,128]{1,0:T(8,128)} %upwind.7) | copy-start | bytes 55300
  0.6 15.6 %copy-start.2 = (f32[36,128]{1,0:T(8,128)S(1)}, f32[36,128]{1,0:T(8,128)}, u32[]{:S(2)}) copy-start(f32[36,128]{1,0:T(8,128)} %courant.7) | copy-start | bytes 55300
  0.7 15.6 %copy-start.1 = (f32[1,36,32,128]{3,2,1,0:T(8,128)S(1)}, f32[1,36,32,128]{3,2,1,0:T(8,128)}, u32[]{:S(2)}) copy-start(f32[1,36,32,128]{3,2,1,0:T(8,128)} %cot.1) | copy-start | bytes 1769476
  0.7 15.6 %copy-start = (f32[1,36,32,128]{3,2,1,0:T(8,128)S(1)}, f32[1,36,32,128]{3,2,1,0:T(8,128)}, u32[]{:S(2)}) copy-start(f32[1,36,32,128]{3,2,1,0:T(8,128)} %spec.1) | copy-start | bytes 1769476
  0.7 15.6 %copy-start.4 = (bf16[128,128]{1,0:T(8,128)(2,1)S(1)}, bf16[128,128]{1,0:T(8,128)(2,1)}, u32[]{:S(2)}) copy-start(bf16[128,128]{1,0:T(8,128)(2,1)} %w_mid.3) | copy-start | bytes 98308
  0.7 15.6 %copy-start.5 = (bf16[32,128]{1,0:T(8,128)(2,1)S(1)}, bf16[32,128]{1,0:T(8,128)(2,1)}, u32[]{:S(2)}) copy-start(bf16[32,128]{1,0:T(8,128)(2,1)} %w_in.3) | copy-start | bytes 24580
  0.7 15.6 %copy-start.6 = (bf16[128,32]{0,1:T(8,128)(2,1)S(1)}, bf16[128,32]{0,1:T(8,128)(2,1)}, u32[]{:S(2)}) copy-start(bf16[128,32]{0,1:T(8,128)(2,1)} %param.18) | copy-start | bytes 24580
  2.3 13.9 %collective-permute-start = (f32[1200,128]{1,0:T(8,128)S(1)}, f32[1200,128]{1,0:T(8,128)S(1)}, u32[]{:S(2)}, u32[]{:S(2)}) collective-permute-start(f32[1200,128]{1,0:T(8,128)S(1)} %get-tuple-element.34), channel_id=1, source_target_pairs={{4,8},{8,4},{12,16},{16,12},{20,24},{24,20},{28,32},{32,28},{36,40... | collective-permute-start | bytes 1843208 | tf_op jit(solution)/shard_map/ppermute | solution.py:483
  6.9 9.3 %collective-permute-start.1 = (f32[1200,128]{1,0:T(8,128)S(1)}, f32[1200,128]{1,0:T(8,128)S(1)}, u32[]{:S(2)}, u32[]{:S(2)}) collective-permute-start(f32[1200,128]{1,0:T(8,128)S(1)} %get-tuple-element.35), channel_id=1, source_target_pairs={{0,4},{4,0},{8,12},{12,8},{16,20},{20,16},{24,28},{28,24},{32,36},... | collective-permute-start | bytes 1843208 | tf_op jit(solution)/shard_map/ppermute | solution.py:483
  40.0 27.2 %all-to-all-start.1 = ((f32[16,8,128]{2,1,0:T(8,128)}), f32[16,8,128]{2,1,0:T(8,128)S(1)}, u32[]{:S(2)}, u32[]{:S(2)}) async-start(f32[16,8,128]{2,1,0:T(8,128)} %broadcast_in_dim.24), calls=%async_computation.1 | async-start | bytes 131072 | tf_op jit(solution)/shard_map/all_to_all | solution.py:450
  55.8 17.6 %collective-permute-start.2 = (f32[36,16,128]{2,1,0:T(8,128)}, f32[36,16,128]{2,1,0:T(8,128)S(1)}, u32[]{:S(2)}, u32[]{:S(2)}) collective-permute-start(f32[36,16,128]{2,1,0:T(8,128)} %get-tuple-element.52), channel_id=1, source_target_pairs={{4,8},{8,4},{12,16},{16,12},{20,24},{24,20},{28,32},{32,28},{36,40... | collective-permute-start | bytes 884744 | tf_op jit(solution)/shard_map/ppermute | solution.py:483
  58.2 15.3 %collective-permute-start.3 = (f32[36,16,128]{2,1,0:T(8,128)S(1)}, f32[36,16,128]{2,1,0:T(8,128)S(1)}, u32[]{:S(2)}, u32[]{:S(2)}) collective-permute-start(f32[36,16,128]{2,1,0:T(8,128)S(1)} %get-tuple-element.53), channel_id=1, source_target_pairs={{0,4},{4,0},{8,12},{12,8},{16,20},{20,16},{24,28},{28,24},{32,36},... | collective-permute-start | bytes 884744 | tf_op jit(solution)/shard_map/ppermute | solution.py:483
  67.8 13.6 %all-to-all-start.2 = ((f32[32,8,128]{2,1,0:T(8,128)}), f32[32,8,128]{2,1,0:T(8,128)S(1)}, u32[]{:S(2)}, u32[]{:S(2)}) async-start(f32[32,8,128]{2,1,0:T(8,128)} %broadcast_in_dim.25), calls=%async_computation.2 | async-start | bytes 262144 | tf_op jit(solution)/shard_map/all_to_all | solution.py:450
